TPU v7x, 32 devices: a whole 2x2x4 slice. The times are simulated.
32 devices in a mesh: blk: 32 (over z, y, x, core), section: 1.
Axes of the slice: x: 2, y: 2, z: 4, core: 2. Of those that a mesh axis runs over, the one named last changes fastest.
Arguments:
- stream_sent: bfloat16 [1, 128, 3072], P('section', 'blk'), may hold values from -6 to 6
- grad_sent: bfloat16 [1, 128, 3072], P('section', 'blk'), may hold values from -3 to 3
- preact_now: bfloat16 [1, 128, 16384], P('section', None, 'blk'), may hold values from -6 to 6
- preact_back: bfloat16 [1, 128, 16384], P('section', None, 'blk'), may hold values from -6 to 6
- down_weight: bfloat16 [1, 16384, 3072], P('section', 'blk'), may hold values from -0.109375 to 0.109375
- block_mask: int32 [1, 128, 24], P('section', 'blk'), may hold values from 0 to 1, as said below
Outputs:
- stream_out: bfloat16 [1, 128, 3072], P('section', 'blk')
- preact_grad: bfloat16 [1, 128, 16384], P('section', None, 'blk')
- weight_grad: bfloat16 [1, 16384, 3072], P('section', 'blk')
Inputs may be any that keep to these rules, and one draw needn't show every extreme that they name: `block_mask`: 1 marks a nonzero 128 x 128 block of the down projection, 0 an empty one.
All inputs are finite; a program needn't handle non-finite values.
Results may differ from a plain program's by a relative error of at most 0.005.
Values may be sent and summed in bfloat16 or wider, within the bound.
No kernel may reach another device: no remote copies, remote signals or barrier semaphores. Data moves between devices by JAX's collectives and lax.ppermute only.
A program may use at most 64 MiB of HBM per device.

v0:
```python
import jax
import jax.numpy as jnp
from jax import lax
from jax.sharding import PartitionSpec as P

BLOCK = 128


def shifted(block, axis, distance):
    devices = range(lax.axis_size(axis))
    route = [(i - distance, i) for i in devices if i - distance in devices]
    return lax.ppermute(block, axis, route)


def expand(blocks):
    values = blocks.astype(jnp.bfloat16)
    return jnp.repeat(jnp.repeat(values, BLOCK, axis=0), BLOCK, axis=1)


def body(stream_sent, grad_sent, preact_now, preact_back, down_weight, block_mask):
    section_index = lax.axis_index("section")
    final_section = lax.axis_size("section") - 1
    expanded = expand(block_mask[0])
    masked = down_weight[0] * expanded
    arrived = shifted(stream_sent, "section", 1)
    stream = jnp.where(section_index == 0, stream_sent, arrived)[0]
    hidden_now = jax.nn.gelu(preact_now[0].astype(jnp.float32)).astype(jnp.bfloat16)
    summed = lax.psum_scatter(
        jnp.dot(hidden_now, masked, preferred_element_type=jnp.float32),
        "blk",
        scatter_dimension=0,
        tiled=True,
    )
    stream_out = (stream.astype(jnp.float32) + summed).astype(jnp.bfloat16)[None]
    arrived = shifted(grad_sent, "section", -1)
    grad = jnp.where(section_index == final_section, grad_sent, arrived)[0]
    gathered = lax.all_gather(grad, "blk", axis=0, tiled=True)
    grad_hidden = lax.dot_general(
        gathered, masked, (((1,), (1,)), ((), ())), preferred_element_type=jnp.float32
    )
    preact_f = preact_back[0].astype(jnp.float32)
    hidden_f, pullback = jax.vjp(jax.nn.gelu, preact_f)
    preact_grad = pullback(grad_hidden)[0].astype(jnp.bfloat16)
    hidden_back = hidden_f.astype(jnp.bfloat16)
    weight_full = lax.dot_general(
        hidden_back, gathered, (((0,), (0,)), ((), ())), preferred_element_type=jnp.float32
    )
    weight_grad = (weight_full * expanded.astype(jnp.float32)).astype(jnp.bfloat16)
    preact_grad, weight_grad = (preact_grad[None], weight_grad[None])
    return (stream_out, preact_grad, weight_grad)


def solution(mesh):
    placed = (
        P("section", "blk", None),
        P("section", "blk", None),
        P("section", None, "blk"),
        P("section", None, "blk"),
        P("section", "blk", None),
        P("section", "blk", None),
    )
    return jax.shard_map(
        body,
        mesh=mesh,
        in_specs=placed,
        out_specs=(P("section", "blk", None), P("section", None, "blk"), P("section", "blk", None)),
        check_vma=False,
    )
```

profile of v0, /device:TPU:0, one launch (start us, length us, event | category | flops | bytes accessed | tf_op | source)
XLA Modules:
  0.0 161.8 jit_solution(8575451650951467659)
XLA Ops:
  7.2 0.0 all-reduce.3.cloned.1.call-start
  7.2 0.7 convert_bitcast_fusion
  7.9 1.9 %broadcast_in_dim.16 = bf16[512,24,128]{2,1,0:T(8,128)(2,1)S(1)} broadcast(bf16[512,24]{1,0:T(8,128)(2,1)S(1)} %bitcast.64), dimensions={0,1} | broadcast | bytes 3170304 | tf_op jit(solution)/shard_map/broadcast_in_dim | solution.py:17
  9.9 0.0 copy-start
  9.9 2.8 %reshape.23 = bf16[1,512,3072]{2,1,0:T(8,128)(2,1)} reshape(bf16[512,24,128]{2,1,0:T(8,128)(2,1)S(1)} %broadcast_in_dim.16) | data formatting | bytes 6291456 | tf_op jit(solution)/shard_map/reshape | solution.py:17
  12.7 0.0 copy-done
  12.7 0.0 copy-start.2
  12.7 4.9 %fusion.3 = f32[128,3072]{1,0:T(8,128)} fusion(bf16[1,512,3072]{2,1,0:T(8,128)(2,1)} %param.10, bf16[1,512,3072]{2,1,0:T(8,128)(2,1)} %reshape.23, bf16[1,128,512]{2,1,0:T(8,128)(2,1)S(1)} %copy-done), kind=kOutput, calls=%fused_computation.5 | convolution fusion | flops 404881408 | bytes 7995392 | tf_op jit(solution)/shard_map/dot_general | solution.py:29
  17.5 0.0 copy-start.1
  17.5 0.0 all-reduce.3.cloned.1.call-update
  17.6 0.0 copy-done.2
  17.6 51.8 %all-gather = bf16[1,128,3072]{2,0,1:T(2,128)(2,1)} all-gather(bf16[1,4,3072]{2,0,1:T(2,128)(2,1)S(1)} %copy.14), channel_id=2, replica_groups=mesh['blk'=32,'section'=1] {'blk'}, dimensions={1}, use_global_device_ids=true | all-gather | bytes 811008 | tf_op jit(solution)/shard_map/all_gather | solution.py:37
  69.4 0.0 copy-done.1
  69.4 0.1 copy.15
  69.5 3.4 %fusion.30 = bf16[1,128,512]{1,2,0:T(8,128)(2,1)S(1)} fusion(bf16[1,128,3072]{2,0,1:T(2,128)(2,1)} %all-gather, bf16[1,512,3072]{2,1,0:T(8,128)(2,1)} %param.10, bf16[64,8,24,128]{3,2,1,0:T(8,128)(2,1)S(1)} %bitcast.62, bf16[1,128,512]{1,2,0:T(8,128)(2,1)S(1)} %copy.15), kind=kOutput, calls=%fused_computation.39 | convolution fusion | flops 405602304 | bytes 7340032 | tf_op jit(solution)/shard_map/dot_general | solution.py:38
  72.9 0.8 copy.16
  73.7 0.0 copy-start.3
  73.7 4.1 %fusion = bf16[1,512,3072]{2,1,0:T(8,128)(2,1)} fusion(bf16[64,8,24,128]{3,2,1,0:T(8,128)(2,1)S(1)} %bitcast.63, bf16[1,128,3072]{2,0,1:T(2,128)(2,1)} %all-gather, bf16[1,128,512]{1,2,0:T(8,128)(2,1)S(1)} %copy.15), kind=kOutput, calls=%fused_computation.1 | convolution fusion | flops 408027136 | bytes 7208960 | tf_op jit(solution)/shard_map/dot_general | solution.py:45
  77.8 75.6 %all-reduce.3.cloned.1.call-done = f32[128,3072]{1,0:T(8,128)} async-done(((f32[128,3072]{1,0:T(8,128)}), f32[128,3072]{1,0:T(8,128)}) %all-reduce.3.cloned.1.call-update) | async-done | bytes 1572880
  153.4 0.0 copy-done.3
  153.4 1.5 fusion.46
  (2 shorter events, 0.1 us)
Async XLA Ops:
  7.2 146.2 %all-reduce.3.cloned.1.call-start = ((), (), s32[]{:S(2)}) async-start(), calls=%async_computation | async-start | bytes 3145728
  9.9 2.8 %copy-start = (bf16[1,128,512]{2,1,0:T(8,128)(2,1)S(1)}, bf16[1,128,512]{2,1,0:T(8,128)(2,1)}, u32[]{:S(2)}) copy-start(bf16[1,128,512]{2,1,0:T(8,128)(2,1)} %param.8) | copy-start | bytes 393220
  12.7 4.9 %copy-start.2 = (bf16[1,4,3072]{2,1,0:T(4,128)(2,1)S(1)}, bf16[1,4,3072]{2,1,0:T(4,128)(2,1)}, u32[]{:S(2)}) copy-start(bf16[1,4,3072]{2,1,0:T(4,128)(2,1)} %param.7) | copy-start | bytes 73732
  17.5 51.9 %copy-start.1 = (bf16[1,128,512]{2,1,0:T(8,128)(2,1)S(1)}, bf16[1,128,512]{2,1,0:T(8,128)(2,1)}, u32[]{:S(2)}) copy-start(bf16[1,128,512]{2,1,0:T(8,128)(2,1)} %param.9) | copy-start | bytes 393220
  73.7 79.7 %copy-start.3 = (bf16[1,4,3072]{2,1,0:T(4,128)(2,1)S(1)}, bf16[1,4,3072]{2,1,0:T(4,128)(2,1)}, u32[]{:S(2)}) copy-start(bf16[1,4,3072]{2,1,0:T(4,128)(2,1)} %param.6) | copy-start | bytes 73732
Sparse Core Ops, SparseCore 0:
  17.7 135.6 all-reduce.2
where the time goes:
time: 162 us
  waiting for transfers between devices  75.6 us (47%)
  blocking collectives  51.8 us (32%)
  between operations  14.1 us (9%)
  matrix products  12.3 us (8%)
  local copies, waits for them, and re-layouts  5.69 us (4%)
  other arithmetic  2.21 us (1%)
    unnamed x2, waiting for transfers between devices  75.6 us
    all_gather x1, blocking collectives, body(): gathered = lax.all_gather(grad, 'blk', axis=0, tiled=True)  51.8 us
    dot_general x1, matrix products, body(): jnp.dot(hidden_now, masked, preferred_element_type=jnp.float32)  4.86 us
    dot_general x1, matrix products, body(): lax.dot_general(hidden_back, gathered, (((0,), (0,)), ((), ())), preferre...  4.1 us
    dot_general x1, matrix products, body(): lax.dot_general(gathered, masked, (((1,), (1,)), ((), ())), preferred_ele...  3.37 us
  transfers between devices with their start and end apart: 1, of which 1 were waited for; matrix products, arithmetic and copies ran while one was open for 5% of the time, Pallas kernels for 0%

commit v1 on v0

v1 whole, which is shorter than its diff:
```python
import functools
import math

import jax
import jax.numpy as jnp
from jax import lax
from jax.experimental import pallas as pl
from jax.experimental.pallas import tpu as pltpu
from jax.sharding import PartitionSpec as P

BLOCK = 128
SCALE = math.sqrt(2.0 / math.pi)
CUBIC = 0.044715
CHUNK = 512
bf16 = jnp.bfloat16
f32 = jnp.float32


def shifted(block, axis, distance):
    devices = range(lax.axis_size(axis))
    route = [(i - distance, i) for i in devices if i - distance in devices]
    return lax.ppermute(block, axis, route)


def exchange(block, bit):
    return lax.ppermute(block, "blk", [(i, i ^ bit) for i in range(lax.axis_size("blk"))])


def own_token(place, me, order, each):
    group, within = place // each, place % each
    owner = me
    for k, bit in enumerate(order):
        owner = owner ^ jnp.where((group >> (len(order) - 1 - k)) & 1 == 1, bit, 0)
    return owner * each + within


def reorder(me, tokens, order, back=False):
    rows = lax.broadcasted_iota(jnp.int32, (tokens, tokens), 1 if back else 0)
    cols = lax.broadcasted_iota(jnp.int32, (tokens, tokens), 0 if back else 1)
    return (own_token(rows, me, order, tokens >> len(order)) == cols).astype(bf16)


def masked_block(w_ref, mask_ref, first):
    rows = []
    for i in range(w_ref.shape[0] // BLOCK):
        row = []
        for j in range(w_ref.shape[1] // BLOCK):
            block = w_ref[i * BLOCK : (i + 1) * BLOCK, j * BLOCK : (j + 1) * BLOCK]
            row.append(jnp.where(mask_ref[i, first + j] != 0, block, jnp.zeros_like(block)))
        rows.append(jnp.concatenate(row, axis=1))
    return jnp.concatenate(rows, axis=0)


def forward_kernel(order, me_ref, mask_ref, pre_ref, w_ref, keep_ref, send_ref, hidden_ref):
    step = pl.program_id(0)
    tokens = pre_ref.shape[0]

    @pl.when(step == 0)
    def _():
        x = pre_ref[...].astype(f32)
        hidden = 0.5 * x * (1.0 + jnp.tanh(SCALE * (x + CUBIC * x * x * x)))
        moved = jnp.dot(reorder(me_ref[0], tokens, order), hidden.astype(bf16), preferred_element_type=f32)
        hidden_ref[...] = moved.astype(bf16)

    masked = masked_block(w_ref, mask_ref, step * (w_ref.shape[1] // BLOCK))
    product = jnp.dot(hidden_ref[...], masked, preferred_element_type=f32)
    keep_ref[...] = product[: tokens // 2]
    send_ref[...] = product[tokens // 2 :].astype(bf16)


def prepare_kernel(order, me_ref, pre_ref, hidden_ref, slope_ref):
    tokens = pre_ref.shape[0]
    moved = jnp.dot(reorder(me_ref[0], tokens, order), pre_ref[...], preferred_element_type=f32)
    square = moved * moved
    t = jnp.tanh(SCALE * (moved + CUBIC * moved * square))
    half = 0.5 * (1.0 + t)
    hidden_ref[...] = (moved * half).astype(bf16)
    slope_ref[...] = half + 0.5 * moved * (1.0 - t * t) * (SCALE * (1.0 + 3.0 * CUBIC * square))


def backward_kernel(order, me_ref, mask_ref, mine_ref, other_ref, w_ref, hidden_ref, slope_ref, wg_ref, pg_ref, acc_ref):
    step = pl.program_id(0)
    first = step * (w_ref.shape[1] // BLOCK)
    grad = jnp.concatenate([mine_ref[...], other_ref[...]], axis=0)
    masked = masked_block(w_ref, mask_ref, first)
    part = lax.dot_general(grad, masked, (((1,), (1,)), ((), ())), preferred_element_type=f32)

    @pl.when(step == 0)
    def _():
        acc_ref[...] = part

    @pl.when(step > 0)
    def _():
        acc_ref[...] += part

    full = lax.dot_general(hidden_ref[...], grad, (((0,), (0,)), ((), ())), preferred_element_type=f32)
    for i in range(w_ref.shape[0] // BLOCK):
        for j in range(w_ref.shape[1] // BLOCK):
            block = full[i * BLOCK : (i + 1) * BLOCK, j * BLOCK : (j + 1) * BLOCK]
            kept = jnp.where(mask_ref[i, first + j] != 0, block, jnp.zeros_like(block))
            wg_ref[i * BLOCK : (i + 1) * BLOCK, j * BLOCK : (j + 1) * BLOCK] = kept.astype(bf16)

    @pl.when(step == pl.num_programs(0) - 1)
    def _():
        tokens = pg_ref.shape[0]
        moved = (acc_ref[...] * slope_ref[...]).astype(bf16)
        back = reorder(me_ref[0], tokens, order, back=True)
        pg_ref[...] = jnp.dot(back, moved, preferred_element_type=f32).astype(bf16)


SMEM = functools.partial(pl.BlockSpec, memory_space=pltpu.SMEM)


def body(stream_sent, grad_sent, preact_now, preact_back, down_weight, block_mask):
    sections = lax.axis_size("section")
    stream, grad = stream_sent, grad_sent
    if sections > 1:
        section_index = lax.axis_index("section")
        stream = jnp.where(section_index == 0, stream, shifted(stream, "section", 1))
        grad = jnp.where(section_index == sections - 1, grad, shifted(grad, "section", -1))
    stream, grad, mask, weight = stream[0], grad[0], block_mask[0], down_weight[0]
    pre_now, pre_back = preact_now[0], preact_back[0]
    tokens, hidden = pre_now.shape
    width = weight.shape[1]
    chunk = CHUNK if width % CHUNK == 0 else BLOCK
    devices = lax.axis_size("blk")
    order = [1 << k for k in range(devices.bit_length() - 1)]
    me = lax.axis_index("blk").astype(jnp.int32).reshape(1)

    def whole(rows, cols):
        return pl.BlockSpec((rows, cols), lambda c: (0, 0))

    def column(rows):
        return pl.BlockSpec((rows, chunk), lambda c: (0, c))

    half = tokens // 2
    keep, send = pl.pallas_call(
        functools.partial(forward_kernel, order),
        grid=(width // chunk,),
        out_shape=(jax.ShapeDtypeStruct((half, width), f32), jax.ShapeDtypeStruct((half, width), bf16)),
        in_specs=[SMEM(), SMEM(), whole(tokens, hidden), column(hidden)],
        out_specs=(column(half), column(half)),
        scratch_shapes=[pltpu.VMEM((tokens, hidden), bf16)],
        cost_estimate=pl.CostEstimate(flops=2 * tokens * hidden * width, bytes_accessed=2 * hidden * width, transcendentals=0),
        name="forward",
    )(me, mask, pre_now, weight)

    hidden_back, slope = pl.pallas_call(
        functools.partial(prepare_kernel, order),
        out_shape=(jax.ShapeDtypeStruct((tokens, hidden), bf16), jax.ShapeDtypeStruct((tokens, hidden), f32)),
        in_specs=[SMEM(), pl.BlockSpec(memory_space=pltpu.VMEM)],
        name="prepare",
    )(me, pre_back)

    mine = grad
    for bit in order[:0:-1]:
        mine = jnp.concatenate([mine, exchange(mine, bit)], axis=0)
    other = exchange(mine, order[0])

    for bit in order:
        total = keep + exchange(send, bit).astype(f32)
        rows = total.shape[0] // 2
        keep, send = total[:rows], total[rows:].astype(bf16)
    stream_out = (stream.astype(f32) + total).astype(bf16)

    weight_grad, preact_grad = pl.pallas_call(
        functools.partial(backward_kernel, order),
        grid=(width // chunk,),
        out_shape=(jax.ShapeDtypeStruct((hidden, width), bf16), jax.ShapeDtypeStruct((tokens, hidden), bf16)),
        in_specs=[SMEM(), SMEM(), column(half), column(half), column(hidden), whole(tokens, hidden), whole(tokens, hidden)],
        out_specs=(column(hidden), whole(tokens, hidden)),
        scratch_shapes=[pltpu.VMEM((tokens, hidden), f32)],
        cost_estimate=pl.CostEstimate(flops=4 * tokens * hidden * width, bytes_accessed=4 * hidden * width, transcendentals=0),
        name="backward",
    )(me, mask, mine, other, weight, hidden_back, slope)
    return stream_out[None], preact_grad[None], weight_grad[None]


def solution(mesh):
    placed = (
        P("section", "blk", None),
        P("section", "blk", None),
        P("section", None, "blk"),
        P("section", None, "blk"),
        P("section", "blk", None),
        P("section", "blk", None),
    )
    return jax.shard_map(
        body,
        mesh=mesh,
        in_specs=placed,
        out_specs=(P("section", "blk", None), P("section", None, "blk"), P("section", "blk", None)),
        check_vma=False,
    )
```

time: 162 us -> 43 us (0.27)
  waiting for transfers between devices: 75.6 us -> 9.05 us
  blocking collectives: 51.8 us -> 0 us
  Pallas kernels: 0 us -> 15.3 us
  starting transfers between devices: 0.04 us -> 14.6 us
  between operations: 14.1 us -> 0.74 us
  matrix products: 12.3 us -> 0 us
  local copies, waits for them, and re-layouts: 5.69 us -> 0.95 us
    unnamed x2 -> x0, waiting for transfers between devices: 75.6 us -> none
    all_gather x1 -> x0, blocking collectives: 51.8 us -> none  [body(): gathered = lax.all_gather(grad, 'blk', axis=0, tiled=True)]
    pallas_call x0 -> x3, Pallas kernels: none -> 15.3 us  [the longest x1 7.61 us: body(): pl.pallas_call(functools.partial(backward_kernel, order), grid=(width //...]
    ppermute x0 -> x10, starting transfers between devices: none -> 14.6 us  [exchange(): lax.ppermute(block, 'blk', [(i, i ^ bit) for i in range(lax.axis_size('bl...]
    dot_general x3 -> x0, matrix products: 12.3 us -> none  [the longest x1 4.86 us: body(): jnp.dot(hidden_now, masked, preferred_element_type=jnp.float32)]
    ppermute x0 -> x10, waiting for transfers between devices: none -> 9.05 us  [exchange(): lax.ppermute(block, 'blk', [(i, i ^ bit) for i in range(lax.axis_size('bl...]
    reshape x1 -> x0, local copies, waits for them, and re-layouts: 2.79 us -> none  [expand(): return jnp.repeat(jnp.repeat(values, BLOCK, axis=0), BLOCK, axis=1)]
    broadcast_in_dim x2 -> x0, local copies, waits for them, and re-layouts: 1.95 us -> none  [expand(): return jnp.repeat(jnp.repeat(values, BLOCK, axis=0), BLOCK, axis=1)]
  transfers between devices with their start and end apart: 1 -> 10, of which waited for: 1 -> 5; matrix products, arithmetic and copies ran while one was open for 5% -> 5% of each run, Pallas kernels for 0% -> 5%
where the time goes in v1:
time: 43 us; the launch traced here: 42.6 us
  Pallas kernels  15.3 us (36%)
  starting transfers between devices  14.6 us (34%)
  waiting for transfers between devices  9.05 us (21%)
  other arithmetic  2.02 us (5%)
  local copies, waits for them, and re-layouts  0.95 us (2%)
  between operations  0.74 us (2%)
    ppermute x10, starting transfers between devices, exchange(): lax.ppermute(block, 'blk', [(i, i ^ bit) for i in range(lax.axis_size('bl...  14.6 us
    ppermute x10, waiting for transfers between devices, exchange(): lax.ppermute(block, 'blk', [(i, i ^ bit) for i in range(lax.axis_size('bl...  9.05 us
    pallas_call x1, Pallas kernels, body(): pl.pallas_call(functools.partial(backward_kernel, order), grid=(width //...  7.61 us
    pallas_call x1, Pallas kernels, body(): pl.pallas_call(functools.partial(forward_kernel, order), grid=(width // c...  5.71 us
    pallas_call x1, Pallas kernels, body(): pl.pallas_call(functools.partial(prepare_kernel, order), out_shape=(jax.S...  1.96 us
    add x4, other arithmetic, body(): total = keep + exchange(send, bit).astype(f32)  1.27 us
  transfers between devices with their start and end apart: 10, of which 5 were waited for; matrix products, arithmetic and copies ran while one was open for 5% of the time, Pallas kernels for 5%

profile of v1, /device:TPU:0, one launch (start us, length us, event | category | flops | bytes accessed | tf_op | source)
XLA Modules:
  0.0 42.6 jit_solution(590363008206683183)
XLA Ops:
  0.6 0.0 copy-start.1
  0.6 5.7 %forward.1 = (f32[64,3072]{1,0:T(8,128)}, bf16[64,3072]{1,0:T(8,128)(2,1)}) custom-call(s32[1]{0:T(128)} %bitcast.1.me_ref, s32[4,24]{1,0:T(4,128)} %bitcast.22, bf16[128,512]{1,0:T(8,128)(2,1)} %bitcast.20, bf16[512,3072]{1,0:T(8,128)(2,1)} %bitcast.13), custom_call_target="tpu_custom_call" | custom-call | flops 402653184 | bytes 3145728 | tf_op jit(solution)/shard_map/forward/pallas_call | solution.py:137
  6.4 0.5 %collective-permute-start = (bf16[64,3072]{1,0:T(8,128)(2,1)}, bf16[64,3072]{1,0:T(8,128)(2,1)S(1)}, u32[]{:S(2)}, u32[]{:S(2)}) collective-permute-start(bf16[64,3072]{1,0:T(8,128)(2,1)} %get-tuple-element.10), channel_id=1, source_target_pairs={{0,1},{1,0},{2,3},{3,2},{4,5},{5,4},{6,7},{7,6},{8,9},{9,8},{10,11... | collective-permute-start | bytes 1179656 | tf_op jit(solution)/shard_map/ppermute | solution.py:26
  6.8 0.0 copy-done.1
  6.8 3.7 %collective-permute-start.5 = (bf16[4,3072]{1,0:T(4,128)(2,1)S(1)}, bf16[4,3072]{1,0:T(4,128)(2,1)S(1)}, u32[]{:S(2)}, u32[]{:S(2)}) collective-permute-start(bf16[4,3072]{1,0:T(4,128)(2,1)S(1)} %bitcast.15), channel_id=1, source_target_pairs={{0,16},{1,17},{2,18},{3,19},{4,20},{5,21},{6,22},{7,23},{8,24},{9,... | collective-permute-start | bytes 73736 | tf_op jit(solution)/shard_map/ppermute | solution.py:26
  10.5 0.0 collective-permute-done
  10.5 1.2 %convert_add_fusion = f32[64,3072]{1,0:T(8,128)S(1)} fusion(f32[64,3072]{1,0:T(8,128)} %get-tuple-element.9, bf16[64,3072]{1,0:T(8,128)(2,1)S(1)} %collective-permute-done), kind=kLoop, calls=%fused_computation | loop fusion | flops 393216 | bytes 1966080 | tf_op jit(solution)/shard_map/add | solution.py:161
  11.7 1.6 %collective-permute-start.1 = (bf16[32,3072]{1,0:T(8,128)(2,1)S(1)}, bf16[32,3072]{1,0:T(8,128)(2,1)S(1)}, u32[]{:S(2)}, u32[]{:S(2)}) collective-permute-start(bf16[32,3072]{1,0:T(8,128)(2,1)S(1)} %slice.58), channel_id=1, source_target_pairs={{0,2},{1,3},{2,0},{3,1},{4,6},{5,7},{6,4},{7,5},{8,10},{9,11},{10,... | collective-permute-start | bytes 589832 | tf_op jit(solution)/shard_map/ppermute | solution.py:26
  13.3 0.0 collective-permute-done.5
  13.3 1.6 %collective-permute-start.6 = (bf16[8,3072]{1,0:T(8,128)(2,1)S(1)}, bf16[8,3072]{1,0:T(8,128)(2,1)S(1)}, u32[]{:S(2)}, u32[]{:S(2)}) collective-permute-start(bf16[8,3072]{1,0:T(8,128)(2,1)S(1)} %pad_maximum_fusion.2), channel_id=1, source_target_pairs={{0,8},{1,9},{2,10},{3,11},{4,12},{5,13},{6,14},{7,15},{8,0},{9,1},... | collective-permute-start | bytes 147464 | tf_op jit(solution)/shard_map/ppermute | solution.py:26
  15.0 3.8 %collective-permute-done.1 = bf16[32,3072]{1,0:T(8,128)(2,1)S(1)} collective-permute-done((bf16[32,3072]{1,0:T(8,128)(2,1)S(1)}, bf16[32,3072]{1,0:T(8,128)(2,1)S(1)}, u32[]{:S(2)}, u32[]{:S(2)}) %collective-permute-start.1) | collective-permute-done | bytes 196640 | tf_op jit(solution)/shard_map/ppermute | solution.py:26
  18.8 1.6 %collective-permute-start.2 = (bf16[16,3072]{1,0:T(8,128)(2,1)S(1)}, bf16[16,3072]{1,0:T(8,128)(2,1)S(1)}, u32[]{:S(2)}, u32[]{:S(2)}) collective-permute-start(bf16[16,3072]{1,0:T(8,128)(2,1)S(1)} %slice.59), channel_id=1, source_target_pairs={{0,4},{1,5},{2,6},{3,7},{4,0},{5,1},{6,2},{7,3},{8,12},{9,13},{10,... | collective-permute-start | bytes 294920 | tf_op jit(solution)/shard_map/ppermute | solution.py:26
  20.4 0.0 collective-permute-done.6
  20.5 0.6 %collective-permute-start.7 = (bf16[16,3072]{1,0:T(8,128)(2,1)S(1)}, bf16[16,3072]{1,0:T(8,128)(2,1)S(1)}, u32[]{:S(2)}, u32[]{:S(2)}) collective-permute-start(bf16[16,3072]{1,0:T(8,128)(2,1)S(1)} %pad_maximum_fusion.1), channel_id=1, source_target_pairs={{0,4},{1,5},{2,6},{3,7},{4,0},{5,1},{6,2},{7,3},{8,12},{9,13},{10,... | collective-permute-start | bytes 294920 | tf_op jit(solution)/shard_map/ppermute | solution.py:26
  21.0 3.3 %collective-permute-done.2 = bf16[16,3072]{1,0:T(8,128)(2,1)S(1)} collective-permute-done((bf16[16,3072]{1,0:T(8,128)(2,1)S(1)}, bf16[16,3072]{1,0:T(8,128)(2,1)S(1)}, u32[]{:S(2)}, u32[]{:S(2)}) %collective-permute-start.2) | collective-permute-done | bytes 98336 | tf_op jit(solution)/shard_map/ppermute | solution.py:26
  24.3 1.6 %collective-permute-start.3 = (bf16[8,3072]{1,0:T(8,128)(2,1)S(1)}, bf16[8,3072]{1,0:T(8,128)(2,1)S(1)}, u32[]{:S(2)}, u32[]{:S(2)}) collective-permute-start(bf16[8,3072]{1,0:T(8,128)(2,1)S(1)} %slice.60), channel_id=1, source_target_pairs={{0,8},{1,9},{2,10},{3,11},{4,12},{5,13},{6,14},{7,15},{8,0},{9,1},... | collective-permute-start | bytes 147464 | tf_op jit(solution)/shard_map/ppermute | solution.py:26
  26.0 0.0 collective-permute-done.7
  26.0 1.6 %collective-permute-start.8 = (bf16[32,3072]{1,0:T(8,128)(2,1)S(1)}, bf16[32,3072]{1,0:T(8,128)(2,1)S(1)}, u32[]{:S(2)}, u32[]{:S(2)}) collective-permute-start(bf16[32,3072]{1,0:T(8,128)(2,1)S(1)} %pad_maximum_fusion), channel_id=1, source_target_pairs={{0,2},{1,3},{2,0},{3,1},{4,6},{5,7},{6,4},{7,5},{8,10},{9,11},{10,... | collective-permute-start | bytes 589832 | tf_op jit(solution)/shard_map/ppermute | solution.py:26
  27.6 0.9 %collective-permute-done.3 = bf16[8,3072]{1,0:T(8,128)(2,1)S(1)} collective-permute-done((bf16[8,3072]{1,0:T(8,128)(2,1)S(1)}, bf16[8,3072]{1,0:T(8,128)(2,1)S(1)}, u32[]{:S(2)}, u32[]{:S(2)}) %collective-permute-start.3) | collective-permute-done | bytes 49184 | tf_op jit(solution)/shard_map/ppermute | solution.py:26
  28.5 1.9 %collective-permute-start.4 = (bf16[4,3072]{1,0:T(4,128)(2,1)S(1)}, bf16[4,3072]{1,0:T(4,128)(2,1)S(1)}, u32[]{:S(2)}, u32[]{:S(2)}) collective-permute-start(bf16[4,3072]{1,0:T(4,128)(2,1)S(1)} %slice.61), channel_id=1, source_target_pairs={{0,16},{1,17},{2,18},{3,19},{4,20},{5,21},{6,22},{7,23},{8,24},{9,... | collective-permute-start | bytes 73736 | tf_op jit(solution)/shard_map/ppermute | solution.py:26
  30.4 2.0 %prepare.1 = (bf16[128,512]{1,0:T(8,128)(2,1)}, f32[128,512]{1,0:T(8,128)}) custom-call(s32[1]{0:T(128)} %bitcast.1.me_ref, bf16[128,512]{1,0:T(8,128)(2,1)} %bitcast.21), custom_call_target="tpu_custom_call" | custom-call | tf_op jit(solution)/shard_map/prepare/pallas_call | solution.py:148
  32.3 0.0 collective-permute-done.8
  32.3 0.1 concatenate.18.mine_ref
  32.5 0.0 copy-start
  32.5 0.1 collective-permute-start.9
  32.6 0.7 %collective-permute-done.4 = bf16[4,3072]{1,0:T(4,128)(2,1)S(1)} collective-permute-done((bf16[4,3072]{1,0:T(4,128)(2,1)S(1)}, bf16[4,3072]{1,0:T(4,128)(2,1)S(1)}, u32[]{:S(2)}, u32[]{:S(2)}) %collective-permute-start.4) | collective-permute-done | bytes 24608 | tf_op jit(solution)/shard_map/ppermute | solution.py:26
  33.3 0.0 copy-done.3
  33.3 0.6 %fusion.2 = bf16[1,4,3072]{2,1,0:T(4,128)(2,1)} fusion(bf16[4,3072]{1,0:T(4,128)(2,1)S(1)} %collective-permute-done.4, f32[8,3072]{1,0:T(8,128)S(1)} %slice_add_fusion.2, bf16[1,4,3072]{2,1,0:T(4,128)(2,1)S(1)} %copy-done.3), kind=kLoop, calls=%fused_computation.14 | loop fusion | flops 61440 | bytes 122880 | tf_op jit(solution)/shard_map/broadcast_in_dim | solution.py:176
  33.9 0.3 collective-permute-done.9.other_ref
  34.3 0.0 copy-done
  34.3 0.7 %copy-done.2 = bf16[64,3072]{1,0:T(8,128)(2,1)} copy-done((bf16[64,3072]{1,0:T(8,128)(2,1)}, bf16[64,3072]{1,0:T(8,128)(2,1)S(1)}, u32[]{:S(2)}) %copy-start.2) | copy-done | bytes 393240
  35.0 7.6 %backward.1 = (bf16[512,3072]{1,0:T(8,128)(2,1)}, bf16[128,512]{1,0:T(8,128)(2,1)}) custom-call(s32[1]{0:T(128)} %bitcast.1.me_ref, s32[4,24]{1,0:T(4,128)} %bitcast.23, bf16[64,3072]{1,0:T(8,128)(2,1)} %copy-done, bf16[64,3072]{1,0:T(8,128)(2,1)} %copy-done.2, bf16[512,3072]{1,0:T(8,128)(2,1)} %bitcast.14, bf16[128,512]{1,0:T(8,128)(2,1)} %get-tuple-element.11.hidden_ref, ...), custom_call_target="tpu_custom_call" | custom-call | flops 805306368 | bytes 6291456 | tf_op jit(solution)/shard_map/backward/pallas_call | solution.py:166
  (12 shorter events, 0.3 us)
Async XLA Ops:
  0.6 6.2 %copy-start.1 = (bf16[1,4,3072]{2,1,0:T(4,128)(2,1)S(1)}, bf16[1,4,3072]{2,1,0:T(4,128)(2,1)}, u32[]{:S(2)}) copy-start(bf16[1,4,3072]{2,1,0:T(4,128)(2,1)} %param.7) | copy-start | bytes 73732
  6.4 26.9 %copy-start.3 = (bf16[1,4,3072]{2,1,0:T(4,128)(2,1)S(1)}, bf16[1,4,3072]{2,1,0:T(4,128)(2,1)}, u32[]{:S(2)}) copy-start(bf16[1,4,3072]{2,1,0:T(4,128)(2,1)} %param.6) | copy-start | bytes 73732
  6.4 4.1 %collective-permute-start = (bf16[64,3072]{1,0:T(8,128)(2,1)}, bf16[64,3072]{1,0:T(8,128)(2,1)S(1)}, u32[]{:S(2)}, u32[]{:S(2)}) collective-permute-start(bf16[64,3072]{1,0:T(8,128)(2,1)} %get-tuple-element.10), channel_id=1, source_target_pairs={{0,1},{1,0},{2,3},{3,2},{4,5},{5,4},{6,7},{7,6},{8,9},{9,8},{10,11... | collective-permute-start | bytes 1179656 | tf_op jit(solution)/shard_map/ppermute | solution.py:26
  6.8 6.5 %collective-permute-start.5 = (bf16[4,3072]{1,0:T(4,128)(2,1)S(1)}, bf16[4,3072]{1,0:T(4,128)(2,1)S(1)}, u32[]{:S(2)}, u32[]{:S(2)}) collective-permute-start(bf16[4,3072]{1,0:T(4,128)(2,1)S(1)} %bitcast.15), channel_id=1, source_target_pairs={{0,16},{1,17},{2,18},{3,19},{4,20},{5,21},{6,22},{7,23},{8,24},{9,... | collective-permute-start | bytes 73736 | tf_op jit(solution)/shard_map/ppermute | solution.py:26
  11.7 7.0 %collective-permute-start.1 = (bf16[32,3072]{1,0:T(8,128)(2,1)S(1)}, bf16[32,3072]{1,0:T(8,128)(2,1)S(1)}, u32[]{:S(2)}, u32[]{:S(2)}) collective-permute-start(bf16[32,3072]{1,0:T(8,128)(2,1)S(1)} %slice.58), channel_id=1, source_target_pairs={{0,2},{1,3},{2,0},{3,1},{4,6},{5,7},{6,4},{7,5},{8,10},{9,11},{10,... | collective-permute-start | bytes 589832 | tf_op jit(solution)/shard_map/ppermute | solution.py:26
  13.3 7.1 %collective-permute-start.6 = (bf16[8,3072]{1,0:T(8,128)(2,1)S(1)}, bf16[8,3072]{1,0:T(8,128)(2,1)S(1)}, u32[]{:S(2)}, u32[]{:S(2)}) collective-permute-start(bf16[8,3072]{1,0:T(8,128)(2,1)S(1)} %pad_maximum_fusion.2), channel_id=1, source_target_pairs={{0,8},{1,9},{2,10},{3,11},{4,12},{5,13},{6,14},{7,15},{8,0},{9,1},... | collective-permute-start | bytes 147464 | tf_op jit(solution)/shard_map/ppermute | solution.py:26
  18.8 5.5 %collective-permute-start.2 = (bf16[16,3072]{1,0:T(8,128)(2,1)S(1)}, bf16[16,3072]{1,0:T(8,128)(2,1)S(1)}, u32[]{:S(2)}, u32[]{:S(2)}) collective-permute-start(bf16[16,3072]{1,0:T(8,128)(2,1)S(1)} %slice.59), channel_id=1, source_target_pairs={{0,4},{1,5},{2,6},{3,7},{4,0},{5,1},{6,2},{7,3},{8,12},{9,13},{10,... | collective-permute-start | bytes 294920 | tf_op jit(solution)/shard_map/ppermute | solution.py:26
  20.5 5.5 %collective-permute-start.7 = (bf16[16,3072]{1,0:T(8,128)(2,1)S(1)}, bf16[16,3072]{1,0:T(8,128)(2,1)S(1)}, u32[]{:S(2)}, u32[]{:S(2)}) collective-permute-start(bf16[16,3072]{1,0:T(8,128)(2,1)S(1)} %pad_maximum_fusion.1), channel_id=1, source_target_pairs={{0,4},{1,5},{2,6},{3,7},{4,0},{5,1},{6,2},{7,3},{8,12},{9,13},{10,... | collective-permute-start | bytes 294920 | tf_op jit(solution)/shard_map/ppermute | solution.py:26
  24.3 4.2 %collective-permute-start.3 = (bf16[8,3072]{1,0:T(8,128)(2,1)S(1)}, bf16[8,3072]{1,0:T(8,128)(2,1)S(1)}, u32[]{:S(2)}, u32[]{:S(2)}) collective-permute-start(bf16[8,3072]{1,0:T(8,128)(2,1)S(1)} %slice.60), channel_id=1, source_target_pairs={{0,8},{1,9},{2,10},{3,11},{4,12},{5,13},{6,14},{7,15},{8,0},{9,1},... | collective-permute-start | bytes 147464 | tf_op jit(solution)/shard_map/ppermute | solution.py:26
  26.0 6.3 %collective-permute-start.8 = (bf16[32,3072]{1,0:T(8,128)(2,1)S(1)}, bf16[32,3072]{1,0:T(8,128)(2,1)S(1)}, u32[]{:S(2)}, u32[]{:S(2)}) collective-permute-start(bf16[32,3072]{1,0:T(8,128)(2,1)S(1)} %pad_maximum_fusion), channel_id=1, source_target_pairs={{0,2},{1,3},{2,0},{3,1},{4,6},{5,7},{6,4},{7,5},{8,10},{9,11},{10,... | collective-permute-start | bytes 589832 | tf_op jit(solution)/shard_map/ppermute | solution.py:26
  28.5 4.8 %collective-permute-start.4 = (bf16[4,3072]{1,0:T(4,128)(2,1)S(1)}, bf16[4,3072]{1,0:T(4,128)(2,1)S(1)}, u32[]{:S(2)}, u32[]{:S(2)}) collective-permute-start(bf16[4,3072]{1,0:T(4,128)(2,1)S(1)} %slice.61), channel_id=1, source_target_pairs={{0,16},{1,17},{2,18},{3,19},{4,20},{5,21},{6,22},{7,23},{8,24},{9,... | collective-permute-start | bytes 73736 | tf_op jit(solution)/shard_map/ppermute | solution.py:26
  32.5 1.8 %copy-start = (bf16[64,3072]{1,0:T(8,128)(2,1)}, bf16[64,3072]{1,0:T(8,128)(2,1)S(1)}, u32[]{:S(2)}) copy-start(bf16[64,3072]{1,0:T(8,128)(2,1)S(1)} %concatenate.18.mine_ref) | copy-start | bytes 1179652
  32.5 1.8 %collective-permute-start.9 = (bf16[64,3072]{1,0:T(8,128)(2,1)S(1)}, bf16[64,3072]{1,0:T(8,128)(2,1)S(1)}, u32[]{:S(2)}, u32[]{:S(2)}) collective-permute-start(bf16[64,3072]{1,0:T(8,128)(2,1)S(1)} %concatenate.18.mine_ref), channel_id=1, source_target_pairs={{0,1},{1,0},{2,3},{3,2},{4,5},{5,4},{6,7},{7,6},{8,9},{9,8},{10,11... | collective-permute-start | bytes 1179656 | tf_op jit(solution)/shard_map/ppermute | solution.py:26
  34.3 0.8 %copy-start.2 = (bf16[64,3072]{1,0:T(8,128)(2,1)}, bf16[64,3072]{1,0:T(8,128)(2,1)S(1)}, u32[]{:S(2)}) copy-start(bf16[64,3072]{1,0:T(8,128)(2,1)S(1)} %collective-permute-done.9.other_ref) | copy-start | bytes 1179652

commit v2 on v0

v2 whole, which is shorter than its diff:
```python
import functools
import math

import jax
import jax.numpy as jnp
from jax import lax
from jax.experimental import pallas as pl
from jax.experimental.pallas import tpu as pltpu
from jax.sharding import PartitionSpec as P

BLOCK = 128
SCALE = math.sqrt(2.0 / math.pi)
CUBIC = 0.044715
CHUNK = 512
LIMIT = 16 * 1024 * 1024
SEND_BYTES = 6_000_000
KEEP_BYTES = 3_000_000
bf16 = jnp.bfloat16
f32 = jnp.float32


def shifted(block, axis, distance):
    devices = range(lax.axis_size(axis))
    route = [(i - distance, i) for i in devices if i - distance in devices]
    return lax.ppermute(block, axis, route)


def exchange(block, bit):
    return lax.ppermute(block, "blk", [(i, i ^ bit) for i in range(lax.axis_size("blk"))])


def combinations(bits):
    found = [0]
    for bit in bits[::-1]:
        found += [bit ^ other for other in found]
    return found


def own_token(place, me, order, each):
    group, within = place // each, place % each
    owner = me
    for k, bit in enumerate(order):
        owner = owner ^ jnp.where((group >> (len(order) - 1 - k)) & 1 == 1, bit, 0)
    return owner * each + within


def reorder(me, tokens, order, back=False):
    rows = lax.broadcasted_iota(jnp.int32, (tokens, tokens), 1 if back else 0)
    cols = lax.broadcasted_iota(jnp.int32, (tokens, tokens), 0 if back else 1)
    return (own_token(rows, me, order, tokens >> len(order)) == cols).astype(bf16)


def columns(width):
    chunk = CHUNK if width % CHUNK == 0 else BLOCK
    return [pl.ds(first, chunk) for first in range(0, width, chunk)]


def keep_blocks(array, mask_ref, i, first):
    blocks = []
    for j in range(array.shape[1] // BLOCK):
        block = array[:, j * BLOCK : (j + 1) * BLOCK]
        blocks.append(jnp.where(mask_ref[i, first + j] != 0, block, jnp.zeros_like(block)))
    return jnp.concatenate(blocks, axis=1)


def gelu_and_slope(x):
    square = x * x
    t = jnp.tanh(SCALE * (x + CUBIC * x * square))
    half = 0.5 * (1.0 + t)
    slope = half + 0.5 * x * (1.0 - t * t) * (SCALE * (1.0 + 3.0 * CUBIC * square))
    return x * half, slope


def send_kernel(
    order, me_ref, mask_hbm, now_hbm, back_hbm, w_hbm, send_ref, hidden_ref, masked_ref, back_ref, mask_ref, now_ref, w_ref, sems
):
    bands = w_ref.shape[0] // BLOCK
    pairs = [(now_hbm, now_ref), (mask_hbm, mask_ref)]
    pairs += [(w_hbm.at[pl.ds(i * BLOCK, BLOCK)], w_ref.at[pl.ds(i * BLOCK, BLOCK)]) for i in range(bands)]
    pairs += [(back_hbm, back_ref)]
    copies = [pltpu.make_async_copy(source, target, sems.at[k]) for k, (source, target) in enumerate(pairs)]
    for copy in copies:
        copy.start()
    tokens = now_ref.shape[0]
    moves = reorder(me_ref[0], tokens, order)
    copies[0].wait()
    hidden, _ = gelu_and_slope(jnp.dot(moves, now_ref[...], preferred_element_type=f32))
    hidden_ref[...] = hidden.astype(bf16)
    copies[1].wait()
    for i in range(bands):
        copies[2 + i].wait()
        rows = pl.ds(i * BLOCK, BLOCK)
        masked_ref[rows] = keep_blocks(w_ref[rows], mask_ref, i, 0)
    half = send_ref.shape[0]
    for part in columns(w_ref.shape[1]):
        product = jnp.dot(hidden_ref[half:], masked_ref[:, part], preferred_element_type=f32)
        send_ref[:, part] = product.astype(bf16)
    copies[-1].wait()


def keep_kernel(order, me_ref, hidden_now_ref, masked_ref, back_ref, keep_ref, hidden_ref, slope_ref):
    half = keep_ref.shape[0]
    for part in columns(masked_ref.shape[1]):
        keep_ref[:, part] = jnp.dot(hidden_now_ref[:half], masked_ref[:, part], preferred_element_type=f32)
    moves = reorder(me_ref[0], back_ref.shape[0], order)
    hidden, slope = gelu_and_slope(jnp.dot(moves, back_ref[...], preferred_element_type=f32))
    hidden_ref[...] = hidden.astype(bf16)
    slope_ref[...] = slope


def backward_kernel(order, pieces, me_ref, mask_ref, *refs):
    grads = refs[:pieces]
    w_ref, hidden_ref, slope_ref, wg_hbm, pg_ref, wg_ref, sems = refs[pieces:]
    tokens = pg_ref.shape[0]
    results = []
    total = jnp.zeros((tokens, w_ref.shape[0]), f32)
    for c, part in enumerate(columns(w_ref.shape[1])):
        grad = jnp.concatenate([g[:, part] for g in grads], axis=0)
        full = lax.dot_general(hidden_ref[...], grad, (((0,), (0,)), ((), ())), preferred_element_type=f32)
        for i in range(w_ref.shape[0] // BLOCK):
            rows = pl.ds(i * BLOCK, BLOCK)
            wg_ref[rows, part] = keep_blocks(full[i * BLOCK : (i + 1) * BLOCK], mask_ref, i, part.start // BLOCK).astype(bf16)
        result = pltpu.make_async_copy(wg_ref.at[:, part], wg_hbm.at[:, part], sems.at[c])
        result.start()
        results.append(result)
        total += lax.dot_general(grad, w_ref[:, part], (((1,), (1,)), ((), ())), preferred_element_type=f32)
    moved = (total * slope_ref[...]).astype(bf16)
    back = reorder(me_ref[0], tokens, order, back=True)
    pg_ref[...] = jnp.dot(back, moved, preferred_element_type=f32).astype(bf16)
    for result in results:
        result.wait()


SMEM = functools.partial(pl.BlockSpec, memory_space=pltpu.SMEM)
VMEM = functools.partial(pl.BlockSpec, memory_space=pltpu.VMEM)
HBM = functools.partial(pl.BlockSpec, memory_space=pltpu.HBM)


def body(stream_sent, grad_sent, preact_now, preact_back, down_weight, block_mask):
    sections = lax.axis_size("section")
    stream, grad = stream_sent, grad_sent
    if sections > 1:
        section_index = lax.axis_index("section")
        stream = jnp.where(section_index == 0, stream, shifted(stream, "section", 1))
        grad = jnp.where(section_index == sections - 1, grad, shifted(grad, "section", -1))
    stream, grad, mask, weight = stream[0], grad[0], block_mask[0], down_weight[0]
    pre_now, pre_back = preact_now[0], preact_back[0]
    held = [pltpu.with_memory_space_constraint(x, pltpu.HBM) for x in (mask, pre_now, pre_back, weight)]
    tokens, hidden = preact_now.shape[1:]
    width = down_weight.shape[2]
    devices = lax.axis_size("blk")
    bits = [1 << k for k in range(devices.bit_length() - 1)]
    near, plane, far = bits[:1], bits[1:3], bits[3:]
    scatter_order = near + plane + far
    gather_order = near + plane + far[::-1]
    me = lax.axis_index("blk").astype(jnp.int32).reshape(1)
    chunks = len(columns(width))
    half = tokens // 2

    def shape(dtype, *dims):
        return jax.ShapeDtypeStruct(dims, dtype)

    params = pltpu.CompilerParams(vmem_limit_bytes=LIMIT)
    send, hidden_now, masked, held_back = pl.pallas_call(
        functools.partial(send_kernel, scatter_order),
        out_shape=(shape(bf16, half, width), shape(bf16, tokens, hidden), shape(bf16, hidden, width), shape(bf16, tokens, hidden)),
        in_specs=[SMEM()] + [HBM()] * 4,
        out_specs=(VMEM(),) * 4,
        scratch_shapes=[
            pltpu.SMEM(mask.shape, jnp.int32),
            pltpu.VMEM((tokens, hidden), bf16),
            pltpu.VMEM((hidden, width), bf16),
            pltpu.SemaphoreType.DMA((3 + hidden // BLOCK,)),
        ],
        compiler_params=params,
        cost_estimate=pl.CostEstimate(flops=tokens * hidden * width, bytes_accessed=SEND_BYTES, transcendentals=0),
        name="send",
    )(me, *held)

    mine = grad
    for k, bit in enumerate(far):
        other = exchange(mine, bit)
        if k == 0:
            send, other = lax.optimization_barrier((send, other))
        mine = jnp.concatenate([mine, other], axis=0)

    keep, hidden_back, slope = pl.pallas_call(
        functools.partial(keep_kernel, gather_order),
        out_shape=(shape(f32, half, width), shape(bf16, tokens, hidden), shape(f32, tokens, hidden)),
        in_specs=[SMEM()] + [VMEM()] * 3,
        out_specs=(VMEM(),) * 3,
        compiler_params=params,
        cost_estimate=pl.CostEstimate(flops=tokens * hidden * width, bytes_accessed=KEEP_BYTES, transcendentals=0),
        name="keep",
    )(me, hidden_now, masked, held_back)

    total = keep + exchange(send, near[0]).astype(f32)
    for group in [plane] + [[bit] for bit in far]:
        masks = combinations(group)
        parts = jnp.split(total, len(masks), axis=0)
        total = parts[0]
        for part, bit in zip(parts[1:], masks[1:]):
            total = total + exchange(part.astype(bf16), bit).astype(f32)
    stream_out = (stream.astype(f32) + total).astype(bf16)

    grads = [mine] + [exchange(mine, bit) for bit in combinations(plane)[1:]]
    grads += [exchange(piece, near[0]) for piece in grads]

    weight_grad, preact_grad = pl.pallas_call(
        functools.partial(backward_kernel, gather_order, len(grads)),
        out_shape=(jax.ShapeDtypeStruct((hidden, width), bf16), jax.ShapeDtypeStruct((tokens, hidden), bf16)),
        in_specs=[SMEM(), SMEM()] + [VMEM()] * (len(grads) + 3),
        out_specs=(HBM(), VMEM()),
        scratch_shapes=[
            pltpu.VMEM((hidden, width), bf16),
            pltpu.SemaphoreType.DMA((chunks,)),
        ],
        compiler_params=params,
        cost_estimate=pl.CostEstimate(flops=4 * tokens * hidden * width, bytes_accessed=4 * hidden * width, transcendentals=0),
        name="backward",
    )(me, mask, *grads, masked, hidden_back, slope)
    return stream_out[None], preact_grad[None], weight_grad[None]


def solution(mesh):
    placed = (
        P("section", "blk", None),
        P("section", "blk", None),
        P("section", None, "blk"),
        P("section", None, "blk"),
        P("section", "blk", None),
        P("section", "blk", None),
    )
    return jax.shard_map(
        body,
        mesh=mesh,
        in_specs=placed,
        out_specs=(P("section", "blk", None), P("section", None, "blk"), P("section", "blk", None)),
        check_vma=False,
    )
```

time: 162 us -> 29.1 us (0.18)
  waiting for transfers between devices: 75.6 us -> 2.44 us
  blocking collectives: 51.8 us -> 0 us
  starting transfers between devices: 0.04 us -> 17.4 us
  between operations: 14.1 us -> 0.78 us
  matrix products: 12.3 us -> 0 us
  Pallas kernels: 0 us -> 7.43 us
  local copies, waits for them, and re-layouts: 5.69 us -> 0.06 us
    unnamed x2 -> x0, waiting for transfers between devices: 75.6 us -> none
    all_gather x1 -> x0, blocking collectives: 51.8 us -> none  [body(): gathered = lax.all_gather(grad, 'blk', axis=0, tiled=True)]
    ppermute x0 -> x15, starting transfers between devices: none -> 17.4 us  [exchange(): lax.ppermute(block, 'blk', [(i, i ^ bit) for i in range(lax.axis_size('bl...]
    dot_general x3 -> x0, matrix products: 12.3 us -> none  [the longest x1 4.86 us: body(): jnp.dot(hidden_now, masked, preferred_element_type=jnp.float32)]
    pallas_call x0 -> x3, Pallas kernels: none -> 7.43 us  [the longest x1 3.88 us: body(): pl.pallas_call(functools.partial(backward_kernel, gather_order, len(grads...]
    reshape x1 -> x0, local copies, waits for them, and re-layouts: 2.79 us -> none  [expand(): return jnp.repeat(jnp.repeat(values, BLOCK, axis=0), BLOCK, axis=1)]
    ppermute x0 -> x15, waiting for transfers between devices: none -> 2.44 us  [exchange(): lax.ppermute(block, 'blk', [(i, i ^ bit) for i in range(lax.axis_size('bl...]
    broadcast_in_dim x2 -> x0, local copies, waits for them, and re-layouts: 1.95 us -> none  [expand(): return jnp.repeat(jnp.repeat(values, BLOCK, axis=0), BLOCK, axis=1)]
  transfers between devices with their start and end apart: 1 -> 15, of which waited for: 1 -> 4; matrix products, arithmetic and copies ran while one was open for 5% -> 1% of each run, Pallas kernels for 0% -> 16%
where the time goes in v2:
time: 29.1 us; the launch traced here: 29 us
  starting transfers between devices  17.4 us (60%)
  Pallas kernels  7.43 us (26%)
  waiting for transfers between devices  2.44 us (8%)
  other arithmetic  0.85 us (3%)
  between operations  0.78 us (3%)
    ppermute x15, starting transfers between devices, exchange(): lax.ppermute(block, 'blk', [(i, i ^ bit) for i in range(lax.axis_size('bl...  17.4 us
    pallas_call x1, Pallas kernels, body(): pl.pallas_call(functools.partial(backward_kernel, gather_order, len(grads...  3.88 us
    pallas_call x1, Pallas kernels, body(): pl.pallas_call(functools.partial(send_kernel, scatter_order), out_shape=(...  2.7 us
    ppermute x15, waiting for transfers between devices, exchange(): lax.ppermute(block, 'blk', [(i, i ^ bit) for i in range(lax.axis_size('bl...  2.44 us
    pallas_call x1, Pallas kernels, body(): pl.pallas_call(functools.partial(keep_kernel, gather_order), out_shape=(s...  0.84 us
    broadcast_in_dim x1, other arithmetic, body(): return (stream_out[None], preact_grad[None], weight_grad[None])  0.63 us
  transfers between devices with their start and end apart: 15, of which 4 were waited for; matrix products, arithmetic and copies ran while one was open for 1% of the time, Pallas kernels for 16%

profile of v2, /device:TPU:0, one launch (start us, length us, event | category | flops | bytes accessed | tf_op | source)
XLA Modules:
  0.0 29.0 jit_solution(15588490719367822364)
XLA Ops:
  0.6 3.1 %collective-permute-start = (bf16[4,3072]{1,0:T(4,128)(2,1)}, bf16[4,3072]{1,0:T(4,128)(2,1)S(1)}, u32[]{:S(2)}, u32[]{:S(2)}) collective-permute-start(bf16[4,3072]{1,0:T(4,128)(2,1)} %bitcast.18), channel_id=1, source_target_pairs={{0,8},{1,9},{2,10},{3,11},{4,12},{5,13},{6,14},{7,15},{8,0},{9,1},... | collective-permute-start | bytes 73736 | tf_op jit(solution)/shard_map/ppermute | solution.py:29
  3.7 2.7 %send.1 = (bf16[64,3072]{1,0:T(8,128)(2,1)S(1)}, bf16[128,512]{1,0:T(8,128)(2,1)S(1)}, bf16[512,3072]{1,0:T(8,128)(2,1)S(1)}, bf16[128,512]{1,0:T(8,128)(2,1)S(1)}) custom-call(s32[1]{0:T(128)} %bitcast.1.me_ref, s32[4,24]{1,0:T(4,128)} %bitcast.13, bf16[128,512]{1,0:T(8,128)(2,1)} %bitcast.16, bf16[128,512]{1,0:T(8,128)(2,1)} %bitcast.17, ...), custom_call_target="tpu_custom_call" | custom-call | flops 201326592 | bytes 6000000 | tf_op jit(solution)/shard_map/send/pallas_call | solution.py:164
  6.4 0.0 collective-permute-done
  6.4 0.1 collective-permute-start.1
  6.5 0.0 copy-start
  6.5 0.8 %keep.1 = (f32[64,3072]{1,0:T(8,128)S(1)}, bf16[128,512]{1,0:T(8,128)(2,1)S(1)}, f32[128,512]{1,0:T(8,128)S(1)}) custom-call(s32[1]{0:T(128)} %bitcast.1.me_ref, bf16[128,512]{1,0:T(8,128)(2,1)S(1)} %get-tuple-element.14.hidden_now_ref, bf16[512,3072]{1,0:T(8,128)(2,1)S(1)} %get-tuple-element.15.masked_ref.refs_8_, ...), custom_call_target="tpu_custom_call" | custom-call | flops 201326592 | bytes 3000000 | tf_op jit(solution)/shard_map/keep/pallas_call | solution.py:187
  7.4 2.6 %collective-permute-start.7 = (bf16[8,3072]{1,0:T(8,128)(2,1)S(1)}, bf16[8,3072]{1,0:T(8,128)(2,1)S(1)}, u32[]{:S(2)}, u32[]{:S(2)}) collective-permute-start(bf16[8,3072]{1,0:T(8,128)(2,1)S(1)} %pad_maximum_fusion.1), channel_id=1, source_target_pairs={{0,16},{1,17},{2,18},{3,19},{4,20},{5,21},{6,22},{7,23},{8,24},{9,... | collective-permute-start | bytes 147464 | tf_op jit(solution)/shard_map/ppermute | solution.py:29
  10.1 0.0 collective-permute-done.1
  10.1 0.1 fusion.5
  10.2 0.0 copy-start.2
  10.2 2.5 %collective-permute-start.4 = (bf16[16,3072]{1,0:T(8,128)(2,1)S(1)}, bf16[16,3072]{1,0:T(8,128)(2,1)S(1)}, u32[]{:S(2)}, u32[]{:S(2)}) collective-permute-start(bf16[16,3072]{1,0:T(8,128)(2,1)S(1)} %get-tuple-element.28), channel_id=1, source_target_pairs={{0,6},{1,7},{2,4},{3,5},{4,2},{5,3},{6,0},{7,1},{8,14},{9,15},{10,... | collective-permute-start | bytes 294920 | tf_op jit(solution)/shard_map/ppermute | solution.py:29
  12.7 0.5 %collective-permute-start.3 = (bf16[16,3072]{1,0:T(8,128)(2,1)S(1)}, bf16[16,3072]{1,0:T(8,128)(2,1)S(1)}, u32[]{:S(2)}, u32[]{:S(2)}) collective-permute-start(bf16[16,3072]{1,0:T(8,128)(2,1)S(1)} %get-tuple-element.29), channel_id=1, source_target_pairs={{0,2},{1,3},{2,0},{3,1},{4,6},{5,7},{6,4},{7,5},{8,10},{9,11},{10,... | collective-permute-start | bytes 294920 | tf_op jit(solution)/shard_map/ppermute | solution.py:29
  13.3 0.5 %collective-permute-start.2 = (bf16[16,3072]{1,0:T(8,128)(2,1)S(1)}, bf16[16,3072]{1,0:T(8,128)(2,1)S(1)}, u32[]{:S(2)}, u32[]{:S(2)}) collective-permute-start(bf16[16,3072]{1,0:T(8,128)(2,1)S(1)} %get-tuple-element.27), channel_id=1, source_target_pairs={{0,4},{1,5},{2,6},{3,7},{4,0},{5,1},{6,2},{7,3},{8,12},{9,13},{10,... | collective-permute-start | bytes 294920 | tf_op jit(solution)/shard_map/ppermute | solution.py:29
  13.8 0.0 collective-permute-done.7
  13.8 1.6 %collective-permute-start.8 = (bf16[16,3072]{1,0:T(8,128)(2,1)S(1)}, bf16[16,3072]{1,0:T(8,128)(2,1)S(1)}, u32[]{:S(2)}, u32[]{:S(2)}) collective-permute-start(bf16[16,3072]{1,0:T(8,128)(2,1)S(1)} %pad_maximum_fusion.refs_0_), channel_id=1, source_target_pairs={{0,4},{1,5},{2,6},{3,7},{4,0},{5,1},{6,2},{7,3},{8,12},{9,13},{10,... | collective-permute-start | bytes 294920 | tf_op jit(solution)/shard_map/ppermute | solution.py:29
  15.4 1.5 %collective-permute-start.9 = (bf16[16,3072]{1,0:T(8,128)(2,1)S(1)}, bf16[16,3072]{1,0:T(8,128)(2,1)S(1)}, u32[]{:S(2)}, u32[]{:S(2)}) collective-permute-start(bf16[16,3072]{1,0:T(8,128)(2,1)S(1)} %pad_maximum_fusion.refs_0_), channel_id=1, source_target_pairs={{0,2},{1,3},{2,0},{3,1},{4,6},{5,7},{6,4},{7,5},{8,10},{9,11},{10,... | collective-permute-start | bytes 294920 | tf_op jit(solution)/shard_map/ppermute | solution.py:29
  16.9 2.4 %collective-permute-start.10 = (bf16[16,3072]{1,0:T(8,128)(2,1)S(1)}, bf16[16,3072]{1,0:T(8,128)(2,1)S(1)}, u32[]{:S(2)}, u32[]{:S(2)}) collective-permute-start(bf16[16,3072]{1,0:T(8,128)(2,1)S(1)} %pad_maximum_fusion.refs_0_), channel_id=1, source_target_pairs={{0,6},{1,7},{2,4},{3,5},{4,2},{5,3},{6,0},{7,1},{8,14},{9,15},{10,... | collective-permute-start | bytes 294920 | tf_op jit(solution)/shard_map/ppermute | solution.py:29
  19.3 0.0 collective-permute-done.3
  19.3 1.3 %collective-permute-start.5 = (bf16[8,3072]{1,0:T(8,128)(2,1)S(1)}, bf16[8,3072]{1,0:T(8,128)(2,1)S(1)}, u32[]{:S(2)}, u32[]{:S(2)}) collective-permute-start(bf16[8,3072]{1,0:T(8,128)(2,1)S(1)} %split.60), channel_id=1, source_target_pairs={{0,8},{1,9},{2,10},{3,11},{4,12},{5,13},{6,14},{7,15},{8,0},{9,1},... | collective-permute-start | bytes 147464 | tf_op jit(solution)/shard_map/ppermute | solution.py:29
  20.6 0.0 collective-permute-start.11
  20.6 0.5 %collective-permute-done.8.refs_1_ = bf16[16,3072]{1,0:T(8,128)(2,1)S(1)} collective-permute-done((bf16[16,3072]{1,0:T(8,128)(2,1)S(1)}, bf16[16,3072]{1,0:T(8,128)(2,1)S(1)}, u32[]{:S(2)}, u32[]{:S(2)}) %collective-permute-start.8) | collective-permute-done | bytes 98336 | tf_op jit(solution)/shard_map/ppermute | solution.py:29
  21.1 0.0 collective-permute-start.12
  21.2 0.0 collective-permute-done.9.refs_2_
  21.2 0.5 %collective-permute-start.13 = (bf16[16,3072]{1,0:T(8,128)(2,1)S(1)}, bf16[16,3072]{1,0:T(8,128)(2,1)S(1)}, u32[]{:S(2)}, u32[]{:S(2)}) collective-permute-start(bf16[16,3072]{1,0:T(8,128)(2,1)S(1)} %collective-permute-done.9.refs_2_), channel_id=1, source_target_pairs={{0,1},{1,0},{2,3},{3,2},{4,5},{5,4},{6,7},{7,6},{8,9},{9,8},{10,11... | collective-permute-start | bytes 294920 | tf_op jit(solution)/shard_map/ppermute | solution.py:29
  21.6 0.9 %collective-permute-done.10.refs_3_ = bf16[16,3072]{1,0:T(8,128)(2,1)S(1)} collective-permute-done((bf16[16,3072]{1,0:T(8,128)(2,1)S(1)}, bf16[16,3072]{1,0:T(8,128)(2,1)S(1)}, u32[]{:S(2)}, u32[]{:S(2)}) %collective-permute-start.10) | collective-permute-done | bytes 98336 | tf_op jit(solution)/shard_map/ppermute | solution.py:29
  22.5 1.0 %collective-permute-done.5 = bf16[8,3072]{1,0:T(8,128)(2,1)S(1)} collective-permute-done((bf16[8,3072]{1,0:T(8,128)(2,1)S(1)}, bf16[8,3072]{1,0:T(8,128)(2,1)S(1)}, u32[]{:S(2)}, u32[]{:S(2)}) %collective-permute-start.5) | collective-permute-done | bytes 49184 | tf_op jit(solution)/shard_map/ppermute | solution.py:29
  23.5 0.8 %collective-permute-start.6 = (bf16[4,3072]{1,0:T(4,128)(2,1)S(1)}, bf16[4,3072]{1,0:T(4,128)(2,1)S(1)}, u32[]{:S(2)}, u32[]{:S(2)}) collective-permute-start(bf16[4,3072]{1,0:T(4,128)(2,1)S(1)} %split.61), channel_id=1, source_target_pairs={{0,16},{1,17},{2,18},{3,19},{4,20},{5,21},{6,22},{7,23},{8,24},{9,... | collective-permute-start | bytes 73736 | tf_op jit(solution)/shard_map/ppermute | solution.py:29
  24.3 0.0 collective-permute-done.11.refs_4_
  24.3 0.0 collective-permute-done.14.refs_7_
  24.4 3.9 %backward.1 = (bf16[512,3072]{1,0:T(8,128)(2,1)}, bf16[128,512]{1,0:T(8,128)(2,1)}) custom-call(s32[1]{0:T(128)} %bitcast.1.me_ref, s32[4,24]{1,0:T(4,128)S(1)} %bitcast.14, bf16[16,3072]{1,0:T(8,128)(2,1)S(1)} %pad_maximum_fusion.refs_0_, bf16[16,3072]{1,0:T(8,128)(2,1)S(1)} %collective-permute-done.8.refs_1_, ...), custom_call_target="tpu_custom_call" | custom-call | flops 805306368 | bytes 6291456 | tf_op jit(solution)/shard_map/backward/pallas_call | solution.py:209
  28.3 0.1 collective-permute-done.6
  28.3 0.6 %fusion.4 = bf16[1,4,3072]{2,1,0:T(4,128)(2,1)} fusion(bf16[4,3072]{1,0:T(4,128)(2,1)S(1)} %collective-permute-done.6, f32[8,3072]{1,0:T(8,128)S(1)} %slice_add_fusion.1, bf16[1,4,3072]{2,1,0:T(4,128)(2,1)S(1)} %copy-done.2), kind=kLoop, calls=%fused_computation.12 | loop fusion | flops 61440 | bytes 122880 | tf_op jit(solution)/shard_map/broadcast_in_dim | solution.py:222
  (16 shorter events, 0.2 us)
Async XLA Ops:
  0.6 5.8 %collective-permute-start = (bf16[4,3072]{1,0:T(4,128)(2,1)}, bf16[4,3072]{1,0:T(4,128)(2,1)S(1)}, u32[]{:S(2)}, u32[]{:S(2)}) collective-permute-start(bf16[4,3072]{1,0:T(4,128)(2,1)} %bitcast.18), channel_id=1, source_target_pairs={{0,8},{1,9},{2,10},{3,11},{4,12},{5,13},{6,14},{7,15},{8,0},{9,1},... | collective-permute-start | bytes 73736 | tf_op jit(solution)/shard_map/ppermute | solution.py:29
  3.7 3.7 %copy-start.1 = (bf16[1,4,3072]{2,1,0:T(4,128)(2,1)S(1)}, bf16[1,4,3072]{2,1,0:T(4,128)(2,1)}, u32[]{:S(2)}) copy-start(bf16[1,4,3072]{2,1,0:T(4,128)(2,1)} %param.7) | copy-start | bytes 73732
  6.4 3.6 %collective-permute-start.1 = (bf16[64,3072]{1,0:T(8,128)(2,1)S(1)}, bf16[64,3072]{1,0:T(8,128)(2,1)S(1)}, u32[]{:S(2)}, u32[]{:S(2)}) collective-permute-start(bf16[64,3072]{1,0:T(8,128)(2,1)S(1)} %get-tuple-element.19), channel_id=1, source_target_pairs={{0,1},{1,0},{2,3},{3,2},{4,5},{5,4},{6,7},{7,6},{8,9},{9,8},{10,11... | collective-permute-start | bytes 1179656 | tf_op jit(solution)/shard_map/ppermute | solution.py:29
  6.5 17.8 %copy-start = (s32[1,4,24]{2,1,0:T(4,128)S(1)}, s32[1,4,24]{2,1,0:T(4,128)}, u32[]{:S(2)}) copy-start(s32[1,4,24]{2,1,0:T(4,128)} %param.11) | copy-start | bytes 1156
  7.4 6.4 %collective-permute-start.7 = (bf16[8,3072]{1,0:T(8,128)(2,1)S(1)}, bf16[8,3072]{1,0:T(8,128)(2,1)S(1)}, u32[]{:S(2)}, u32[]{:S(2)}) collective-permute-start(bf16[8,3072]{1,0:T(8,128)(2,1)S(1)} %pad_maximum_fusion.1), channel_id=1, source_target_pairs={{0,16},{1,17},{2,18},{3,19},{4,20},{5,21},{6,22},{7,23},{8,24},{9,... | collective-permute-start | bytes 147464 | tf_op jit(solution)/shard_map/ppermute | solution.py:29
  10.2 18.1 %copy-start.2 = (bf16[1,4,3072]{2,1,0:T(4,128)(2,1)S(1)}, bf16[1,4,3072]{2,1,0:T(4,128)(2,1)}, u32[]{:S(2)}) copy-start(bf16[1,4,3072]{2,1,0:T(4,128)(2,1)} %param.6) | copy-start | bytes 73732
  10.2 6.7 %collective-permute-start.4 = (bf16[16,3072]{1,0:T(8,128)(2,1)S(1)}, bf16[16,3072]{1,0:T(8,128)(2,1)S(1)}, u32[]{:S(2)}, u32[]{:S(2)}) collective-permute-start(bf16[16,3072]{1,0:T(8,128)(2,1)S(1)} %get-tuple-element.28), channel_id=1, source_target_pairs={{0,6},{1,7},{2,4},{3,5},{4,2},{5,3},{6,0},{7,1},{8,14},{9,15},{10,... | collective-permute-start | bytes 294920 | tf_op jit(solution)/shard_map/ppermute | solution.py:29
  12.7 6.5 %collective-permute-start.3 = (bf16[16,3072]{1,0:T(8,128)(2,1)S(1)}, bf16[16,3072]{1,0:T(8,128)(2,1)S(1)}, u32[]{:S(2)}, u32[]{:S(2)}) collective-permute-start(bf16[16,3072]{1,0:T(8,128)(2,1)S(1)} %get-tuple-element.29), channel_id=1, source_target_pairs={{0,2},{1,3},{2,0},{3,1},{4,6},{5,7},{6,4},{7,5},{8,10},{9,11},{10,... | collective-permute-start | bytes 294920 | tf_op jit(solution)/shard_map/ppermute | solution.py:29
  13.3 6.0 %collective-permute-start.2 = (bf16[16,3072]{1,0:T(8,128)(2,1)S(1)}, bf16[16,3072]{1,0:T(8,128)(2,1)S(1)}, u32[]{:S(2)}, u32[]{:S(2)}) collective-permute-start(bf16[16,3072]{1,0:T(8,128)(2,1)S(1)} %get-tuple-element.27), channel_id=1, source_target_pairs={{0,4},{1,5},{2,6},{3,7},{4,0},{5,1},{6,2},{7,3},{8,12},{9,13},{10,... | collective-permute-start | bytes 294920 | tf_op jit(solution)/shard_map/ppermute | solution.py:29
  13.8 7.3 %collective-permute-start.8 = (bf16[16,3072]{1,0:T(8,128)(2,1)S(1)}, bf16[16,3072]{1,0:T(8,128)(2,1)S(1)}, u32[]{:S(2)}, u32[]{:S(2)}) collective-permute-start(bf16[16,3072]{1,0:T(8,128)(2,1)S(1)} %pad_maximum_fusion.refs_0_), channel_id=1, source_target_pairs={{0,4},{1,5},{2,6},{3,7},{4,0},{5,1},{6,2},{7,3},{8,12},{9,13},{10,... | collective-permute-start | bytes 294920 | tf_op jit(solution)/shard_map/ppermute | solution.py:29
  15.4 5.7 %collective-permute-start.9 = (bf16[16,3072]{1,0:T(8,128)(2,1)S(1)}, bf16[16,3072]{1,0:T(8,128)(2,1)S(1)}, u32[]{:S(2)}, u32[]{:S(2)}) collective-permute-start(bf16[16,3072]{1,0:T(8,128)(2,1)S(1)} %pad_maximum_fusion.refs_0_), channel_id=1, source_target_pairs={{0,2},{1,3},{2,0},{3,1},{4,6},{5,7},{6,4},{7,5},{8,10},{9,11},{10,... | collective-permute-start | bytes 294920 | tf_op jit(solution)/shard_map/ppermute | solution.py:29
  16.9 5.6 %collective-permute-start.10 = (bf16[16,3072]{1,0:T(8,128)(2,1)S(1)}, bf16[16,3072]{1,0:T(8,128)(2,1)S(1)}, u32[]{:S(2)}, u32[]{:S(2)}) collective-permute-start(bf16[16,3072]{1,0:T(8,128)(2,1)S(1)} %pad_maximum_fusion.refs_0_), channel_id=1, source_target_pairs={{0,6},{1,7},{2,4},{3,5},{4,2},{5,3},{6,0},{7,1},{8,14},{9,15},{10,... | collective-permute-start | bytes 294920 | tf_op jit(solution)/shard_map/ppermute | solution.py:29
  19.3 4.2 %collective-permute-start.5 = (bf16[8,3072]{1,0:T(8,128)(2,1)S(1)}, bf16[8,3072]{1,0:T(8,128)(2,1)S(1)}, u32[]{:S(2)}, u32[]{:S(2)}) collective-permute-start(bf16[8,3072]{1,0:T(8,128)(2,1)S(1)} %split.60), channel_id=1, source_target_pairs={{0,8},{1,9},{2,10},{3,11},{4,12},{5,13},{6,14},{7,15},{8,0},{9,1},... | collective-permute-start | bytes 147464 | tf_op jit(solution)/shard_map/ppermute | solution.py:29
  20.6 3.7 %collective-permute-start.11 = (bf16[16,3072]{1,0:T(8,128)(2,1)S(1)}, bf16[16,3072]{1,0:T(8,128)(2,1)S(1)}, u32[]{:S(2)}, u32[]{:S(2)}) collective-permute-start(bf16[16,3072]{1,0:T(8,128)(2,1)S(1)} %pad_maximum_fusion.refs_0_), channel_id=1, source_target_pairs={{0,1},{1,0},{2,3},{3,2},{4,5},{5,4},{6,7},{7,6},{8,9},{9,8},{10,11... | collective-permute-start | bytes 294920 | tf_op jit(solution)/shard_map/ppermute | solution.py:29
  21.1 3.2 %collective-permute-start.12 = (bf16[16,3072]{1,0:T(8,128)(2,1)S(1)}, bf16[16,3072]{1,0:T(8,128)(2,1)S(1)}, u32[]{:S(2)}, u32[]{:S(2)}) collective-permute-start(bf16[16,3072]{1,0:T(8,128)(2,1)S(1)} %collective-permute-done.8.refs_1_), channel_id=1, source_target_pairs={{0,1},{1,0},{2,3},{3,2},{4,5},{5,4},{6,7},{7,6},{8,9},{9,8},{10,11... | collective-permute-start | bytes 294920 | tf_op jit(solution)/shard_map/ppermute | solution.py:29
  21.2 3.2 %collective-permute-start.13 = (bf16[16,3072]{1,0:T(8,128)(2,1)S(1)}, bf16[16,3072]{1,0:T(8,128)(2,1)S(1)}, u32[]{:S(2)}, u32[]{:S(2)}) collective-permute-start(bf16[16,3072]{1,0:T(8,128)(2,1)S(1)} %collective-permute-done.9.refs_2_), channel_id=1, source_target_pairs={{0,1},{1,0},{2,3},{3,2},{4,5},{5,4},{6,7},{7,6},{8,9},{9,8},{10,11... | collective-permute-start | bytes 294920 | tf_op jit(solution)/shard_map/ppermute | solution.py:29
  22.5 1.9 %collective-permute-start.14 = (bf16[16,3072]{1,0:T(8,128)(2,1)S(1)}, bf16[16,3072]{1,0:T(8,128)(2,1)S(1)}, u32[]{:S(2)}, u32[]{:S(2)}) collective-permute-start(bf16[16,3072]{1,0:T(8,128)(2,1)S(1)} %collective-permute-done.10.refs_3_), channel_id=1, source_target_pairs={{0,1},{1,0},{2,3},{3,2},{4,5},{5,4},{6,7},{7,6},{8,9},{9,8},{10,11... | collective-permute-start | bytes 294920 | tf_op jit(solution)/shard_map/ppermute | solution.py:29
  23.5 4.8 %collective-permute-start.6 = (bf16[4,3072]{1,0:T(4,128)(2,1)S(1)}, bf16[4,3072]{1,0:T(4,128)(2,1)S(1)}, u32[]{:S(2)}, u32[]{:S(2)}) collective-permute-start(bf16[4,3072]{1,0:T(4,128)(2,1)S(1)} %split.61), channel_id=1, source_target_pairs={{0,16},{1,17},{2,18},{3,19},{4,20},{5,21},{6,22},{7,23},{8,24},{9,... | collective-permute-start | bytes 73736 | tf_op jit(solution)/shard_map/ppermute | solution.py:29

commit v3 on v2

v3 whole, which is shorter than its diff:
```python
import functools
import math

import jax
import jax.numpy as jnp
from jax import lax
from jax.experimental import pallas as pl
from jax.experimental.pallas import tpu as pltpu
from jax.sharding import PartitionSpec as P

BLOCK = 128
SCALE = math.sqrt(2.0 / math.pi)
CUBIC = 0.044715
CHUNK = 512
WIDE = 1024
LIMIT = 16 * 1024 * 1024
FORWARD_BYTES = 6_000_000
PREPARE_BYTES = 1_500_000
bf16 = jnp.bfloat16
f32 = jnp.float32


def shifted(block, axis, distance):
    devices = range(lax.axis_size(axis))
    route = [(i - distance, i) for i in devices if i - distance in devices]
    return lax.ppermute(block, axis, route)


def exchange(block, bit):
    return lax.ppermute(block, "blk", [(i, i ^ bit) for i in range(lax.axis_size("blk"))])


def combinations(bits):
    found = [0]
    for bit in bits[::-1]:
        found += [bit ^ other for other in found]
    return found


def own_token(place, me, order, each):
    group, within = place // each, place % each
    owner = me
    for k, bit in enumerate(order):
        owner = owner ^ jnp.where((group >> (len(order) - 1 - k)) & 1 == 1, bit, 0)
    return owner * each + within


def reorder(me, tokens, order, back=False):
    rows = lax.broadcasted_iota(jnp.int32, (tokens, tokens), 1 if back else 0)
    cols = lax.broadcasted_iota(jnp.int32, (tokens, tokens), 0 if back else 1)
    return (own_token(rows, me, order, tokens >> len(order)) == cols).astype(bf16)


def columns(width, chunk):
    chunk = chunk if width % chunk == 0 else BLOCK
    return [pl.ds(first, chunk) for first in range(0, width, chunk)]


def keep_blocks(array, mask_ref, i, first):
    blocks = []
    for j in range(array.shape[1] // BLOCK):
        block = array[:, j * BLOCK : (j + 1) * BLOCK]
        blocks.append(jnp.where(mask_ref[i, first + j] != 0, block, jnp.zeros_like(block)))
    return jnp.concatenate(blocks, axis=1)


def gelu_and_slope(x):
    square = x * x
    t = jnp.tanh(SCALE * (x + CUBIC * x * square))
    half = 0.5 * (1.0 + t)
    slope = half + 0.5 * x * (1.0 - t * t) * (SCALE * (1.0 + 3.0 * CUBIC * square))
    return x * half, slope


def forward_kernel(order, me_ref, mask_hbm, now_hbm, back_hbm, w_hbm, *refs):
    total_ref, send_ref, masked_ref, kept_ref, back_ref, mask_ref, now_ref, w_ref, sems = refs
    parts = columns(w_ref.shape[1], WIDE)
    pairs = [(now_hbm, now_ref), (mask_hbm, mask_ref)]
    pairs += [(w_hbm.at[:, part], w_ref.at[:, part]) for part in parts]
    pairs += [(back_hbm, back_ref)]
    copies = [pltpu.make_async_copy(source, target, sems.at[k]) for k, (source, target) in enumerate(pairs)]
    for copy in copies:
        copy.start()
    tokens = now_ref.shape[0]
    half = send_ref.shape[0]
    moves = reorder(me_ref[0], tokens, order)
    copies[0].wait()
    hidden = gelu_and_slope(jnp.dot(moves, now_ref[...], preferred_element_type=f32))[0].astype(bf16)
    copies[1].wait()
    for i in range(w_ref.shape[0] // BLOCK):
        for j in range(w_ref.shape[1] // BLOCK):
            kept_ref[i : i + 1, j * BLOCK : (j + 1) * BLOCK] = jnp.where(mask_ref[i, j] != 0, jnp.ones((1, BLOCK), f32), 0.0)
    for c, part in enumerate(parts):
        copies[2 + c].wait()
        for i in range(w_ref.shape[0] // BLOCK):
            rows = pl.ds(i * BLOCK, BLOCK)
            masked_ref[rows, part] = keep_blocks(w_ref[rows, part], mask_ref, i, part.start // BLOCK)
        product = jnp.dot(hidden, masked_ref[:, part], preferred_element_type=f32)
        total_ref[:, part] = product[:half]
        send_ref[:, part] = product[half:].astype(bf16)
    copies[-1].wait()


def prepare_kernel(order, me_ref, back_ref, hidden_ref, slope_ref):
    moves = reorder(me_ref[0], back_ref.shape[0], order, back=True)
    hidden, slope = gelu_and_slope(jnp.dot(back_ref[...].T, moves, preferred_element_type=f32))
    hidden_ref[...] = hidden.astype(bf16)
    slope_ref[...] = slope


def backward_kernel(order, pieces, me_ref, *refs):
    grads = refs[:pieces]
    kept_ref, w_ref, hidden_ref, slope_ref, wg_hbm, pg_hbm, grad_ref, wg_ref, pg_ref, sems = refs[pieces:]
    tokens = pg_ref.shape[0]
    parts = columns(w_ref.shape[1], CHUNK)
    results = []
    for c, part in enumerate(parts):
        for k, piece in enumerate(grads):
            rows = piece.shape[0]
            grad_ref[k * rows : (k + 1) * rows, part] = piece[:, part]
        full = jnp.dot(hidden_ref[...], grad_ref[:, part], preferred_element_type=f32)
        for i in range(w_ref.shape[0] // BLOCK):
            band = full[i * BLOCK : (i + 1) * BLOCK] * kept_ref[i : i + 1, part]
            wg_ref[pl.ds(i * BLOCK, BLOCK), part] = band.astype(bf16)
        results.append(pltpu.make_async_copy(wg_ref.at[:, part], wg_hbm.at[:, part], sems.at[c]))
        results[-1].start()
    total = lax.dot_general(w_ref[...], grad_ref[...], (((1,), (1,)), ((), ())), preferred_element_type=f32)
    moved = (total * slope_ref[...]).astype(bf16)
    back = reorder(me_ref[0], tokens, order, back=True)
    pg_ref[...] = lax.dot_general(back, moved, (((1,), (1,)), ((), ())), preferred_element_type=f32).astype(bf16)
    results.append(pltpu.make_async_copy(pg_ref, pg_hbm, sems.at[len(parts)]))
    results[-1].start()
    for result in results:
        result.wait()


SMEM = functools.partial(pl.BlockSpec, memory_space=pltpu.SMEM)
VMEM = functools.partial(pl.BlockSpec, memory_space=pltpu.VMEM)
HBM = functools.partial(pl.BlockSpec, memory_space=pltpu.HBM)


def body(stream_sent, grad_sent, preact_now, preact_back, down_weight, block_mask):
    sections = lax.axis_size("section")
    stream, grad = stream_sent, grad_sent
    if sections > 1:
        section_index = lax.axis_index("section")
        stream = jnp.where(section_index == 0, stream, shifted(stream, "section", 1))
        grad = jnp.where(section_index == sections - 1, grad, shifted(grad, "section", -1))
    stream, grad, mask, weight = stream[0], grad[0], block_mask[0], down_weight[0]
    pre_now, pre_back = preact_now[0], preact_back[0]
    held = [pltpu.with_memory_space_constraint(x, pltpu.HBM) for x in (mask, pre_now, pre_back, weight)]
    tokens, hidden = preact_now.shape[1:]
    width = down_weight.shape[2]
    devices = lax.axis_size("blk")
    bits = [1 << k for k in range(devices.bit_length() - 1)]
    near, plane, far = bits[:1], bits[1:3], bits[3:]
    scatter_order = near + plane + far
    gather_order = near + plane + far[::-1]
    me = lax.axis_index("blk").astype(jnp.int32).reshape(1)
    half = tokens // 2

    def shape(dtype, *dims):
        return jax.ShapeDtypeStruct(dims, dtype)

    params = pltpu.CompilerParams(vmem_limit_bytes=LIMIT)
    total, send, masked, kept, held_back = pl.pallas_call(
        functools.partial(forward_kernel, scatter_order),
        out_shape=(
            shape(f32, half, width),
            shape(bf16, half, width),
            shape(bf16, hidden, width),
            shape(f32, hidden // BLOCK, width),
            shape(bf16, tokens, hidden),
        ),
        in_specs=[SMEM()] + [HBM()] * 4,
        out_specs=(VMEM(),) * 5,
        scratch_shapes=[
            pltpu.SMEM(mask.shape, jnp.int32),
            pltpu.VMEM((tokens, hidden), bf16),
            pltpu.VMEM((hidden, width), bf16),
            pltpu.SemaphoreType.DMA((3 + len(columns(width, WIDE)),)),
        ],
        compiler_params=params,
        cost_estimate=pl.CostEstimate(flops=2 * tokens * hidden * width, bytes_accessed=FORWARD_BYTES, transcendentals=0),
        name="forward",
    )(me, *held)

    hidden_back, slope = pl.pallas_call(
        functools.partial(prepare_kernel, gather_order),
        out_shape=(shape(bf16, hidden, tokens), shape(f32, hidden, tokens)),
        in_specs=[SMEM(), VMEM()],
        out_specs=(VMEM(),) * 2,
        compiler_params=params,
        cost_estimate=pl.CostEstimate(flops=2 * tokens * tokens * hidden, bytes_accessed=PREPARE_BYTES, transcendentals=0),
        name="prepare",
    )(me, held_back)

    mine = grad
    for k, bit in enumerate(far):
        other = exchange(mine, bit)
        if k == 0:
            send, other = lax.optimization_barrier((send, other))
        mine = jnp.concatenate([mine, other], axis=0)

    total = total + exchange(send, near[0]).astype(f32)
    parts = jnp.split(total, 1 << len(plane), axis=0)
    total = parts[0]
    for part, bit in zip(parts[1:], combinations(plane)[1:]):
        total = total + exchange(part.astype(bf16), bit).astype(f32)
    for bit in far:
        part = total[total.shape[0] // 2 :].astype(bf16)
        total = total[: total.shape[0] // 2]
        if bit == far[-1]:
            total = total + stream.astype(f32)
        total = total + exchange(part, bit).astype(f32)
    stream_out = total.astype(bf16)

    grads = [mine] + [exchange(mine, bit) for bit in combinations(plane)[1:]]
    grads += [exchange(piece, near[0]) for piece in grads]

    weight_grad, preact_grad = pl.pallas_call(
        functools.partial(backward_kernel, gather_order, len(grads)),
        out_shape=(shape(bf16, hidden, width), shape(bf16, tokens, hidden)),
        in_specs=[SMEM()] + [VMEM()] * (len(grads) + 4),
        out_specs=(HBM(), HBM()),
        scratch_shapes=[
            pltpu.VMEM((tokens, width), bf16),
            pltpu.VMEM((hidden, width), bf16),
            pltpu.VMEM((tokens, hidden), bf16),
            pltpu.SemaphoreType.DMA((1 + len(columns(width, CHUNK)),)),
        ],
        compiler_params=params,
        cost_estimate=pl.CostEstimate(flops=4 * tokens * hidden * width, bytes_accessed=4 * hidden * width, transcendentals=0),
        name="backward",
    )(me, *grads, kept, masked, hidden_back, slope)
    return stream_out[None], preact_grad[None], weight_grad[None]


def solution(mesh):
    placed = (
        P("section", "blk", None),
        P("section", "blk", None),
        P("section", None, "blk"),
        P("section", None, "blk"),
        P("section", "blk", None),
        P("section", "blk", None),
    )
    return jax.shard_map(
        body,
        mesh=mesh,
        in_specs=placed,
        out_specs=(P("section", "blk", None), P("section", None, "blk"), P("section", "blk", None)),
        check_vma=False,
    )
```

time: 29.1 us -> 28.1 us (0.966)
  Pallas kernels: 7.43 us -> 5.55 us
  starting transfers between devices: 17.4 us -> 18.6 us
  waiting for transfers between devices: 2.44 us -> 2.06 us
    ppermute x15, starting transfers between devices: 17.4 us -> 18.6 us  [exchange(): lax.ppermute(block, 'blk', [(i, i ^ bit) for i in range(lax.axis_size('bl...]
    pallas_call x1, Pallas kernels: 3.88 us -> 2.73 us  [body(): pl.pallas_call(functools.partial(backward_kernel, gather_order, len(grads...]
    pallas_call x2, Pallas kernels: 3.54 us -> 2.82 us  [the longest x1 2.49 us: body(): pl.pallas_call(functools.partial(forward_kernel, scatter_order), out_shap...]
    ppermute x15, waiting for transfers between devices: 2.44 us -> 2.06 us  [exchange(): lax.ppermute(block, 'blk', [(i, i ^ bit) for i in range(lax.axis_size('bl...]
  transfers between devices with their start and end apart: 15 -> 15, of which waited for: 4 -> 3; matrix products, arithmetic and copies ran while one was open for 1% -> 1% of each run, Pallas kernels for 16% -> 20%
where the time goes in v3:
time: 28.1 us; the launch traced here: 27.9 us
  starting transfers between devices  18.6 us (66%)
  Pallas kernels  5.55 us (20%)
  waiting for transfers between devices  2.06 us (7%)
  other arithmetic  0.86 us (3%)
  between operations  0.79 us (3%)
    ppermute x15, starting transfers between devices, exchange(): lax.ppermute(block, 'blk', [(i, i ^ bit) for i in range(lax.axis_size('bl...  18.6 us
    pallas_call x1, Pallas kernels, body(): pl.pallas_call(functools.partial(backward_kernel, gather_order, len(grads...  2.73 us
    pallas_call x1, Pallas kernels, body(): pl.pallas_call(functools.partial(forward_kernel, scatter_order), out_shap...  2.49 us
    ppermute x15, waiting for transfers between devices, exchange(): lax.ppermute(block, 'blk', [(i, i ^ bit) for i in range(lax.axis_size('bl...  2.06 us
    broadcast_in_dim x1, other arithmetic, body(): return (stream_out[None], preact_grad[None], weight_grad[None])  0.63 us
  transfers between devices with their start and end apart: 15, of which 3 were waited for; matrix products, arithmetic and copies ran while one was open for 1% of the time, Pallas kernels for 20%

profile of v3, /device:TPU:0, one launch (start us, length us, event | category | flops | bytes accessed | tf_op | source)
XLA Modules:
  0.0 27.9 jit_solution(5356821335442547612)
XLA Ops:
  0.6 3.1 %collective-permute-start = (bf16[4,3072]{1,0:T(4,128)(2,1)}, bf16[4,3072]{1,0:T(4,128)(2,1)S(1)}, u32[]{:S(2)}, u32[]{:S(2)}) collective-permute-start(bf16[4,3072]{1,0:T(4,128)(2,1)} %bitcast.16), channel_id=1, source_target_pairs={{0,8},{1,9},{2,10},{3,11},{4,12},{5,13},{6,14},{7,15},{8,0},{9,1},... | collective-permute-start | bytes 73736 | tf_op jit(solution)/shard_map/ppermute | solution.py:30
  3.7 2.5 %forward.1 = (f32[64,3072]{1,0:T(8,128)S(1)}, bf16[64,3072]{1,0:T(8,128)(2,1)S(1)}, bf16[512,3072]{1,0:T(8,128)(2,1)S(1)}, f32[4,3072]{1,0:T(4,128)S(1)}, bf16[128,512]{1,0:T(8,128)(2,1)S(1)}) custom-call(s32[1]{0:T(128)} %bitcast.me_ref, s32[4,24]{1,0:T(4,128)} %bitcast.19, bf16[128,512]{1,0:T(8,128)(2,1)} %bitcast.14, bf16[128,512]{1,0:T(8,128)(2,1)} %bitcast.15, ...), custom_call_target="tpu_custom_call" | custom-call | flops 402653184 | bytes 6000000 | tf_op jit(solution)/shard_map/forward/pallas_call | solution.py:166
  6.2 0.0 collective-permute-done
  6.2 0.1 collective-permute-start.1
  6.4 2.7 %collective-permute-start.7 = (bf16[8,3072]{1,0:T(8,128)(2,1)S(1)}, bf16[8,3072]{1,0:T(8,128)(2,1)S(1)}, u32[]{:S(2)}, u32[]{:S(2)}) collective-permute-start(bf16[8,3072]{1,0:T(8,128)(2,1)S(1)} %pad_maximum_fusion.1), channel_id=1, source_target_pairs={{0,16},{1,17},{2,18},{3,19},{4,20},{5,21},{6,22},{7,23},{8,24},{9,... | collective-permute-start | bytes 147464 | tf_op jit(solution)/shard_map/ppermute | solution.py:30
  9.0 0.0 collective-permute-done.1
  9.0 0.1 fusion.5
  9.1 0.0 copy-start.1
  9.2 2.5 %collective-permute-start.4 = (bf16[16,3072]{1,0:T(8,128)(2,1)S(1)}, bf16[16,3072]{1,0:T(8,128)(2,1)S(1)}, u32[]{:S(2)}, u32[]{:S(2)}) collective-permute-start(bf16[16,3072]{1,0:T(8,128)(2,1)S(1)} %get-tuple-element.28), channel_id=1, source_target_pairs={{0,6},{1,7},{2,4},{3,5},{4,2},{5,3},{6,0},{7,1},{8,14},{9,15},{10,... | collective-permute-start | bytes 294920 | tf_op jit(solution)/shard_map/ppermute | solution.py:30
  11.7 0.5 %collective-permute-start.3 = (bf16[16,3072]{1,0:T(8,128)(2,1)S(1)}, bf16[16,3072]{1,0:T(8,128)(2,1)S(1)}, u32[]{:S(2)}, u32[]{:S(2)}) collective-permute-start(bf16[16,3072]{1,0:T(8,128)(2,1)S(1)} %get-tuple-element.29), channel_id=1, source_target_pairs={{0,2},{1,3},{2,0},{3,1},{4,6},{5,7},{6,4},{7,5},{8,10},{9,11},{10,... | collective-permute-start | bytes 294920 | tf_op jit(solution)/shard_map/ppermute | solution.py:30
  12.2 0.5 %collective-permute-start.2 = (bf16[16,3072]{1,0:T(8,128)(2,1)S(1)}, bf16[16,3072]{1,0:T(8,128)(2,1)S(1)}, u32[]{:S(2)}, u32[]{:S(2)}) collective-permute-start(bf16[16,3072]{1,0:T(8,128)(2,1)S(1)} %get-tuple-element.27), channel_id=1, source_target_pairs={{0,4},{1,5},{2,6},{3,7},{4,0},{5,1},{6,2},{7,3},{8,12},{9,13},{10,... | collective-permute-start | bytes 294920 | tf_op jit(solution)/shard_map/ppermute | solution.py:30
  12.7 0.0 collective-permute-done.7
  12.8 1.6 %collective-permute-start.8 = (bf16[16,3072]{1,0:T(8,128)(2,1)S(1)}, bf16[16,3072]{1,0:T(8,128)(2,1)S(1)}, u32[]{:S(2)}, u32[]{:S(2)}) collective-permute-start(bf16[16,3072]{1,0:T(8,128)(2,1)S(1)} %pad_maximum_fusion.refs_0_), channel_id=1, source_target_pairs={{0,4},{1,5},{2,6},{3,7},{4,0},{5,1},{6,2},{7,3},{8,12},{9,13},{10,... | collective-permute-start | bytes 294920 | tf_op jit(solution)/shard_map/ppermute | solution.py:30
  14.4 1.5 %collective-permute-start.9 = (bf16[16,3072]{1,0:T(8,128)(2,1)S(1)}, bf16[16,3072]{1,0:T(8,128)(2,1)S(1)}, u32[]{:S(2)}, u32[]{:S(2)}) collective-permute-start(bf16[16,3072]{1,0:T(8,128)(2,1)S(1)} %pad_maximum_fusion.refs_0_), channel_id=1, source_target_pairs={{0,2},{1,3},{2,0},{3,1},{4,6},{5,7},{6,4},{7,5},{8,10},{9,11},{10,... | collective-permute-start | bytes 294920 | tf_op jit(solution)/shard_map/ppermute | solution.py:30
  15.9 0.0 collective-permute-done.4
  15.9 2.4 %collective-permute-start.10 = (bf16[16,3072]{1,0:T(8,128)(2,1)S(1)}, bf16[16,3072]{1,0:T(8,128)(2,1)S(1)}, u32[]{:S(2)}, u32[]{:S(2)}) collective-permute-start(bf16[16,3072]{1,0:T(8,128)(2,1)S(1)} %pad_maximum_fusion.refs_0_), channel_id=1, source_target_pairs={{0,6},{1,7},{2,4},{3,5},{4,2},{5,3},{6,0},{7,1},{8,14},{9,15},{10,... | collective-permute-start | bytes 294920 | tf_op jit(solution)/shard_map/ppermute | solution.py:30
  18.2 0.0 collective-permute-done.3
  18.2 0.0 collective-permute-done.2
  18.3 1.5 %collective-permute-start.5 = (bf16[8,3072]{1,0:T(8,128)(2,1)S(1)}, bf16[8,3072]{1,0:T(8,128)(2,1)S(1)}, u32[]{:S(2)}, u32[]{:S(2)}) collective-permute-start(bf16[8,3072]{1,0:T(8,128)(2,1)S(1)} %slice.32), channel_id=1, source_target_pairs={{0,8},{1,9},{2,10},{3,11},{4,12},{5,13},{6,14},{7,15},{8,0},{9,1},... | collective-permute-start | bytes 147464 | tf_op jit(solution)/shard_map/ppermute | solution.py:30
  19.8 0.3 %prepare.1 = (bf16[512,128]{1,0:T(8,128)(2,1)S(1)}, f32[512,128]{1,0:T(8,128)S(1)}) custom-call(s32[1]{0:T(128)} %bitcast.me_ref, bf16[128,512]{1,0:T(8,128)(2,1)S(1)} %get-tuple-element.20.back_ref), custom_call_target="tpu_custom_call" | custom-call | flops 16777216 | bytes 1500000 | tf_op jit(solution)/shard_map/prepare/pallas_call | solution.py:188
  20.1 0.1 collective-permute-start.11
  20.2 0.0 collective-permute-done.8.refs_1_
  20.2 0.5 %collective-permute-start.12 = (bf16[16,3072]{1,0:T(8,128)(2,1)S(1)}, bf16[16,3072]{1,0:T(8,128)(2,1)S(1)}, u32[]{:S(2)}, u32[]{:S(2)}) collective-permute-start(bf16[16,3072]{1,0:T(8,128)(2,1)S(1)} %collective-permute-done.8.refs_1_), channel_id=1, source_target_pairs={{0,1},{1,0},{2,3},{3,2},{4,5},{5,4},{6,7},{7,6},{8,9},{9,8},{10,11... | collective-permute-start | bytes 294920 | tf_op jit(solution)/shard_map/ppermute | solution.py:30
  20.7 0.1 collective-permute-start.13
  20.8 0.6 %collective-permute-done.10.refs_3_ = bf16[16,3072]{1,0:T(8,128)(2,1)S(1)} collective-permute-done((bf16[16,3072]{1,0:T(8,128)(2,1)S(1)}, bf16[16,3072]{1,0:T(8,128)(2,1)S(1)}, u32[]{:S(2)}, u32[]{:S(2)}) %collective-permute-start.10) | collective-permute-done | bytes 98336 | tf_op jit(solution)/shard_map/ppermute | solution.py:30
  21.4 0.0 collective-permute-start.14
  21.5 1.0 %collective-permute-done.5 = bf16[8,3072]{1,0:T(8,128)(2,1)S(1)} collective-permute-done((bf16[8,3072]{1,0:T(8,128)(2,1)S(1)}, bf16[8,3072]{1,0:T(8,128)(2,1)S(1)}, u32[]{:S(2)}, u32[]{:S(2)}) %collective-permute-start.5) | collective-permute-done | bytes 49184 | tf_op jit(solution)/shard_map/ppermute | solution.py:30
  22.5 1.7 %collective-permute-start.6 = (bf16[4,3072]{1,0:T(4,128)(2,1)S(1)}, bf16[4,3072]{1,0:T(4,128)(2,1)S(1)}, u32[]{:S(2)}, u32[]{:S(2)}) collective-permute-start(bf16[4,3072]{1,0:T(4,128)(2,1)S(1)} %slice.33), channel_id=1, source_target_pairs={{0,16},{1,17},{2,18},{3,19},{4,20},{5,21},{6,22},{7,23},{8,24},{9,... | collective-permute-start | bytes 73736 | tf_op jit(solution)/shard_map/ppermute | solution.py:30
  24.2 0.0 collective-permute-done.13.refs_6_
  24.2 2.7 %backward.1 = (bf16[512,3072]{1,0:T(8,128)(2,1)}, bf16[128,512]{1,0:T(8,128)(2,1)}) custom-call(s32[1]{0:T(128)} %bitcast.me_ref, bf16[16,3072]{1,0:T(8,128)(2,1)S(1)} %pad_maximum_fusion.refs_0_, bf16[16,3072]{1,0:T(8,128)(2,1)S(1)} %collective-permute-done.8.refs_1_, bf16[16,3072]{1,0:T(8,128)(2,1)S(1)} %collective-permute-done.9.refs_2_, ...), custom_call_target="tpu_custom_call" | custom-call | flops 805306368 | bytes 6291456 | tf_op jit(solution)/shard_map/backward/pallas_call | solution.py:221
  26.9 0.4 %collective-permute-done.6 = bf16[4,3072]{1,0:T(4,128)(2,1)S(1)} collective-permute-done((bf16[4,3072]{1,0:T(4,128)(2,1)S(1)}, bf16[4,3072]{1,0:T(4,128)(2,1)S(1)}, u32[]{:S(2)}, u32[]{:S(2)}) %collective-permute-start.6) | collective-permute-done | bytes 24608 | tf_op jit(solution)/shard_map/ppermute | solution.py:30
  27.3 0.6 %fusion.4 = bf16[1,4,3072]{2,1,0:T(4,128)(2,1)} fusion(bf16[4,3072]{1,0:T(4,128)(2,1)S(1)} %collective-permute-done.6, f32[8,3072]{1,0:T(8,128)S(1)} %slice_add_fusion.1, bf16[1,4,3072]{2,1,0:T(4,128)(2,1)S(1)} %copy-done.1), kind=kLoop, calls=%fused_computation.12 | loop fusion | flops 61440 | bytes 122880 | tf_op jit(solution)/shard_map/broadcast_in_dim | solution.py:236
  (14 shorter events, 0.2 us)
Async XLA Ops:
  0.6 5.7 %copy-start = (bf16[1,4,3072]{2,1,0:T(4,128)(2,1)S(1)}, bf16[1,4,3072]{2,1,0:T(4,128)(2,1)}, u32[]{:S(2)}) copy-start(bf16[1,4,3072]{2,1,0:T(4,128)(2,1)} %param.7) | copy-start | bytes 73732
  0.6 5.6 %collective-permute-start = (bf16[4,3072]{1,0:T(4,128)(2,1)}, bf16[4,3072]{1,0:T(4,128)(2,1)S(1)}, u32[]{:S(2)}, u32[]{:S(2)}) collective-permute-start(bf16[4,3072]{1,0:T(4,128)(2,1)} %bitcast.16), channel_id=1, source_target_pairs={{0,8},{1,9},{2,10},{3,11},{4,12},{5,13},{6,14},{7,15},{8,0},{9,1},... | collective-permute-start | bytes 73736 | tf_op jit(solution)/shard_map/ppermute | solution.py:30
  6.2 2.8 %collective-permute-start.1 = (bf16[64,3072]{1,0:T(8,128)(2,1)S(1)}, bf16[64,3072]{1,0:T(8,128)(2,1)S(1)}, u32[]{:S(2)}, u32[]{:S(2)}) collective-permute-start(bf16[64,3072]{1,0:T(8,128)(2,1)S(1)} %get-tuple-element.16), channel_id=1, source_target_pairs={{0,1},{1,0},{2,3},{3,2},{4,5},{5,4},{6,7},{7,6},{8,9},{9,8},{10,11... | collective-permute-start | bytes 1179656 | tf_op jit(solution)/shard_map/ppermute | solution.py:30
  6.4 6.4 %collective-permute-start.7 = (bf16[8,3072]{1,0:T(8,128)(2,1)S(1)}, bf16[8,3072]{1,0:T(8,128)(2,1)S(1)}, u32[]{:S(2)}, u32[]{:S(2)}) collective-permute-start(bf16[8,3072]{1,0:T(8,128)(2,1)S(1)} %pad_maximum_fusion.1), channel_id=1, source_target_pairs={{0,16},{1,17},{2,18},{3,19},{4,20},{5,21},{6,22},{7,23},{8,24},{9,... | collective-permute-start | bytes 147464 | tf_op jit(solution)/shard_map/ppermute | solution.py:30
  9.1 18.2 %copy-start.1 = (bf16[1,4,3072]{2,1,0:T(4,128)(2,1)S(1)}, bf16[1,4,3072]{2,1,0:T(4,128)(2,1)}, u32[]{:S(2)}) copy-start(bf16[1,4,3072]{2,1,0:T(4,128)(2,1)} %param.6) | copy-start | bytes 73732
  9.2 6.7 %collective-permute-start.4 = (bf16[16,3072]{1,0:T(8,128)(2,1)S(1)}, bf16[16,3072]{1,0:T(8,128)(2,1)S(1)}, u32[]{:S(2)}, u32[]{:S(2)}) collective-permute-start(bf16[16,3072]{1,0:T(8,128)(2,1)S(1)} %get-tuple-element.28), channel_id=1, source_target_pairs={{0,6},{1,7},{2,4},{3,5},{4,2},{5,3},{6,0},{7,1},{8,14},{9,15},{10,... | collective-permute-start | bytes 294920 | tf_op jit(solution)/shard_map/ppermute | solution.py:30
  11.7 6.5 %collective-permute-start.3 = (bf16[16,3072]{1,0:T(8,128)(2,1)S(1)}, bf16[16,3072]{1,0:T(8,128)(2,1)S(1)}, u32[]{:S(2)}, u32[]{:S(2)}) collective-permute-start(bf16[16,3072]{1,0:T(8,128)(2,1)S(1)} %get-tuple-element.29), channel_id=1, source_target_pairs={{0,2},{1,3},{2,0},{3,1},{4,6},{5,7},{6,4},{7,5},{8,10},{9,11},{10,... | collective-permute-start | bytes 294920 | tf_op jit(solution)/shard_map/ppermute | solution.py:30
  12.2 6.0 %collective-permute-start.2 = (bf16[16,3072]{1,0:T(8,128)(2,1)S(1)}, bf16[16,3072]{1,0:T(8,128)(2,1)S(1)}, u32[]{:S(2)}, u32[]{:S(2)}) collective-permute-start(bf16[16,3072]{1,0:T(8,128)(2,1)S(1)} %get-tuple-element.27), channel_id=1, source_target_pairs={{0,4},{1,5},{2,6},{3,7},{4,0},{5,1},{6,2},{7,3},{8,12},{9,13},{10,... | collective-permute-start | bytes 294920 | tf_op jit(solution)/shard_map/ppermute | solution.py:30
  12.8 7.4 %collective-permute-start.8 = (bf16[16,3072]{1,0:T(8,128)(2,1)S(1)}, bf16[16,3072]{1,0:T(8,128)(2,1)S(1)}, u32[]{:S(2)}, u32[]{:S(2)}) collective-permute-start(bf16[16,3072]{1,0:T(8,128)(2,1)S(1)} %pad_maximum_fusion.refs_0_), channel_id=1, source_target_pairs={{0,4},{1,5},{2,6},{3,7},{4,0},{5,1},{6,2},{7,3},{8,12},{9,13},{10,... | collective-permute-start | bytes 294920 | tf_op jit(solution)/shard_map/ppermute | solution.py:30
  14.4 6.3 %collective-permute-start.9 = (bf16[16,3072]{1,0:T(8,128)(2,1)S(1)}, bf16[16,3072]{1,0:T(8,128)(2,1)S(1)}, u32[]{:S(2)}, u32[]{:S(2)}) collective-permute-start(bf16[16,3072]{1,0:T(8,128)(2,1)S(1)} %pad_maximum_fusion.refs_0_), channel_id=1, source_target_pairs={{0,2},{1,3},{2,0},{3,1},{4,6},{5,7},{6,4},{7,5},{8,10},{9,11},{10,... | collective-permute-start | bytes 294920 | tf_op jit(solution)/shard_map/ppermute | solution.py:30
  15.9 5.6 %collective-permute-start.10 = (bf16[16,3072]{1,0:T(8,128)(2,1)S(1)}, bf16[16,3072]{1,0:T(8,128)(2,1)S(1)}, u32[]{:S(2)}, u32[]{:S(2)}) collective-permute-start(bf16[16,3072]{1,0:T(8,128)(2,1)S(1)} %pad_maximum_fusion.refs_0_), channel_id=1, source_target_pairs={{0,6},{1,7},{2,4},{3,5},{4,2},{5,3},{6,0},{7,1},{8,14},{9,15},{10,... | collective-permute-start | bytes 294920 | tf_op jit(solution)/shard_map/ppermute | solution.py:30
  18.3 4.2 %collective-permute-start.5 = (bf16[8,3072]{1,0:T(8,128)(2,1)S(1)}, bf16[8,3072]{1,0:T(8,128)(2,1)S(1)}, u32[]{:S(2)}, u32[]{:S(2)}) collective-permute-start(bf16[8,3072]{1,0:T(8,128)(2,1)S(1)} %slice.32), channel_id=1, source_target_pairs={{0,8},{1,9},{2,10},{3,11},{4,12},{5,13},{6,14},{7,15},{8,0},{9,1},... | collective-permute-start | bytes 147464 | tf_op jit(solution)/shard_map/ppermute | solution.py:30
  20.1 4.0 %collective-permute-start.11 = (bf16[16,3072]{1,0:T(8,128)(2,1)S(1)}, bf16[16,3072]{1,0:T(8,128)(2,1)S(1)}, u32[]{:S(2)}, u32[]{:S(2)}) collective-permute-start(bf16[16,3072]{1,0:T(8,128)(2,1)S(1)} %pad_maximum_fusion.refs_0_), channel_id=1, source_target_pairs={{0,1},{1,0},{2,3},{3,2},{4,5},{5,4},{6,7},{7,6},{8,9},{9,8},{10,11... | collective-permute-start | bytes 294920 | tf_op jit(solution)/shard_map/ppermute | solution.py:30
  20.2 3.9 %collective-permute-start.12 = (bf16[16,3072]{1,0:T(8,128)(2,1)S(1)}, bf16[16,3072]{1,0:T(8,128)(2,1)S(1)}, u32[]{:S(2)}, u32[]{:S(2)}) collective-permute-start(bf16[16,3072]{1,0:T(8,128)(2,1)S(1)} %collective-permute-done.8.refs_1_), channel_id=1, source_target_pairs={{0,1},{1,0},{2,3},{3,2},{4,5},{5,4},{6,7},{7,6},{8,9},{9,8},{10,11... | collective-permute-start | bytes 294920 | tf_op jit(solution)/shard_map/ppermute | solution.py:30
  20.7 3.4 %collective-permute-start.13 = (bf16[16,3072]{1,0:T(8,128)(2,1)S(1)}, bf16[16,3072]{1,0:T(8,128)(2,1)S(1)}, u32[]{:S(2)}, u32[]{:S(2)}) collective-permute-start(bf16[16,3072]{1,0:T(8,128)(2,1)S(1)} %collective-permute-done.9.refs_2_), channel_id=1, source_target_pairs={{0,1},{1,0},{2,3},{3,2},{4,5},{5,4},{6,7},{7,6},{8,9},{9,8},{10,11... | collective-permute-start | bytes 294920 | tf_op jit(solution)/shard_map/ppermute | solution.py:30
  21.4 2.7 %collective-permute-start.14 = (bf16[16,3072]{1,0:T(8,128)(2,1)S(1)}, bf16[16,3072]{1,0:T(8,128)(2,1)S(1)}, u32[]{:S(2)}, u32[]{:S(2)}) collective-permute-start(bf16[16,3072]{1,0:T(8,128)(2,1)S(1)} %collective-permute-done.10.refs_3_), channel_id=1, source_target_pairs={{0,1},{1,0},{2,3},{3,2},{4,5},{5,4},{6,7},{7,6},{8,9},{9,8},{10,11... | collective-permute-start | bytes 294920 | tf_op jit(solution)/shard_map/ppermute | solution.py:30
  22.5 4.8 %collective-permute-start.6 = (bf16[4,3072]{1,0:T(4,128)(2,1)S(1)}, bf16[4,3072]{1,0:T(4,128)(2,1)S(1)}, u32[]{:S(2)}, u32[]{:S(2)}) collective-permute-start(bf16[4,3072]{1,0:T(4,128)(2,1)S(1)} %slice.33), channel_id=1, source_target_pairs={{0,16},{1,17},{2,18},{3,19},{4,20},{5,21},{6,22},{7,23},{8,24},{9,... | collective-permute-start | bytes 73736 | tf_op jit(solution)/shard_map/ppermute | solution.py:30

commit v4 on v3

--- a/solution.py
+++ b/solution.py
@@ -108,6 +108,13 @@
     slope_ref[...] = slope
 
 
+def pack_kernel(places, *refs):
+    *pieces, out_ref = refs
+    for k, piece in zip(places, pieces):
+        rows = piece.shape[0]
+        out_ref[k * rows : (k + 1) * rows] = piece[...]
+
+
 def backward_kernel(order, pieces, me_ref, *refs):
     grads = refs[:pieces]
     kept_ref, w_ref, hidden_ref, slope_ref, wg_hbm, pg_hbm, grad_ref, wg_ref, pg_ref, sems = refs[pieces:]
@@ -205,8 +212,8 @@
     total = total + exchange(send, near[0]).astype(f32)
     parts = jnp.split(total, 1 << len(plane), axis=0)
     total = parts[0]
-    for part, bit in zip(parts[1:], combinations(plane)[1:]):
-        total = total + exchange(part.astype(bf16), bit).astype(f32)
+    for k in [2, 1, 3]:
+        total = total + exchange(parts[k].astype(bf16), combinations(plane)[k]).astype(f32)
     for bit in far:
         part = total[total.shape[0] // 2 :].astype(bf16)
         total = total[: total.shape[0] // 2]
@@ -215,8 +222,18 @@
         total = total + exchange(part, bit).astype(f32)
     stream_out = total.astype(bf16)
 
-    grads = [mine] + [exchange(mine, bit) for bit in combinations(plane)[1:]]
-    grads += [exchange(piece, near[0]) for piece in grads]
+    masks = combinations(plane)
+    places = [0] + [1, 3, 2]
+    grads = [mine] + [exchange(mine, masks[k]) for k in places[1:]]
+    mine = pl.pallas_call(
+        functools.partial(pack_kernel, places),
+        out_shape=shape(bf16, half, width),
+        in_specs=[VMEM()] * len(grads),
+        out_specs=VMEM(),
+        compiler_params=params,
+        name="pack",
+    )(*grads)
+    grads = [mine, exchange(mine, near[0])]
 
     weight_grad, preact_grad = pl.pallas_call(
         functools.partial(backward_kernel, gather_order, len(grads)),

time: 28.1 us -> 27.8 us (0.989)
  starting transfers between devices: 18.6 us -> 16.9 us
  waiting for transfers between devices: 2.06 us -> 3.49 us
    ppermute x15 -> x12, starting transfers between devices: 18.6 us -> 16.9 us  [exchange(): lax.ppermute(block, 'blk', [(i, i ^ bit) for i in range(lax.axis_size('bl...]
    ppermute x15 -> x12, waiting for transfers between devices: 2.06 us -> 3.49 us  [exchange(): lax.ppermute(block, 'blk', [(i, i ^ bit) for i in range(lax.axis_size('bl...]
  transfers between devices with their start and end apart: 15 -> 12, of which waited for: 3 -> 6; matrix products, arithmetic and copies ran while one was open for 1% -> 1% of each run, Pallas kernels for 20% -> 20%
where the time goes in v4:
time: 27.8 us; the launch traced here: 27.7 us
  starting transfers between devices  16.9 us (61%)
  Pallas kernels  5.59 us (20%)
  waiting for transfers between devices  3.49 us (13%)
  other arithmetic  0.86 us (3%)
  between operations  0.76 us (3%)
    ppermute x12, starting transfers between devices, exchange(): lax.ppermute(block, 'blk', [(i, i ^ bit) for i in range(lax.axis_size('bl...  16.9 us
    ppermute x12, waiting for transfers between devices, exchange(): lax.ppermute(block, 'blk', [(i, i ^ bit) for i in range(lax.axis_size('bl...  3.49 us
    pallas_call x1, Pallas kernels, body(): pl.pallas_call(functools.partial(backward_kernel, gather_order, len(grads...  2.73 us
    pallas_call x1, Pallas kernels, body(): pl.pallas_call(functools.partial(forward_kernel, scatter_order), out_shap...  2.49 us
    broadcast_in_dim x1, other arithmetic, body(): return (stream_out[None], preact_grad[None], weight_grad[None])  0.63 us
  transfers between devices with their start and end apart: 12, of which 6 were waited for; matrix products, arithmetic and copies ran while one was open for 1% of the time, Pallas kernels for 20%

profile of v4, /device:TPU:0, one launch (start us, length us, event | category | flops | bytes accessed | tf_op | source)
XLA Modules:
  0.0 27.7 jit_solution(10300971209777057504)
XLA Ops:
  0.6 0.0 copy-start
  0.6 3.1 %collective-permute-start = (bf16[4,3072]{1,0:T(4,128)(2,1)}, bf16[4,3072]{1,0:T(4,128)(2,1)S(1)}, u32[]{:S(2)}, u32[]{:S(2)}) collective-permute-start(bf16[4,3072]{1,0:T(4,128)(2,1)} %bitcast.16), channel_id=1, source_target_pairs={{0,8},{1,9},{2,10},{3,11},{4,12},{5,13},{6,14},{7,15},{8,0},{9,1},... | collective-permute-start | bytes 73736 | tf_op jit(solution)/shard_map/ppermute | solution.py:30
  3.7 2.5 %forward.1 = (f32[64,3072]{1,0:T(8,128)S(1)}, bf16[64,3072]{1,0:T(8,128)(2,1)S(1)}, bf16[512,3072]{1,0:T(8,128)(2,1)S(1)}, f32[4,3072]{1,0:T(4,128)S(1)}, bf16[128,512]{1,0:T(8,128)(2,1)S(1)}) custom-call(s32[1]{0:T(128)} %bitcast.me_ref, s32[4,24]{1,0:T(4,128)} %bitcast.19, bf16[128,512]{1,0:T(8,128)(2,1)} %bitcast.14, bf16[128,512]{1,0:T(8,128)(2,1)} %bitcast.15, ...), custom_call_target="tpu_custom_call" | custom-call | flops 402653184 | bytes 6000000 | tf_op jit(solution)/shard_map/forward/pallas_call | solution.py:173
  6.2 0.0 collective-permute-done
  6.2 0.1 collective-permute-start.1
  6.3 0.0 copy-done
  6.4 2.7 %collective-permute-start.7 = (bf16[8,3072]{1,0:T(8,128)(2,1)S(1)}, bf16[8,3072]{1,0:T(8,128)(2,1)S(1)}, u32[]{:S(2)}, u32[]{:S(2)}) collective-permute-start(bf16[8,3072]{1,0:T(8,128)(2,1)S(1)} %pad_maximum_fusion.1), channel_id=1, source_target_pairs={{0,16},{1,17},{2,18},{3,19},{4,20},{5,21},{6,22},{7,23},{8,24},{9,... | collective-permute-start | bytes 147464 | tf_op jit(solution)/shard_map/ppermute | solution.py:30
  9.0 0.0 collective-permute-done.1
  9.0 0.1 fusion.5
  9.2 2.5 %collective-permute-start.4 = (bf16[16,3072]{1,0:T(8,128)(2,1)S(1)}, bf16[16,3072]{1,0:T(8,128)(2,1)S(1)}, u32[]{:S(2)}, u32[]{:S(2)}) collective-permute-start(bf16[16,3072]{1,0:T(8,128)(2,1)S(1)} %get-tuple-element.28), channel_id=1, source_target_pairs={{0,6},{1,7},{2,4},{3,5},{4,2},{5,3},{6,0},{7,1},{8,14},{9,15},{10,... | collective-permute-start | bytes 294920 | tf_op jit(solution)/shard_map/ppermute | solution.py:30
  11.7 0.5 %collective-permute-start.3 = (bf16[16,3072]{1,0:T(8,128)(2,1)S(1)}, bf16[16,3072]{1,0:T(8,128)(2,1)S(1)}, u32[]{:S(2)}, u32[]{:S(2)}) collective-permute-start(bf16[16,3072]{1,0:T(8,128)(2,1)S(1)} %get-tuple-element.29), channel_id=1, source_target_pairs={{0,4},{1,5},{2,6},{3,7},{4,0},{5,1},{6,2},{7,3},{8,12},{9,13},{10,... | collective-permute-start | bytes 294920 | tf_op jit(solution)/shard_map/ppermute | solution.py:30
  12.2 0.5 %collective-permute-start.2 = (bf16[16,3072]{1,0:T(8,128)(2,1)S(1)}, bf16[16,3072]{1,0:T(8,128)(2,1)S(1)}, u32[]{:S(2)}, u32[]{:S(2)}) collective-permute-start(bf16[16,3072]{1,0:T(8,128)(2,1)S(1)} %get-tuple-element.27), channel_id=1, source_target_pairs={{0,2},{1,3},{2,0},{3,1},{4,6},{5,7},{6,4},{7,5},{8,10},{9,11},{10,... | collective-permute-start | bytes 294920 | tf_op jit(solution)/shard_map/ppermute | solution.py:30
  12.7 0.0 collective-permute-done.7
  12.8 1.6 %collective-permute-start.8 = (bf16[16,3072]{1,0:T(8,128)(2,1)S(1)}, bf16[16,3072]{1,0:T(8,128)(2,1)S(1)}, u32[]{:S(2)}, u32[]{:S(2)}) collective-permute-start(bf16[16,3072]{1,0:T(8,128)(2,1)S(1)} %pad_maximum_fusion.refs_0_), channel_id=1, source_target_pairs={{0,4},{1,5},{2,6},{3,7},{4,0},{5,1},{6,2},{7,3},{8,12},{9,13},{10,... | collective-permute-start | bytes 294920 | tf_op jit(solution)/shard_map/ppermute | solution.py:30
  14.4 1.4 %collective-permute-start.9 = (bf16[16,3072]{1,0:T(8,128)(2,1)S(1)}, bf16[16,3072]{1,0:T(8,128)(2,1)S(1)}, u32[]{:S(2)}, u32[]{:S(2)}) collective-permute-start(bf16[16,3072]{1,0:T(8,128)(2,1)S(1)} %pad_maximum_fusion.refs_0_), channel_id=1, source_target_pairs={{0,6},{1,7},{2,4},{3,5},{4,2},{5,3},{6,0},{7,1},{8,14},{9,15},{10,... | collective-permute-start | bytes 294920 | tf_op jit(solution)/shard_map/ppermute | solution.py:30
  15.8 0.0 collective-permute-done.4
  15.8 1.4 %collective-permute-start.10 = (bf16[16,3072]{1,0:T(8,128)(2,1)S(1)}, bf16[16,3072]{1,0:T(8,128)(2,1)S(1)}, u32[]{:S(2)}, u32[]{:S(2)}) collective-permute-start(bf16[16,3072]{1,0:T(8,128)(2,1)S(1)} %pad_maximum_fusion.refs_0_), channel_id=1, source_target_pairs={{0,2},{1,3},{2,0},{3,1},{4,6},{5,7},{6,4},{7,5},{8,10},{9,11},{10,... | collective-permute-start | bytes 294920 | tf_op jit(solution)/shard_map/ppermute | solution.py:30
  17.2 0.6 %collective-permute-done.3 = bf16[16,3072]{1,0:T(8,128)(2,1)S(1)} collective-permute-done((bf16[16,3072]{1,0:T(8,128)(2,1)S(1)}, bf16[16,3072]{1,0:T(8,128)(2,1)S(1)}, u32[]{:S(2)}, u32[]{:S(2)}) %collective-permute-start.3) | collective-permute-done | bytes 98336 | tf_op jit(solution)/shard_map/ppermute | solution.py:30
  17.8 0.2 collective-permute-done.2
  18.0 1.5 %collective-permute-start.5 = (bf16[8,3072]{1,0:T(8,128)(2,1)S(1)}, bf16[8,3072]{1,0:T(8,128)(2,1)S(1)}, u32[]{:S(2)}, u32[]{:S(2)}) collective-permute-start(bf16[8,3072]{1,0:T(8,128)(2,1)S(1)} %slice.32), channel_id=1, source_target_pairs={{0,8},{1,9},{2,10},{3,11},{4,12},{5,13},{6,14},{7,15},{8,0},{9,1},... | collective-permute-start | bytes 147464 | tf_op jit(solution)/shard_map/ppermute | solution.py:30
  19.5 0.3 %prepare.1 = (bf16[512,128]{1,0:T(8,128)(2,1)S(1)}, f32[512,128]{1,0:T(8,128)S(1)}) custom-call(s32[1]{0:T(128)} %bitcast.me_ref, bf16[128,512]{1,0:T(8,128)(2,1)S(1)} %get-tuple-element.20.back_ref), custom_call_target="tpu_custom_call" | custom-call | flops 16777216 | bytes 1500000 | tf_op jit(solution)/shard_map/prepare/pallas_call | solution.py:195
  19.8 1.5 %collective-permute-done.8.refs_1_ = bf16[16,3072]{1,0:T(8,128)(2,1)S(1)} collective-permute-done((bf16[16,3072]{1,0:T(8,128)(2,1)S(1)}, bf16[16,3072]{1,0:T(8,128)(2,1)S(1)}, u32[]{:S(2)}, u32[]{:S(2)}) %collective-permute-start.8) | collective-permute-done | bytes 98336 | tf_op jit(solution)/shard_map/ppermute | solution.py:30
  21.4 0.0 collective-permute-done.9.refs_2_
  21.4 0.1 collective-permute-done.10.refs_3_
  21.4 0.1 collective-permute-start.11
  21.5 0.6 %collective-permute-done.5 = bf16[8,3072]{1,0:T(8,128)(2,1)S(1)} collective-permute-done((bf16[8,3072]{1,0:T(8,128)(2,1)S(1)}, bf16[8,3072]{1,0:T(8,128)(2,1)S(1)}, u32[]{:S(2)}, u32[]{:S(2)}) %collective-permute-start.5) | collective-permute-done | bytes 49184 | tf_op jit(solution)/shard_map/ppermute | solution.py:30
  22.2 1.6 %collective-permute-start.6 = (bf16[4,3072]{1,0:T(4,128)(2,1)S(1)}, bf16[4,3072]{1,0:T(4,128)(2,1)S(1)}, u32[]{:S(2)}, u32[]{:S(2)}) collective-permute-start(bf16[4,3072]{1,0:T(4,128)(2,1)S(1)} %slice.33), channel_id=1, source_target_pairs={{0,16},{1,17},{2,18},{3,19},{4,20},{5,21},{6,22},{7,23},{8,24},{9,... | collective-permute-start | bytes 73736 | tf_op jit(solution)/shard_map/ppermute | solution.py:30
  23.8 0.0 collective-permute-done.11.refs_1_
  23.8 2.7 %backward.1 = (bf16[512,3072]{1,0:T(8,128)(2,1)}, bf16[128,512]{1,0:T(8,128)(2,1)}) custom-call(s32[1]{0:T(128)} %bitcast.me_ref, bf16[64,3072]{1,0:T(8,128)(2,1)S(1)} %pack.1.refs_0_, bf16[64,3072]{1,0:T(8,128)(2,1)S(1)} %collective-permute-done.11.refs_1_, f32[4,3072]{1,0:T(4,128)S(1)} %get-tuple-element.18.refs_2_, ...), custom_call_target="tpu_custom_call" | custom-call | flops 805306368 | bytes 6291456 | tf_op jit(solution)/shard_map/backward/pallas_call | solution.py:238
  26.5 0.5 %collective-permute-done.6 = bf16[4,3072]{1,0:T(4,128)(2,1)S(1)} collective-permute-done((bf16[4,3072]{1,0:T(4,128)(2,1)S(1)}, bf16[4,3072]{1,0:T(4,128)(2,1)S(1)}, u32[]{:S(2)}, u32[]{:S(2)}) %collective-permute-start.6) | collective-permute-done | bytes 24608 | tf_op jit(solution)/shard_map/ppermute | solution.py:30
  27.0 0.0 copy-done.1
  27.0 0.6 %fusion.4 = bf16[1,4,3072]{2,1,0:T(4,128)(2,1)} fusion(bf16[4,3072]{1,0:T(4,128)(2,1)S(1)} %collective-permute-done.6, f32[8,3072]{1,0:T(8,128)S(1)} %slice_add_fusion.1, bf16[1,4,3072]{2,1,0:T(4,128)(2,1)S(1)} %copy-done.1), kind=kLoop, calls=%fused_computation.12 | loop fusion | flops 61440 | bytes 122880 | tf_op jit(solution)/shard_map/broadcast_in_dim | solution.py:253
  (9 shorter events, 0.2 us)
Async XLA Ops:
  0.6 5.7 %copy-start = (bf16[1,4,3072]{2,1,0:T(4,128)(2,1)S(1)}, bf16[1,4,3072]{2,1,0:T(4,128)(2,1)}, u32[]{:S(2)}) copy-start(bf16[1,4,3072]{2,1,0:T(4,128)(2,1)} %param.7) | copy-start | bytes 73732
  0.6 5.6 %collective-permute-start = (bf16[4,3072]{1,0:T(4,128)(2,1)}, bf16[4,3072]{1,0:T(4,128)(2,1)S(1)}, u32[]{:S(2)}, u32[]{:S(2)}) collective-permute-start(bf16[4,3072]{1,0:T(4,128)(2,1)} %bitcast.16), channel_id=1, source_target_pairs={{0,8},{1,9},{2,10},{3,11},{4,12},{5,13},{6,14},{7,15},{8,0},{9,1},... | collective-permute-start | bytes 73736 | tf_op jit(solution)/shard_map/ppermute | solution.py:30
  6.2 2.8 %collective-permute-start.1 = (bf16[64,3072]{1,0:T(8,128)(2,1)S(1)}, bf16[64,3072]{1,0:T(8,128)(2,1)S(1)}, u32[]{:S(2)}, u32[]{:S(2)}) collective-permute-start(bf16[64,3072]{1,0:T(8,128)(2,1)S(1)} %get-tuple-element.16), channel_id=1, source_target_pairs={{0,1},{1,0},{2,3},{3,2},{4,5},{5,4},{6,7},{7,6},{8,9},{9,8},{10,11... | collective-permute-start | bytes 1179656 | tf_op jit(solution)/shard_map/ppermute | solution.py:30
  6.4 6.4 %collective-permute-start.7 = (bf16[8,3072]{1,0:T(8,128)(2,1)S(1)}, bf16[8,3072]{1,0:T(8,128)(2,1)S(1)}, u32[]{:S(2)}, u32[]{:S(2)}) collective-permute-start(bf16[8,3072]{1,0:T(8,128)(2,1)S(1)} %pad_maximum_fusion.1), channel_id=1, source_target_pairs={{0,16},{1,17},{2,18},{3,19},{4,20},{5,21},{6,22},{7,23},{8,24},{9,... | collective-permute-start | bytes 147464 | tf_op jit(solution)/shard_map/ppermute | solution.py:30
  9.2 6.6 %collective-permute-start.4 = (bf16[16,3072]{1,0:T(8,128)(2,1)S(1)}, bf16[16,3072]{1,0:T(8,128)(2,1)S(1)}, u32[]{:S(2)}, u32[]{:S(2)}) collective-permute-start(bf16[16,3072]{1,0:T(8,128)(2,1)S(1)} %get-tuple-element.28), channel_id=1, source_target_pairs={{0,6},{1,7},{2,4},{3,5},{4,2},{5,3},{6,0},{7,1},{8,14},{9,15},{10,... | collective-permute-start | bytes 294920 | tf_op jit(solution)/shard_map/ppermute | solution.py:30
  11.7 6.1 %collective-permute-start.3 = (bf16[16,3072]{1,0:T(8,128)(2,1)S(1)}, bf16[16,3072]{1,0:T(8,128)(2,1)S(1)}, u32[]{:S(2)}, u32[]{:S(2)}) collective-permute-start(bf16[16,3072]{1,0:T(8,128)(2,1)S(1)} %get-tuple-element.29), channel_id=1, source_target_pairs={{0,4},{1,5},{2,6},{3,7},{4,0},{5,1},{6,2},{7,3},{8,12},{9,13},{10,... | collective-permute-start | bytes 294920 | tf_op jit(solution)/shard_map/ppermute | solution.py:30
  12.2 5.8 %collective-permute-start.2 = (bf16[16,3072]{1,0:T(8,128)(2,1)S(1)}, bf16[16,3072]{1,0:T(8,128)(2,1)S(1)}, u32[]{:S(2)}, u32[]{:S(2)}) collective-permute-start(bf16[16,3072]{1,0:T(8,128)(2,1)S(1)} %get-tuple-element.27), channel_id=1, source_target_pairs={{0,2},{1,3},{2,0},{3,1},{4,6},{5,7},{6,4},{7,5},{8,10},{9,11},{10,... | collective-permute-start | bytes 294920 | tf_op jit(solution)/shard_map/ppermute | solution.py:30
  12.8 8.6 %collective-permute-start.8 = (bf16[16,3072]{1,0:T(8,128)(2,1)S(1)}, bf16[16,3072]{1,0:T(8,128)(2,1)S(1)}, u32[]{:S(2)}, u32[]{:S(2)}) collective-permute-start(bf16[16,3072]{1,0:T(8,128)(2,1)S(1)} %pad_maximum_fusion.refs_0_), channel_id=1, source_target_pairs={{0,4},{1,5},{2,6},{3,7},{4,0},{5,1},{6,2},{7,3},{8,12},{9,13},{10,... | collective-permute-start | bytes 294920 | tf_op jit(solution)/shard_map/ppermute | solution.py:30
  14.4 7.0 %collective-permute-start.9 = (bf16[16,3072]{1,0:T(8,128)(2,1)S(1)}, bf16[16,3072]{1,0:T(8,128)(2,1)S(1)}, u32[]{:S(2)}, u32[]{:S(2)}) collective-permute-start(bf16[16,3072]{1,0:T(8,128)(2,1)S(1)} %pad_maximum_fusion.refs_0_), channel_id=1, source_target_pairs={{0,6},{1,7},{2,4},{3,5},{4,2},{5,3},{6,0},{7,1},{8,14},{9,15},{10,... | collective-permute-start | bytes 294920 | tf_op jit(solution)/shard_map/ppermute | solution.py:30
  15.8 5.6 %collective-permute-start.10 = (bf16[16,3072]{1,0:T(8,128)(2,1)S(1)}, bf16[16,3072]{1,0:T(8,128)(2,1)S(1)}, u32[]{:S(2)}, u32[]{:S(2)}) collective-permute-start(bf16[16,3072]{1,0:T(8,128)(2,1)S(1)} %pad_maximum_fusion.refs_0_), channel_id=1, source_target_pairs={{0,2},{1,3},{2,0},{3,1},{4,6},{5,7},{6,4},{7,5},{8,10},{9,11},{10,... | collective-permute-start | bytes 294920 | tf_op jit(solution)/shard_map/ppermute | solution.py:30
  17.9 9.1 %copy-start.1 = (bf16[1,4,3072]{2,1,0:T(4,128)(2,1)S(1)}, bf16[1,4,3072]{2,1,0:T(4,128)(2,1)}, u32[]{:S(2)}) copy-start(bf16[1,4,3072]{2,1,0:T(4,128)(2,1)} %param.6) | copy-start | bytes 73732
  18.0 4.2 %collective-permute-start.5 = (bf16[8,3072]{1,0:T(8,128)(2,1)S(1)}, bf16[8,3072]{1,0:T(8,128)(2,1)S(1)}, u32[]{:S(2)}, u32[]{:S(2)}) collective-permute-start(bf16[8,3072]{1,0:T(8,128)(2,1)S(1)} %slice.32), channel_id=1, source_target_pairs={{0,8},{1,9},{2,10},{3,11},{4,12},{5,13},{6,14},{7,15},{8,0},{9,1},... | collective-permute-start | bytes 147464 | tf_op jit(solution)/shard_map/ppermute | solution.py:30
  21.4 2.4 %collective-permute-start.11 = (bf16[64,3072]{1,0:T(8,128)(2,1)S(1)}, bf16[64,3072]{1,0:T(8,128)(2,1)S(1)}, u32[]{:S(2)}, u32[]{:S(2)}) collective-permute-start(bf16[64,3072]{1,0:T(8,128)(2,1)S(1)} %pack.1.refs_0_), channel_id=1, source_target_pairs={{0,1},{1,0},{2,3},{3,2},{4,5},{5,4},{6,7},{7,6},{8,9},{9,8},{10,11... | collective-permute-start | bytes 1179656 | tf_op jit(solution)/shard_map/ppermute | solution.py:30
  22.2 4.8 %collective-permute-start.6 = (bf16[4,3072]{1,0:T(4,128)(2,1)S(1)}, bf16[4,3072]{1,0:T(4,128)(2,1)S(1)}, u32[]{:S(2)}, u32[]{:S(2)}) collective-permute-start(bf16[4,3072]{1,0:T(4,128)(2,1)S(1)} %slice.33), channel_id=1, source_target_pairs={{0,16},{1,17},{2,18},{3,19},{4,20},{5,21},{6,22},{7,23},{8,24},{9,... | collective-permute-start | bytes 73736 | tf_op jit(solution)/shard_map/ppermute | solution.py:30

commit v5 on v4

--- a/solution.py
+++ b/solution.py
@@ -11,7 +11,7 @@
 BLOCK = 128
 SCALE = math.sqrt(2.0 / math.pi)
 CUBIC = 0.044715
-CHUNK = 512
+CHUNK = 768
 WIDE = 1024
 LIMIT = 16 * 1024 * 1024
 FORWARD_BYTES = 6_000_000
@@ -131,7 +131,9 @@
             wg_ref[pl.ds(i * BLOCK, BLOCK), part] = band.astype(bf16)
         results.append(pltpu.make_async_copy(wg_ref.at[:, part], wg_hbm.at[:, part], sems.at[c]))
         results[-1].start()
-    total = lax.dot_general(w_ref[...], grad_ref[...], (((1,), (1,)), ((), ())), preferred_element_type=f32)
+    total = jnp.zeros((w_ref.shape[0], tokens), f32)
+    for part in parts:
+        total += jnp.dot(w_ref[:, part], grad_ref[:, part].T, preferred_element_type=f32)
     moved = (total * slope_ref[...]).astype(bf16)
     back = reorder(me_ref[0], tokens, order, back=True)
     pg_ref[...] = lax.dot_general(back, moved, (((1,), (1,)), ((), ())), preferred_element_type=f32).astype(bf16)

time: 27.8 us -> 27.8 us (level)
  no operation moved by 1% of the time
where the time goes in v5:
time: 27.8 us; the launch traced here: 27.7 us
  starting transfers between devices  16.9 us (61%)
  Pallas kernels  5.64 us (20%)
  waiting for transfers between devices  3.44 us (12%)
  other arithmetic  0.86 us (3%)
  between operations  0.76 us (3%)
    ppermute x12, starting transfers between devices, exchange(): lax.ppermute(block, 'blk', [(i, i ^ bit) for i in range(lax.axis_size('bl...  16.9 us
    ppermute x12, waiting for transfers between devices, exchange(): lax.ppermute(block, 'blk', [(i, i ^ bit) for i in range(lax.axis_size('bl...  3.44 us
    pallas_call x1, Pallas kernels, body(): pl.pallas_call(functools.partial(backward_kernel, gather_order, len(grads...  2.79 us
    pallas_call x1, Pallas kernels, body(): pl.pallas_call(functools.partial(forward_kernel, scatter_order), out_shap...  2.49 us
    broadcast_in_dim x1, other arithmetic, body(): return (stream_out[None], preact_grad[None], weight_grad[None])  0.63 us
  transfers between devices with their start and end apart: 12, of which 6 were waited for; matrix products, arithmetic and copies ran while one was open for 1% of the time, Pallas kernels for 20%

profile of v5, /device:TPU:0, one launch (start us, length us, event | category | flops | bytes accessed | tf_op | source)
XLA Modules:
  0.0 27.7 jit_solution(17521429552856776521)
XLA Ops:
  0.6 0.0 copy-start
  0.6 3.1 %collective-permute-start = (bf16[4,3072]{1,0:T(4,128)(2,1)}, bf16[4,3072]{1,0:T(4,128)(2,1)S(1)}, u32[]{:S(2)}, u32[]{:S(2)}) collective-permute-start(bf16[4,3072]{1,0:T(4,128)(2,1)} %bitcast.16), channel_id=1, source_target_pairs={{0,8},{1,9},{2,10},{3,11},{4,12},{5,13},{6,14},{7,15},{8,0},{9,1},... | collective-permute-start | bytes 73736 | tf_op jit(solution)/shard_map/ppermute | solution.py:30
  3.7 2.5 %forward.1 = (f32[64,3072]{1,0:T(8,128)S(1)}, bf16[64,3072]{1,0:T(8,128)(2,1)S(1)}, bf16[512,3072]{1,0:T(8,128)(2,1)S(1)}, f32[4,3072]{1,0:T(4,128)S(1)}, bf16[128,512]{1,0:T(8,128)(2,1)S(1)}) custom-call(s32[1]{0:T(128)} %bitcast.me_ref, s32[4,24]{1,0:T(4,128)} %bitcast.19, bf16[128,512]{1,0:T(8,128)(2,1)} %bitcast.14, bf16[128,512]{1,0:T(8,128)(2,1)} %bitcast.15, ...), custom_call_target="tpu_custom_call" | custom-call | flops 402653184 | bytes 6000000 | tf_op jit(solution)/shard_map/forward/pallas_call | solution.py:175
  6.2 0.0 collective-permute-done
  6.2 0.1 collective-permute-start.1
  6.3 0.0 copy-done
  6.4 2.7 %collective-permute-start.7 = (bf16[8,3072]{1,0:T(8,128)(2,1)S(1)}, bf16[8,3072]{1,0:T(8,128)(2,1)S(1)}, u32[]{:S(2)}, u32[]{:S(2)}) collective-permute-start(bf16[8,3072]{1,0:T(8,128)(2,1)S(1)} %pad_maximum_fusion.1), channel_id=1, source_target_pairs={{0,16},{1,17},{2,18},{3,19},{4,20},{5,21},{6,22},{7,23},{8,24},{9,... | collective-permute-start | bytes 147464 | tf_op jit(solution)/shard_map/ppermute | solution.py:30
  9.0 0.0 collective-permute-done.1
  9.0 0.1 fusion.5
  9.2 2.5 %collective-permute-start.4 = (bf16[16,3072]{1,0:T(8,128)(2,1)S(1)}, bf16[16,3072]{1,0:T(8,128)(2,1)S(1)}, u32[]{:S(2)}, u32[]{:S(2)}) collective-permute-start(bf16[16,3072]{1,0:T(8,128)(2,1)S(1)} %get-tuple-element.28), channel_id=1, source_target_pairs={{0,6},{1,7},{2,4},{3,5},{4,2},{5,3},{6,0},{7,1},{8,14},{9,15},{10,... | collective-permute-start | bytes 294920 | tf_op jit(solution)/shard_map/ppermute | solution.py:30
  11.7 0.5 %collective-permute-start.3 = (bf16[16,3072]{1,0:T(8,128)(2,1)S(1)}, bf16[16,3072]{1,0:T(8,128)(2,1)S(1)}, u32[]{:S(2)}, u32[]{:S(2)}) collective-permute-start(bf16[16,3072]{1,0:T(8,128)(2,1)S(1)} %get-tuple-element.29), channel_id=1, source_target_pairs={{0,4},{1,5},{2,6},{3,7},{4,0},{5,1},{6,2},{7,3},{8,12},{9,13},{10,... | collective-permute-start | bytes 294920 | tf_op jit(solution)/shard_map/ppermute | solution.py:30
  12.2 0.5 %collective-permute-start.2 = (bf16[16,3072]{1,0:T(8,128)(2,1)S(1)}, bf16[16,3072]{1,0:T(8,128)(2,1)S(1)}, u32[]{:S(2)}, u32[]{:S(2)}) collective-permute-start(bf16[16,3072]{1,0:T(8,128)(2,1)S(1)} %get-tuple-element.27), channel_id=1, source_target_pairs={{0,2},{1,3},{2,0},{3,1},{4,6},{5,7},{6,4},{7,5},{8,10},{9,11},{10,... | collective-permute-start | bytes 294920 | tf_op jit(solution)/shard_map/ppermute | solution.py:30
  12.7 0.0 collective-permute-done.7
  12.8 1.6 %collective-permute-start.8 = (bf16[16,3072]{1,0:T(8,128)(2,1)S(1)}, bf16[16,3072]{1,0:T(8,128)(2,1)S(1)}, u32[]{:S(2)}, u32[]{:S(2)}) collective-permute-start(bf16[16,3072]{1,0:T(8,128)(2,1)S(1)} %pad_maximum_fusion.refs_0_), channel_id=1, source_target_pairs={{0,4},{1,5},{2,6},{3,7},{4,0},{5,1},{6,2},{7,3},{8,12},{9,13},{10,... | collective-permute-start | bytes 294920 | tf_op jit(solution)/shard_map/ppermute | solution.py:30
  14.4 1.4 %collective-permute-start.9 = (bf16[16,3072]{1,0:T(8,128)(2,1)S(1)}, bf16[16,3072]{1,0:T(8,128)(2,1)S(1)}, u32[]{:S(2)}, u32[]{:S(2)}) collective-permute-start(bf16[16,3072]{1,0:T(8,128)(2,1)S(1)} %pad_maximum_fusion.refs_0_), channel_id=1, source_target_pairs={{0,6},{1,7},{2,4},{3,5},{4,2},{5,3},{6,0},{7,1},{8,14},{9,15},{10,... | collective-permute-start | bytes 294920 | tf_op jit(solution)/shard_map/ppermute | solution.py:30
  15.8 0.0 collective-permute-done.4
  15.8 1.4 %collective-permute-start.10 = (bf16[16,3072]{1,0:T(8,128)(2,1)S(1)}, bf16[16,3072]{1,0:T(8,128)(2,1)S(1)}, u32[]{:S(2)}, u32[]{:S(2)}) collective-permute-start(bf16[16,3072]{1,0:T(8,128)(2,1)S(1)} %pad_maximum_fusion.refs_0_), channel_id=1, source_target_pairs={{0,2},{1,3},{2,0},{3,1},{4,6},{5,7},{6,4},{7,5},{8,10},{9,11},{10,... | collective-permute-start | bytes 294920 | tf_op jit(solution)/shard_map/ppermute | solution.py:30
  17.2 0.6 %collective-permute-done.3 = bf16[16,3072]{1,0:T(8,128)(2,1)S(1)} collective-permute-done((bf16[16,3072]{1,0:T(8,128)(2,1)S(1)}, bf16[16,3072]{1,0:T(8,128)(2,1)S(1)}, u32[]{:S(2)}, u32[]{:S(2)}) %collective-permute-start.3) | collective-permute-done | bytes 98336 | tf_op jit(solution)/shard_map/ppermute | solution.py:30
  17.8 0.2 collective-permute-done.2
  18.0 1.5 %collective-permute-start.5 = (bf16[8,3072]{1,0:T(8,128)(2,1)S(1)}, bf16[8,3072]{1,0:T(8,128)(2,1)S(1)}, u32[]{:S(2)}, u32[]{:S(2)}) collective-permute-start(bf16[8,3072]{1,0:T(8,128)(2,1)S(1)} %slice.32), channel_id=1, source_target_pairs={{0,8},{1,9},{2,10},{3,11},{4,12},{5,13},{6,14},{7,15},{8,0},{9,1},... | collective-permute-start | bytes 147464 | tf_op jit(solution)/shard_map/ppermute | solution.py:30
  19.5 0.3 %prepare.1 = (bf16[512,128]{1,0:T(8,128)(2,1)S(1)}, f32[512,128]{1,0:T(8,128)S(1)}) custom-call(s32[1]{0:T(128)} %bitcast.me_ref, bf16[128,512]{1,0:T(8,128)(2,1)S(1)} %get-tuple-element.20.back_ref), custom_call_target="tpu_custom_call" | custom-call | flops 16777216 | bytes 1500000 | tf_op jit(solution)/shard_map/prepare/pallas_call | solution.py:197
  19.8 1.5 %collective-permute-done.8.refs_1_ = bf16[16,3072]{1,0:T(8,128)(2,1)S(1)} collective-permute-done((bf16[16,3072]{1,0:T(8,128)(2,1)S(1)}, bf16[16,3072]{1,0:T(8,128)(2,1)S(1)}, u32[]{:S(2)}, u32[]{:S(2)}) %collective-permute-start.8) | collective-permute-done | bytes 98336 | tf_op jit(solution)/shard_map/ppermute | solution.py:30
  21.4 0.0 collective-permute-done.9.refs_2_
  21.4 0.1 collective-permute-done.10.refs_3_
  21.4 0.1 collective-permute-start.11
  21.5 0.6 %collective-permute-done.5 = bf16[8,3072]{1,0:T(8,128)(2,1)S(1)} collective-permute-done((bf16[8,3072]{1,0:T(8,128)(2,1)S(1)}, bf16[8,3072]{1,0:T(8,128)(2,1)S(1)}, u32[]{:S(2)}, u32[]{:S(2)}) %collective-permute-start.5) | collective-permute-done | bytes 49184 | tf_op jit(solution)/shard_map/ppermute | solution.py:30
  22.2 1.6 %collective-permute-start.6 = (bf16[4,3072]{1,0:T(4,128)(2,1)S(1)}, bf16[4,3072]{1,0:T(4,128)(2,1)S(1)}, u32[]{:S(2)}, u32[]{:S(2)}) collective-permute-start(bf16[4,3072]{1,0:T(4,128)(2,1)S(1)} %slice.33), channel_id=1, source_target_pairs={{0,16},{1,17},{2,18},{3,19},{4,20},{5,21},{6,22},{7,23},{8,24},{9,... | collective-permute-start | bytes 73736 | tf_op jit(solution)/shard_map/ppermute | solution.py:30
  23.8 0.0 collective-permute-done.11.refs_1_
  23.8 2.8 %backward.1 = (bf16[512,3072]{1,0:T(8,128)(2,1)}, bf16[128,512]{1,0:T(8,128)(2,1)}) custom-call(s32[1]{0:T(128)} %bitcast.me_ref, bf16[64,3072]{1,0:T(8,128)(2,1)S(1)} %pack.1.refs_0_, bf16[64,3072]{1,0:T(8,128)(2,1)S(1)} %collective-permute-done.11.refs_1_, f32[4,3072]{1,0:T(4,128)S(1)} %get-tuple-element.18.refs_2_, ...), custom_call_target="tpu_custom_call" | custom-call | flops 805306368 | bytes 6291456 | tf_op jit(solution)/shard_map/backward/pallas_call | solution.py:240
  26.6 0.4 %collective-permute-done.6 = bf16[4,3072]{1,0:T(4,128)(2,1)S(1)} collective-permute-done((bf16[4,3072]{1,0:T(4,128)(2,1)S(1)}, bf16[4,3072]{1,0:T(4,128)(2,1)S(1)}, u32[]{:S(2)}, u32[]{:S(2)}) %collective-permute-start.6) | collective-permute-done | bytes 24608 | tf_op jit(solution)/shard_map/ppermute | solution.py:30
  27.0 0.0 copy-done.1
  27.0 0.6 %fusion.4 = bf16[1,4,3072]{2,1,0:T(4,128)(2,1)} fusion(bf16[4,3072]{1,0:T(4,128)(2,1)S(1)} %collective-permute-done.6, f32[8,3072]{1,0:T(8,128)S(1)} %slice_add_fusion.1, bf16[1,4,3072]{2,1,0:T(4,128)(2,1)S(1)} %copy-done.1), kind=kLoop, calls=%fused_computation.12 | loop fusion | flops 61440 | bytes 122880 | tf_op jit(solution)/shard_map/broadcast_in_dim | solution.py:255
  (9 shorter events, 0.2 us)
Async XLA Ops:
  0.6 5.7 %copy-start = (bf16[1,4,3072]{2,1,0:T(4,128)(2,1)S(1)}, bf16[1,4,3072]{2,1,0:T(4,128)(2,1)}, u32[]{:S(2)}) copy-start(bf16[1,4,3072]{2,1,0:T(4,128)(2,1)} %param.7) | copy-start | bytes 73732
  0.6 5.6 %collective-permute-start = (bf16[4,3072]{1,0:T(4,128)(2,1)}, bf16[4,3072]{1,0:T(4,128)(2,1)S(1)}, u32[]{:S(2)}, u32[]{:S(2)}) collective-permute-start(bf16[4,3072]{1,0:T(4,128)(2,1)} %bitcast.16), channel_id=1, source_target_pairs={{0,8},{1,9},{2,10},{3,11},{4,12},{5,13},{6,14},{7,15},{8,0},{9,1},... | collective-permute-start | bytes 73736 | tf_op jit(solution)/shard_map/ppermute | solution.py:30
  6.2 2.8 %collective-permute-start.1 = (bf16[64,3072]{1,0:T(8,128)(2,1)S(1)}, bf16[64,3072]{1,0:T(8,128)(2,1)S(1)}, u32[]{:S(2)}, u32[]{:S(2)}) collective-permute-start(bf16[64,3072]{1,0:T(8,128)(2,1)S(1)} %get-tuple-element.16), channel_id=1, source_target_pairs={{0,1},{1,0},{2,3},{3,2},{4,5},{5,4},{6,7},{7,6},{8,9},{9,8},{10,11... | collective-permute-start | bytes 1179656 | tf_op jit(solution)/shard_map/ppermute | solution.py:30
  6.4 6.4 %collective-permute-start.7 = (bf16[8,3072]{1,0:T(8,128)(2,1)S(1)}, bf16[8,3072]{1,0:T(8,128)(2,1)S(1)}, u32[]{:S(2)}, u32[]{:S(2)}) collective-permute-start(bf16[8,3072]{1,0:T(8,128)(2,1)S(1)} %pad_maximum_fusion.1), channel_id=1, source_target_pairs={{0,16},{1,17},{2,18},{3,19},{4,20},{5,21},{6,22},{7,23},{8,24},{9,... | collective-permute-start | bytes 147464 | tf_op jit(solution)/shard_map/ppermute | solution.py:30
  9.2 6.6 %collective-permute-start.4 = (bf16[16,3072]{1,0:T(8,128)(2,1)S(1)}, bf16[16,3072]{1,0:T(8,128)(2,1)S(1)}, u32[]{:S(2)}, u32[]{:S(2)}) collective-permute-start(bf16[16,3072]{1,0:T(8,128)(2,1)S(1)} %get-tuple-element.28), channel_id=1, source_target_pairs={{0,6},{1,7},{2,4},{3,5},{4,2},{5,3},{6,0},{7,1},{8,14},{9,15},{10,... | collective-permute-start | bytes 294920 | tf_op jit(solution)/shard_map/ppermute | solution.py:30
  11.7 6.1 %collective-permute-start.3 = (bf16[16,3072]{1,0:T(8,128)(2,1)S(1)}, bf16[16,3072]{1,0:T(8,128)(2,1)S(1)}, u32[]{:S(2)}, u32[]{:S(2)}) collective-permute-start(bf16[16,3072]{1,0:T(8,128)(2,1)S(1)} %get-tuple-element.29), channel_id=1, source_target_pairs={{0,4},{1,5},{2,6},{3,7},{4,0},{5,1},{6,2},{7,3},{8,12},{9,13},{10,... | collective-permute-start | bytes 294920 | tf_op jit(solution)/shard_map/ppermute | solution.py:30
  12.2 5.8 %collective-permute-start.2 = (bf16[16,3072]{1,0:T(8,128)(2,1)S(1)}, bf16[16,3072]{1,0:T(8,128)(2,1)S(1)}, u32[]{:S(2)}, u32[]{:S(2)}) collective-permute-start(bf16[16,3072]{1,0:T(8,128)(2,1)S(1)} %get-tuple-element.27), channel_id=1, source_target_pairs={{0,2},{1,3},{2,0},{3,1},{4,6},{5,7},{6,4},{7,5},{8,10},{9,11},{10,... | collective-permute-start | bytes 294920 | tf_op jit(solution)/shard_map/ppermute | solution.py:30
  12.8 8.6 %collective-permute-start.8 = (bf16[16,3072]{1,0:T(8,128)(2,1)S(1)}, bf16[16,3072]{1,0:T(8,128)(2,1)S(1)}, u32[]{:S(2)}, u32[]{:S(2)}) collective-permute-start(bf16[16,3072]{1,0:T(8,128)(2,1)S(1)} %pad_maximum_fusion.refs_0_), channel_id=1, source_target_pairs={{0,4},{1,5},{2,6},{3,7},{4,0},{5,1},{6,2},{7,3},{8,12},{9,13},{10,... | collective-permute-start | bytes 294920 | tf_op jit(solution)/shard_map/ppermute | solution.py:30
  14.4 7.0 %collective-permute-start.9 = (bf16[16,3072]{1,0:T(8,128)(2,1)S(1)}, bf16[16,3072]{1,0:T(8,128)(2,1)S(1)}, u32[]{:S(2)}, u32[]{:S(2)}) collective-permute-start(bf16[16,3072]{1,0:T(8,128)(2,1)S(1)} %pad_maximum_fusion.refs_0_), channel_id=1, source_target_pairs={{0,6},{1,7},{2,4},{3,5},{4,2},{5,3},{6,0},{7,1},{8,14},{9,15},{10,... | collective-permute-start | bytes 294920 | tf_op jit(solution)/shard_map/ppermute | solution.py:30
  15.8 5.6 %collective-permute-start.10 = (bf16[16,3072]{1,0:T(8,128)(2,1)S(1)}, bf16[16,3072]{1,0:T(8,128)(2,1)S(1)}, u32[]{:S(2)}, u32[]{:S(2)}) collective-permute-start(bf16[16,3072]{1,0:T(8,128)(2,1)S(1)} %pad_maximum_fusion.refs_0_), channel_id=1, source_target_pairs={{0,2},{1,3},{2,0},{3,1},{4,6},{5,7},{6,4},{7,5},{8,10},{9,11},{10,... | collective-permute-start | bytes 294920 | tf_op jit(solution)/shard_map/ppermute | solution.py:30
  17.9 9.1 %copy-start.1 = (bf16[1,4,3072]{2,1,0:T(4,128)(2,1)S(1)}, bf16[1,4,3072]{2,1,0:T(4,128)(2,1)}, u32[]{:S(2)}) copy-start(bf16[1,4,3072]{2,1,0:T(4,128)(2,1)} %param.6) | copy-start | bytes 73732
  18.0 4.2 %collective-permute-start.5 = (bf16[8,3072]{1,0:T(8,128)(2,1)S(1)}, bf16[8,3072]{1,0:T(8,128)(2,1)S(1)}, u32[]{:S(2)}, u32[]{:S(2)}) collective-permute-start(bf16[8,3072]{1,0:T(8,128)(2,1)S(1)} %slice.32), channel_id=1, source_target_pairs={{0,8},{1,9},{2,10},{3,11},{4,12},{5,13},{6,14},{7,15},{8,0},{9,1},... | collective-permute-start | bytes 147464 | tf_op jit(solution)/shard_map/ppermute | solution.py:30
  21.4 2.4 %collective-permute-start.11 = (bf16[64,3072]{1,0:T(8,128)(2,1)S(1)}, bf16[64,3072]{1,0:T(8,128)(2,1)S(1)}, u32[]{:S(2)}, u32[]{:S(2)}) collective-permute-start(bf16[64,3072]{1,0:T(8,128)(2,1)S(1)} %pack.1.refs_0_), channel_id=1, source_target_pairs={{0,1},{1,0},{2,3},{3,2},{4,5},{5,4},{6,7},{7,6},{8,9},{9,8},{10,11... | collective-permute-start | bytes 1179656 | tf_op jit(solution)/shard_map/ppermute | solution.py:30
  22.2 4.8 %collective-permute-start.6 = (bf16[4,3072]{1,0:T(4,128)(2,1)S(1)}, bf16[4,3072]{1,0:T(4,128)(2,1)S(1)}, u32[]{:S(2)}, u32[]{:S(2)}) collective-permute-start(bf16[4,3072]{1,0:T(4,128)(2,1)S(1)} %slice.33), channel_id=1, source_target_pairs={{0,16},{1,17},{2,18},{3,19},{4,20},{5,21},{6,22},{7,23},{8,24},{9,... | collective-permute-start | bytes 73736 | tf_op jit(solution)/shard_map/ppermute | solution.py:30

commit v6 on v4

--- a/solution.py
+++ b/solution.py
@@ -223,7 +223,7 @@
     stream_out = total.astype(bf16)
 
     masks = combinations(plane)
-    places = [0] + [1, 3, 2]
+    places = [0] + [2, 3, 1]
     grads = [mine] + [exchange(mine, masks[k]) for k in places[1:]]
     mine = pl.pallas_call(
         functools.partial(pack_kernel, places),

time: 27.8 us -> 27.8 us (level)
  no operation moved by 1% of the time
where the time goes in v6:
time: 27.8 us; the launch traced here: 27.6 us
  starting transfers between devices  17.1 us (62%)
  Pallas kernels  5.59 us (20%)
  waiting for transfers between devices  3.3 us (12%)
  other arithmetic  0.86 us (3%)
  between operations  0.76 us (3%)
    ppermute x12, starting transfers between devices, exchange(): lax.ppermute(block, 'blk', [(i, i ^ bit) for i in range(lax.axis_size('bl...  17.1 us
    ppermute x12, waiting for transfers between devices, exchange(): lax.ppermute(block, 'blk', [(i, i ^ bit) for i in range(lax.axis_size('bl...  3.3 us
    pallas_call x1, Pallas kernels, body(): pl.pallas_call(functools.partial(backward_kernel, gather_order, len(grads...  2.73 us
    pallas_call x1, Pallas kernels, body(): pl.pallas_call(functools.partial(forward_kernel, scatter_order), out_shap...  2.49 us
    broadcast_in_dim x1, other arithmetic, body(): return (stream_out[None], preact_grad[None], weight_grad[None])  0.63 us
  transfers between devices with their start and end apart: 12, of which 6 were waited for; matrix products, arithmetic and copies ran while one was open for 1% of the time, Pallas kernels for 20%

profile of v6, /device:TPU:0, one launch (start us, length us, event | category | flops | bytes accessed | tf_op | source)
XLA Modules:
  0.0 27.6 jit_solution(3148422754528002771)
XLA Ops:
  0.6 0.0 copy-start
  0.6 3.1 %collective-permute-start = (bf16[4,3072]{1,0:T(4,128)(2,1)}, bf16[4,3072]{1,0:T(4,128)(2,1)S(1)}, u32[]{:S(2)}, u32[]{:S(2)}) collective-permute-start(bf16[4,3072]{1,0:T(4,128)(2,1)} %bitcast.16), channel_id=1, source_target_pairs={{0,8},{1,9},{2,10},{3,11},{4,12},{5,13},{6,14},{7,15},{8,0},{9,1},... | collective-permute-start | bytes 73736 | tf_op jit(solution)/shard_map/ppermute | solution.py:30
  3.7 2.5 %forward.1 = (f32[64,3072]{1,0:T(8,128)S(1)}, bf16[64,3072]{1,0:T(8,128)(2,1)S(1)}, bf16[512,3072]{1,0:T(8,128)(2,1)S(1)}, f32[4,3072]{1,0:T(4,128)S(1)}, bf16[128,512]{1,0:T(8,128)(2,1)S(1)}) custom-call(s32[1]{0:T(128)} %bitcast.me_ref, s32[4,24]{1,0:T(4,128)} %bitcast.19, bf16[128,512]{1,0:T(8,128)(2,1)} %bitcast.14, bf16[128,512]{1,0:T(8,128)(2,1)} %bitcast.15, ...), custom_call_target="tpu_custom_call" | custom-call | flops 402653184 | bytes 6000000 | tf_op jit(solution)/shard_map/forward/pallas_call | solution.py:173
  6.2 0.0 collective-permute-done
  6.2 0.1 collective-permute-start.1
  6.3 0.0 copy-done
  6.4 2.7 %collective-permute-start.7 = (bf16[8,3072]{1,0:T(8,128)(2,1)S(1)}, bf16[8,3072]{1,0:T(8,128)(2,1)S(1)}, u32[]{:S(2)}, u32[]{:S(2)}) collective-permute-start(bf16[8,3072]{1,0:T(8,128)(2,1)S(1)} %pad_maximum_fusion.1), channel_id=1, source_target_pairs={{0,16},{1,17},{2,18},{3,19},{4,20},{5,21},{6,22},{7,23},{8,24},{9,... | collective-permute-start | bytes 147464 | tf_op jit(solution)/shard_map/ppermute | solution.py:30
  9.0 0.0 collective-permute-done.1
  9.0 0.1 fusion.5
  9.2 2.5 %collective-permute-start.4 = (bf16[16,3072]{1,0:T(8,128)(2,1)S(1)}, bf16[16,3072]{1,0:T(8,128)(2,1)S(1)}, u32[]{:S(2)}, u32[]{:S(2)}) collective-permute-start(bf16[16,3072]{1,0:T(8,128)(2,1)S(1)} %get-tuple-element.28), channel_id=1, source_target_pairs={{0,6},{1,7},{2,4},{3,5},{4,2},{5,3},{6,0},{7,1},{8,14},{9,15},{10,... | collective-permute-start | bytes 294920 | tf_op jit(solution)/shard_map/ppermute | solution.py:30
  11.7 0.5 %collective-permute-start.3 = (bf16[16,3072]{1,0:T(8,128)(2,1)S(1)}, bf16[16,3072]{1,0:T(8,128)(2,1)S(1)}, u32[]{:S(2)}, u32[]{:S(2)}) collective-permute-start(bf16[16,3072]{1,0:T(8,128)(2,1)S(1)} %get-tuple-element.29), channel_id=1, source_target_pairs={{0,4},{1,5},{2,6},{3,7},{4,0},{5,1},{6,2},{7,3},{8,12},{9,13},{10,... | collective-permute-start | bytes 294920 | tf_op jit(solution)/shard_map/ppermute | solution.py:30
  12.2 0.5 %collective-permute-start.2 = (bf16[16,3072]{1,0:T(8,128)(2,1)S(1)}, bf16[16,3072]{1,0:T(8,128)(2,1)S(1)}, u32[]{:S(2)}, u32[]{:S(2)}) collective-permute-start(bf16[16,3072]{1,0:T(8,128)(2,1)S(1)} %get-tuple-element.27), channel_id=1, source_target_pairs={{0,2},{1,3},{2,0},{3,1},{4,6},{5,7},{6,4},{7,5},{8,10},{9,11},{10,... | collective-permute-start | bytes 294920 | tf_op jit(solution)/shard_map/ppermute | solution.py:30
  12.7 0.0 collective-permute-done.7
  12.8 1.5 %collective-permute-start.8 = (bf16[16,3072]{1,0:T(8,128)(2,1)S(1)}, bf16[16,3072]{1,0:T(8,128)(2,1)S(1)}, u32[]{:S(2)}, u32[]{:S(2)}) collective-permute-start(bf16[16,3072]{1,0:T(8,128)(2,1)S(1)} %pad_maximum_fusion.refs_0_), channel_id=1, source_target_pairs={{0,2},{1,3},{2,0},{3,1},{4,6},{5,7},{6,4},{7,5},{8,10},{9,11},{10,... | collective-permute-start | bytes 294920 | tf_op jit(solution)/shard_map/ppermute | solution.py:30
  14.3 1.5 %collective-permute-start.9 = (bf16[16,3072]{1,0:T(8,128)(2,1)S(1)}, bf16[16,3072]{1,0:T(8,128)(2,1)S(1)}, u32[]{:S(2)}, u32[]{:S(2)}) collective-permute-start(bf16[16,3072]{1,0:T(8,128)(2,1)S(1)} %pad_maximum_fusion.refs_0_), channel_id=1, source_target_pairs={{0,6},{1,7},{2,4},{3,5},{4,2},{5,3},{6,0},{7,1},{8,14},{9,15},{10,... | collective-permute-start | bytes 294920 | tf_op jit(solution)/shard_map/ppermute | solution.py:30
  15.8 0.0 collective-permute-done.4
  15.8 1.5 %collective-permute-start.10 = (bf16[16,3072]{1,0:T(8,128)(2,1)S(1)}, bf16[16,3072]{1,0:T(8,128)(2,1)S(1)}, u32[]{:S(2)}, u32[]{:S(2)}) collective-permute-start(bf16[16,3072]{1,0:T(8,128)(2,1)S(1)} %pad_maximum_fusion.refs_0_), channel_id=1, source_target_pairs={{0,4},{1,5},{2,6},{3,7},{4,0},{5,1},{6,2},{7,3},{8,12},{9,13},{10,... | collective-permute-start | bytes 294920 | tf_op jit(solution)/shard_map/ppermute | solution.py:30
  17.3 0.0 collective-permute-done.3
  17.3 0.6 %collective-permute-done.2 = bf16[16,3072]{1,0:T(8,128)(2,1)S(1)} collective-permute-done((bf16[16,3072]{1,0:T(8,128)(2,1)S(1)}, bf16[16,3072]{1,0:T(8,128)(2,1)S(1)}, u32[]{:S(2)}, u32[]{:S(2)}) %collective-permute-start.2) | collective-permute-done | bytes 98336 | tf_op jit(solution)/shard_map/ppermute | solution.py:30
  18.0 1.5 %collective-permute-start.5 = (bf16[8,3072]{1,0:T(8,128)(2,1)S(1)}, bf16[8,3072]{1,0:T(8,128)(2,1)S(1)}, u32[]{:S(2)}, u32[]{:S(2)}) collective-permute-start(bf16[8,3072]{1,0:T(8,128)(2,1)S(1)} %slice.32), channel_id=1, source_target_pairs={{0,8},{1,9},{2,10},{3,11},{4,12},{5,13},{6,14},{7,15},{8,0},{9,1},... | collective-permute-start | bytes 147464 | tf_op jit(solution)/shard_map/ppermute | solution.py:30
  19.5 0.3 %prepare.1 = (bf16[512,128]{1,0:T(8,128)(2,1)S(1)}, f32[512,128]{1,0:T(8,128)S(1)}) custom-call(s32[1]{0:T(128)} %bitcast.me_ref, bf16[128,512]{1,0:T(8,128)(2,1)S(1)} %get-tuple-element.20.back_ref), custom_call_target="tpu_custom_call" | custom-call | flops 16777216 | bytes 1500000 | tf_op jit(solution)/shard_map/prepare/pallas_call | solution.py:195
  19.8 0.2 collective-permute-done.8.refs_1_
  20.0 1.8 %collective-permute-done.9.refs_2_ = bf16[16,3072]{1,0:T(8,128)(2,1)S(1)} collective-permute-done((bf16[16,3072]{1,0:T(8,128)(2,1)S(1)}, bf16[16,3072]{1,0:T(8,128)(2,1)S(1)}, u32[]{:S(2)}, u32[]{:S(2)}) %collective-permute-start.9) | collective-permute-done | bytes 98336 | tf_op jit(solution)/shard_map/ppermute | solution.py:30
  21.8 0.2 collective-permute-done.10.refs_3_
  22.0 0.1 collective-permute-start.11
  22.1 0.1 collective-permute-done.5
  22.2 1.6 %collective-permute-start.6 = (bf16[4,3072]{1,0:T(4,128)(2,1)S(1)}, bf16[4,3072]{1,0:T(4,128)(2,1)S(1)}, u32[]{:S(2)}, u32[]{:S(2)}) collective-permute-start(bf16[4,3072]{1,0:T(4,128)(2,1)S(1)} %slice.33), channel_id=1, source_target_pairs={{0,16},{1,17},{2,18},{3,19},{4,20},{5,21},{6,22},{7,23},{8,24},{9,... | collective-permute-start | bytes 73736 | tf_op jit(solution)/shard_map/ppermute | solution.py:30
  23.8 0.0 collective-permute-done.11.refs_1_
  23.8 2.7 %backward.1 = (bf16[512,3072]{1,0:T(8,128)(2,1)}, bf16[128,512]{1,0:T(8,128)(2,1)}) custom-call(s32[1]{0:T(128)} %bitcast.me_ref, bf16[64,3072]{1,0:T(8,128)(2,1)S(1)} %pack.1.refs_0_, bf16[64,3072]{1,0:T(8,128)(2,1)S(1)} %collective-permute-done.11.refs_1_, f32[4,3072]{1,0:T(4,128)S(1)} %get-tuple-element.18.refs_2_, ...), custom_call_target="tpu_custom_call" | custom-call | flops 805306368 | bytes 6291456 | tf_op jit(solution)/shard_map/backward/pallas_call | solution.py:238
  26.5 0.4 %collective-permute-done.6 = bf16[4,3072]{1,0:T(4,128)(2,1)S(1)} collective-permute-done((bf16[4,3072]{1,0:T(4,128)(2,1)S(1)}, bf16[4,3072]{1,0:T(4,128)(2,1)S(1)}, u32[]{:S(2)}, u32[]{:S(2)}) %collective-permute-start.6) | collective-permute-done | bytes 24608 | tf_op jit(solution)/shard_map/ppermute | solution.py:30
  27.0 0.0 copy-done.1
  27.0 0.6 %fusion.4 = bf16[1,4,3072]{2,1,0:T(4,128)(2,1)} fusion(bf16[4,3072]{1,0:T(4,128)(2,1)S(1)} %collective-permute-done.6, f32[8,3072]{1,0:T(8,128)S(1)} %slice_add_fusion.1, bf16[1,4,3072]{2,1,0:T(4,128)(2,1)S(1)} %copy-done.1), kind=kLoop, calls=%fused_computation.12 | loop fusion | flops 61440 | bytes 122880 | tf_op jit(solution)/shard_map/broadcast_in_dim | solution.py:253
  (9 shorter events, 0.2 us)
Async XLA Ops:
  0.6 5.7 %copy-start = (bf16[1,4,3072]{2,1,0:T(4,128)(2,1)S(1)}, bf16[1,4,3072]{2,1,0:T(4,128)(2,1)}, u32[]{:S(2)}) copy-start(bf16[1,4,3072]{2,1,0:T(4,128)(2,1)} %param.7) | copy-start | bytes 73732
  0.6 5.6 %collective-permute-start = (bf16[4,3072]{1,0:T(4,128)(2,1)}, bf16[4,3072]{1,0:T(4,128)(2,1)S(1)}, u32[]{:S(2)}, u32[]{:S(2)}) collective-permute-start(bf16[4,3072]{1,0:T(4,128)(2,1)} %bitcast.16), channel_id=1, source_target_pairs={{0,8},{1,9},{2,10},{3,11},{4,12},{5,13},{6,14},{7,15},{8,0},{9,1},... | collective-permute-start | bytes 73736 | tf_op jit(solution)/shard_map/ppermute | solution.py:30
  6.2 2.8 %collective-permute-start.1 = (bf16[64,3072]{1,0:T(8,128)(2,1)S(1)}, bf16[64,3072]{1,0:T(8,128)(2,1)S(1)}, u32[]{:S(2)}, u32[]{:S(2)}) collective-permute-start(bf16[64,3072]{1,0:T(8,128)(2,1)S(1)} %get-tuple-element.16), channel_id=1, source_target_pairs={{0,1},{1,0},{2,3},{3,2},{4,5},{5,4},{6,7},{7,6},{8,9},{9,8},{10,11... | collective-permute-start | bytes 1179656 | tf_op jit(solution)/shard_map/ppermute | solution.py:30
  6.4 6.4 %collective-permute-start.7 = (bf16[8,3072]{1,0:T(8,128)(2,1)S(1)}, bf16[8,3072]{1,0:T(8,128)(2,1)S(1)}, u32[]{:S(2)}, u32[]{:S(2)}) collective-permute-start(bf16[8,3072]{1,0:T(8,128)(2,1)S(1)} %pad_maximum_fusion.1), channel_id=1, source_target_pairs={{0,16},{1,17},{2,18},{3,19},{4,20},{5,21},{6,22},{7,23},{8,24},{9,... | collective-permute-start | bytes 147464 | tf_op jit(solution)/shard_map/ppermute | solution.py:30
  9.2 6.7 %collective-permute-start.4 = (bf16[16,3072]{1,0:T(8,128)(2,1)S(1)}, bf16[16,3072]{1,0:T(8,128)(2,1)S(1)}, u32[]{:S(2)}, u32[]{:S(2)}) collective-permute-start(bf16[16,3072]{1,0:T(8,128)(2,1)S(1)} %get-tuple-element.28), channel_id=1, source_target_pairs={{0,6},{1,7},{2,4},{3,5},{4,2},{5,3},{6,0},{7,1},{8,14},{9,15},{10,... | collective-permute-start | bytes 294920 | tf_op jit(solution)/shard_map/ppermute | solution.py:30
  11.7 5.6 %collective-permute-start.3 = (bf16[16,3072]{1,0:T(8,128)(2,1)S(1)}, bf16[16,3072]{1,0:T(8,128)(2,1)S(1)}, u32[]{:S(2)}, u32[]{:S(2)}) collective-permute-start(bf16[16,3072]{1,0:T(8,128)(2,1)S(1)} %get-tuple-element.29), channel_id=1, source_target_pairs={{0,4},{1,5},{2,6},{3,7},{4,0},{5,1},{6,2},{7,3},{8,12},{9,13},{10,... | collective-permute-start | bytes 294920 | tf_op jit(solution)/shard_map/ppermute | solution.py:30
  12.2 5.8 %collective-permute-start.2 = (bf16[16,3072]{1,0:T(8,128)(2,1)S(1)}, bf16[16,3072]{1,0:T(8,128)(2,1)S(1)}, u32[]{:S(2)}, u32[]{:S(2)}) collective-permute-start(bf16[16,3072]{1,0:T(8,128)(2,1)S(1)} %get-tuple-element.27), channel_id=1, source_target_pairs={{0,2},{1,3},{2,0},{3,1},{4,6},{5,7},{6,4},{7,5},{8,10},{9,11},{10,... | collective-permute-start | bytes 294920 | tf_op jit(solution)/shard_map/ppermute | solution.py:30
  12.8 7.3 %collective-permute-start.8 = (bf16[16,3072]{1,0:T(8,128)(2,1)S(1)}, bf16[16,3072]{1,0:T(8,128)(2,1)S(1)}, u32[]{:S(2)}, u32[]{:S(2)}) collective-permute-start(bf16[16,3072]{1,0:T(8,128)(2,1)S(1)} %pad_maximum_fusion.refs_0_), channel_id=1, source_target_pairs={{0,2},{1,3},{2,0},{3,1},{4,6},{5,7},{6,4},{7,5},{8,10},{9,11},{10,... | collective-permute-start | bytes 294920 | tf_op jit(solution)/shard_map/ppermute | solution.py:30
  14.3 7.5 %collective-permute-start.9 = (bf16[16,3072]{1,0:T(8,128)(2,1)S(1)}, bf16[16,3072]{1,0:T(8,128)(2,1)S(1)}, u32[]{:S(2)}, u32[]{:S(2)}) collective-permute-start(bf16[16,3072]{1,0:T(8,128)(2,1)S(1)} %pad_maximum_fusion.refs_0_), channel_id=1, source_target_pairs={{0,6},{1,7},{2,4},{3,5},{4,2},{5,3},{6,0},{7,1},{8,14},{9,15},{10,... | collective-permute-start | bytes 294920 | tf_op jit(solution)/shard_map/ppermute | solution.py:30
  15.8 6.1 %collective-permute-start.10 = (bf16[16,3072]{1,0:T(8,128)(2,1)S(1)}, bf16[16,3072]{1,0:T(8,128)(2,1)S(1)}, u32[]{:S(2)}, u32[]{:S(2)}) collective-permute-start(bf16[16,3072]{1,0:T(8,128)(2,1)S(1)} %pad_maximum_fusion.refs_0_), channel_id=1, source_target_pairs={{0,4},{1,5},{2,6},{3,7},{4,0},{5,1},{6,2},{7,3},{8,12},{9,13},{10,... | collective-permute-start | bytes 294920 | tf_op jit(solution)/shard_map/ppermute | solution.py:30
  17.9 9.1 %copy-start.1 = (bf16[1,4,3072]{2,1,0:T(4,128)(2,1)S(1)}, bf16[1,4,3072]{2,1,0:T(4,128)(2,1)}, u32[]{:S(2)}) copy-start(bf16[1,4,3072]{2,1,0:T(4,128)(2,1)} %param.6) | copy-start | bytes 73732
  18.0 4.2 %collective-permute-start.5 = (bf16[8,3072]{1,0:T(8,128)(2,1)S(1)}, bf16[8,3072]{1,0:T(8,128)(2,1)S(1)}, u32[]{:S(2)}, u32[]{:S(2)}) collective-permute-start(bf16[8,3072]{1,0:T(8,128)(2,1)S(1)} %slice.32), channel_id=1, source_target_pairs={{0,8},{1,9},{2,10},{3,11},{4,12},{5,13},{6,14},{7,15},{8,0},{9,1},... | collective-permute-start | bytes 147464 | tf_op jit(solution)/shard_map/ppermute | solution.py:30
  22.0 1.8 %collective-permute-start.11 = (bf16[64,3072]{1,0:T(8,128)(2,1)S(1)}, bf16[64,3072]{1,0:T(8,128)(2,1)S(1)}, u32[]{:S(2)}, u32[]{:S(2)}) collective-permute-start(bf16[64,3072]{1,0:T(8,128)(2,1)S(1)} %pack.1.refs_0_), channel_id=1, source_target_pairs={{0,1},{1,0},{2,3},{3,2},{4,5},{5,4},{6,7},{7,6},{8,9},{9,8},{10,11... | collective-permute-start | bytes 1179656 | tf_op jit(solution)/shard_map/ppermute | solution.py:30
  22.2 4.8 %collective-permute-start.6 = (bf16[4,3072]{1,0:T(4,128)(2,1)S(1)}, bf16[4,3072]{1,0:T(4,128)(2,1)S(1)}, u32[]{:S(2)}, u32[]{:S(2)}) collective-permute-start(bf16[4,3072]{1,0:T(4,128)(2,1)S(1)} %slice.33), channel_id=1, source_target_pairs={{0,16},{1,17},{2,18},{3,19},{4,20},{5,21},{6,22},{7,23},{8,24},{9,... | collective-permute-start | bytes 73736 | tf_op jit(solution)/shard_map/ppermute | solution.py:30

commit v7 on v6

--- a/solution.py
+++ b/solution.py
@@ -131,7 +131,9 @@
             wg_ref[pl.ds(i * BLOCK, BLOCK), part] = band.astype(bf16)
         results.append(pltpu.make_async_copy(wg_ref.at[:, part], wg_hbm.at[:, part], sems.at[c]))
         results[-1].start()
-    total = lax.dot_general(w_ref[...], grad_ref[...], (((1,), (1,)), ((), ())), preferred_element_type=f32)
+    total = jnp.zeros((w_ref.shape[0], tokens), f32)
+    for part in parts:
+        total += jnp.dot(w_ref[:, part], grad_ref[:, part].T, preferred_element_type=f32)
     moved = (total * slope_ref[...]).astype(bf16)
     back = reorder(me_ref[0], tokens, order, back=True)
     pg_ref[...] = lax.dot_general(back, moved, (((1,), (1,)), ((), ())), preferred_element_type=f32).astype(bf16)

time: 27.8 us -> 27.8 us (level)
  no operation moved by 1% of the time
where the time goes in v7:
time: 27.8 us; the launch traced here: 27.6 us
  starting transfers between devices  17.1 us (62%)
  Pallas kernels  5.58 us (20%)
  waiting for transfers between devices  3.31 us (12%)
  other arithmetic  0.86 us (3%)
  between operations  0.76 us (3%)
    ppermute x12, starting transfers between devices, exchange(): lax.ppermute(block, 'blk', [(i, i ^ bit) for i in range(lax.axis_size('bl...  17.1 us
    ppermute x12, waiting for transfers between devices, exchange(): lax.ppermute(block, 'blk', [(i, i ^ bit) for i in range(lax.axis_size('bl...  3.31 us
    pallas_call x1, Pallas kernels, body(): pl.pallas_call(functools.partial(backward_kernel, gather_order, len(grads...  2.73 us
    pallas_call x1, Pallas kernels, body(): pl.pallas_call(functools.partial(forward_kernel, scatter_order), out_shap...  2.49 us
    broadcast_in_dim x1, other arithmetic, body(): return (stream_out[None], preact_grad[None], weight_grad[None])  0.63 us
  transfers between devices with their start and end apart: 12, of which 6 were waited for; matrix products, arithmetic and copies ran while one was open for 1% of the time, Pallas kernels for 20%

profile of v7, /device:TPU:0, one launch (start us, length us, event | category | flops | bytes accessed | tf_op | source)
XLA Modules:
  0.0 27.6 jit_solution(2115868807766504820)
XLA Ops:
  0.6 0.0 copy-start
  0.6 3.1 %collective-permute-start = (bf16[4,3072]{1,0:T(4,128)(2,1)}, bf16[4,3072]{1,0:T(4,128)(2,1)S(1)}, u32[]{:S(2)}, u32[]{:S(2)}) collective-permute-start(bf16[4,3072]{1,0:T(4,128)(2,1)} %bitcast.16), channel_id=1, source_target_pairs={{0,8},{1,9},{2,10},{3,11},{4,12},{5,13},{6,14},{7,15},{8,0},{9,1},... | collective-permute-start | bytes 73736 | tf_op jit(solution)/shard_map/ppermute | solution.py:30
  3.7 2.5 %forward.1 = (f32[64,3072]{1,0:T(8,128)S(1)}, bf16[64,3072]{1,0:T(8,128)(2,1)S(1)}, bf16[512,3072]{1,0:T(8,128)(2,1)S(1)}, f32[4,3072]{1,0:T(4,128)S(1)}, bf16[128,512]{1,0:T(8,128)(2,1)S(1)}) custom-call(s32[1]{0:T(128)} %bitcast.me_ref, s32[4,24]{1,0:T(4,128)} %bitcast.19, bf16[128,512]{1,0:T(8,128)(2,1)} %bitcast.14, bf16[128,512]{1,0:T(8,128)(2,1)} %bitcast.15, ...), custom_call_target="tpu_custom_call" | custom-call | flops 402653184 | bytes 6000000 | tf_op jit(solution)/shard_map/forward/pallas_call | solution.py:175
  6.2 0.0 collective-permute-done
  6.2 0.1 collective-permute-start.1
  6.3 0.0 copy-done
  6.4 2.7 %collective-permute-start.7 = (bf16[8,3072]{1,0:T(8,128)(2,1)S(1)}, bf16[8,3072]{1,0:T(8,128)(2,1)S(1)}, u32[]{:S(2)}, u32[]{:S(2)}) collective-permute-start(bf16[8,3072]{1,0:T(8,128)(2,1)S(1)} %pad_maximum_fusion.1), channel_id=1, source_target_pairs={{0,16},{1,17},{2,18},{3,19},{4,20},{5,21},{6,22},{7,23},{8,24},{9,... | collective-permute-start | bytes 147464 | tf_op jit(solution)/shard_map/ppermute | solution.py:30
  9.0 0.0 collective-permute-done.1
  9.0 0.1 fusion.5
  9.2 2.5 %collective-permute-start.4 = (bf16[16,3072]{1,0:T(8,128)(2,1)S(1)}, bf16[16,3072]{1,0:T(8,128)(2,1)S(1)}, u32[]{:S(2)}, u32[]{:S(2)}) collective-permute-start(bf16[16,3072]{1,0:T(8,128)(2,1)S(1)} %get-tuple-element.28), channel_id=1, source_target_pairs={{0,6},{1,7},{2,4},{3,5},{4,2},{5,3},{6,0},{7,1},{8,14},{9,15},{10,... | collective-permute-start | bytes 294920 | tf_op jit(solution)/shard_map/ppermute | solution.py:30
  11.7 0.5 %collective-permute-start.3 = (bf16[16,3072]{1,0:T(8,128)(2,1)S(1)}, bf16[16,3072]{1,0:T(8,128)(2,1)S(1)}, u32[]{:S(2)}, u32[]{:S(2)}) collective-permute-start(bf16[16,3072]{1,0:T(8,128)(2,1)S(1)} %get-tuple-element.29), channel_id=1, source_target_pairs={{0,4},{1,5},{2,6},{3,7},{4,0},{5,1},{6,2},{7,3},{8,12},{9,13},{10,... | collective-permute-start | bytes 294920 | tf_op jit(solution)/shard_map/ppermute | solution.py:30
  12.2 0.5 %collective-permute-start.2 = (bf16[16,3072]{1,0:T(8,128)(2,1)S(1)}, bf16[16,3072]{1,0:T(8,128)(2,1)S(1)}, u32[]{:S(2)}, u32[]{:S(2)}) collective-permute-start(bf16[16,3072]{1,0:T(8,128)(2,1)S(1)} %get-tuple-element.27), channel_id=1, source_target_pairs={{0,2},{1,3},{2,0},{3,1},{4,6},{5,7},{6,4},{7,5},{8,10},{9,11},{10,... | collective-permute-start | bytes 294920 | tf_op jit(solution)/shard_map/ppermute | solution.py:30
  12.7 0.0 collective-permute-done.7
  12.8 1.5 %collective-permute-start.8 = (bf16[16,3072]{1,0:T(8,128)(2,1)S(1)}, bf16[16,3072]{1,0:T(8,128)(2,1)S(1)}, u32[]{:S(2)}, u32[]{:S(2)}) collective-permute-start(bf16[16,3072]{1,0:T(8,128)(2,1)S(1)} %pad_maximum_fusion.refs_0_), channel_id=1, source_target_pairs={{0,2},{1,3},{2,0},{3,1},{4,6},{5,7},{6,4},{7,5},{8,10},{9,11},{10,... | collective-permute-start | bytes 294920 | tf_op jit(solution)/shard_map/ppermute | solution.py:30
  14.3 1.5 %collective-permute-start.9 = (bf16[16,3072]{1,0:T(8,128)(2,1)S(1)}, bf16[16,3072]{1,0:T(8,128)(2,1)S(1)}, u32[]{:S(2)}, u32[]{:S(2)}) collective-permute-start(bf16[16,3072]{1,0:T(8,128)(2,1)S(1)} %pad_maximum_fusion.refs_0_), channel_id=1, source_target_pairs={{0,6},{1,7},{2,4},{3,5},{4,2},{5,3},{6,0},{7,1},{8,14},{9,15},{10,... | collective-permute-start | bytes 294920 | tf_op jit(solution)/shard_map/ppermute | solution.py:30
  15.8 0.0 collective-permute-done.4
  15.8 1.5 %collective-permute-start.10 = (bf16[16,3072]{1,0:T(8,128)(2,1)S(1)}, bf16[16,3072]{1,0:T(8,128)(2,1)S(1)}, u32[]{:S(2)}, u32[]{:S(2)}) collective-permute-start(bf16[16,3072]{1,0:T(8,128)(2,1)S(1)} %pad_maximum_fusion.refs_0_), channel_id=1, source_target_pairs={{0,4},{1,5},{2,6},{3,7},{4,0},{5,1},{6,2},{7,3},{8,12},{9,13},{10,... | collective-permute-start | bytes 294920 | tf_op jit(solution)/shard_map/ppermute | solution.py:30
  17.3 0.0 collective-permute-done.3
  17.3 0.6 %collective-permute-done.2 = bf16[16,3072]{1,0:T(8,128)(2,1)S(1)} collective-permute-done((bf16[16,3072]{1,0:T(8,128)(2,1)S(1)}, bf16[16,3072]{1,0:T(8,128)(2,1)S(1)}, u32[]{:S(2)}, u32[]{:S(2)}) %collective-permute-start.2) | collective-permute-done | bytes 98336 | tf_op jit(solution)/shard_map/ppermute | solution.py:30
  18.0 1.5 %collective-permute-start.5 = (bf16[8,3072]{1,0:T(8,128)(2,1)S(1)}, bf16[8,3072]{1,0:T(8,128)(2,1)S(1)}, u32[]{:S(2)}, u32[]{:S(2)}) collective-permute-start(bf16[8,3072]{1,0:T(8,128)(2,1)S(1)} %slice.32), channel_id=1, source_target_pairs={{0,8},{1,9},{2,10},{3,11},{4,12},{5,13},{6,14},{7,15},{8,0},{9,1},... | collective-permute-start | bytes 147464 | tf_op jit(solution)/shard_map/ppermute | solution.py:30
  19.5 0.3 %prepare.1 = (bf16[512,128]{1,0:T(8,128)(2,1)S(1)}, f32[512,128]{1,0:T(8,128)S(1)}) custom-call(s32[1]{0:T(128)} %bitcast.me_ref, bf16[128,512]{1,0:T(8,128)(2,1)S(1)} %get-tuple-element.20.back_ref), custom_call_target="tpu_custom_call" | custom-call | flops 16777216 | bytes 1500000 | tf_op jit(solution)/shard_map/prepare/pallas_call | solution.py:197
  19.8 0.2 collective-permute-done.8.refs_1_
  20.0 1.8 %collective-permute-done.9.refs_2_ = bf16[16,3072]{1,0:T(8,128)(2,1)S(1)} collective-permute-done((bf16[16,3072]{1,0:T(8,128)(2,1)S(1)}, bf16[16,3072]{1,0:T(8,128)(2,1)S(1)}, u32[]{:S(2)}, u32[]{:S(2)}) %collective-permute-start.9) | collective-permute-done | bytes 98336 | tf_op jit(solution)/shard_map/ppermute | solution.py:30
  21.8 0.2 collective-permute-done.10.refs_3_
  22.0 0.1 collective-permute-start.11
  22.1 0.1 collective-permute-done.5
  22.2 1.6 %collective-permute-start.6 = (bf16[4,3072]{1,0:T(4,128)(2,1)S(1)}, bf16[4,3072]{1,0:T(4,128)(2,1)S(1)}, u32[]{:S(2)}, u32[]{:S(2)}) collective-permute-start(bf16[4,3072]{1,0:T(4,128)(2,1)S(1)} %slice.33), channel_id=1, source_target_pairs={{0,16},{1,17},{2,18},{3,19},{4,20},{5,21},{6,22},{7,23},{8,24},{9,... | collective-permute-start | bytes 73736 | tf_op jit(solution)/shard_map/ppermute | solution.py:30
  23.8 0.0 collective-permute-done.11.refs_1_
  23.8 2.7 %backward.1 = (bf16[512,3072]{1,0:T(8,128)(2,1)}, bf16[128,512]{1,0:T(8,128)(2,1)}) custom-call(s32[1]{0:T(128)} %bitcast.me_ref, bf16[64,3072]{1,0:T(8,128)(2,1)S(1)} %pack.1.refs_0_, bf16[64,3072]{1,0:T(8,128)(2,1)S(1)} %collective-permute-done.11.refs_1_, f32[4,3072]{1,0:T(4,128)S(1)} %get-tuple-element.18.refs_2_, ...), custom_call_target="tpu_custom_call" | custom-call | flops 805306368 | bytes 6291456 | tf_op jit(solution)/shard_map/backward/pallas_call | solution.py:240
  26.5 0.5 %collective-permute-done.6 = bf16[4,3072]{1,0:T(4,128)(2,1)S(1)} collective-permute-done((bf16[4,3072]{1,0:T(4,128)(2,1)S(1)}, bf16[4,3072]{1,0:T(4,128)(2,1)S(1)}, u32[]{:S(2)}, u32[]{:S(2)}) %collective-permute-start.6) | collective-permute-done | bytes 24608 | tf_op jit(solution)/shard_map/ppermute | solution.py:30
  27.0 0.0 copy-done.1
  27.0 0.6 %fusion.4 = bf16[1,4,3072]{2,1,0:T(4,128)(2,1)} fusion(bf16[4,3072]{1,0:T(4,128)(2,1)S(1)} %collective-permute-done.6, f32[8,3072]{1,0:T(8,128)S(1)} %slice_add_fusion.1, bf16[1,4,3072]{2,1,0:T(4,128)(2,1)S(1)} %copy-done.1), kind=kLoop, calls=%fused_computation.12 | loop fusion | flops 61440 | bytes 122880 | tf_op jit(solution)/shard_map/broadcast_in_dim | solution.py:255
  (9 shorter events, 0.2 us)
Async XLA Ops:
  0.6 5.7 %copy-start = (bf16[1,4,3072]{2,1,0:T(4,128)(2,1)S(1)}, bf16[1,4,3072]{2,1,0:T(4,128)(2,1)}, u32[]{:S(2)}) copy-start(bf16[1,4,3072]{2,1,0:T(4,128)(2,1)} %param.7) | copy-start | bytes 73732
  0.6 5.6 %collective-permute-start = (bf16[4,3072]{1,0:T(4,128)(2,1)}, bf16[4,3072]{1,0:T(4,128)(2,1)S(1)}, u32[]{:S(2)}, u32[]{:S(2)}) collective-permute-start(bf16[4,3072]{1,0:T(4,128)(2,1)} %bitcast.16), channel_id=1, source_target_pairs={{0,8},{1,9},{2,10},{3,11},{4,12},{5,13},{6,14},{7,15},{8,0},{9,1},... | collective-permute-start | bytes 73736 | tf_op jit(solution)/shard_map/ppermute | solution.py:30
  6.2 2.8 %collective-permute-start.1 = (bf16[64,3072]{1,0:T(8,128)(2,1)S(1)}, bf16[64,3072]{1,0:T(8,128)(2,1)S(1)}, u32[]{:S(2)}, u32[]{:S(2)}) collective-permute-start(bf16[64,3072]{1,0:T(8,128)(2,1)S(1)} %get-tuple-element.16), channel_id=1, source_target_pairs={{0,1},{1,0},{2,3},{3,2},{4,5},{5,4},{6,7},{7,6},{8,9},{9,8},{10,11... | collective-permute-start | bytes 1179656 | tf_op jit(solution)/shard_map/ppermute | solution.py:30
  6.4 6.4 %collective-permute-start.7 = (bf16[8,3072]{1,0:T(8,128)(2,1)S(1)}, bf16[8,3072]{1,0:T(8,128)(2,1)S(1)}, u32[]{:S(2)}, u32[]{:S(2)}) collective-permute-start(bf16[8,3072]{1,0:T(8,128)(2,1)S(1)} %pad_maximum_fusion.1), channel_id=1, source_target_pairs={{0,16},{1,17},{2,18},{3,19},{4,20},{5,21},{6,22},{7,23},{8,24},{9,... | collective-permute-start | bytes 147464 | tf_op jit(solution)/shard_map/ppermute | solution.py:30
  9.2 6.7 %collective-permute-start.4 = (bf16[16,3072]{1,0:T(8,128)(2,1)S(1)}, bf16[16,3072]{1,0:T(8,128)(2,1)S(1)}, u32[]{:S(2)}, u32[]{:S(2)}) collective-permute-start(bf16[16,3072]{1,0:T(8,128)(2,1)S(1)} %get-tuple-element.28), channel_id=1, source_target_pairs={{0,6},{1,7},{2,4},{3,5},{4,2},{5,3},{6,0},{7,1},{8,14},{9,15},{10,... | collective-permute-start | bytes 294920 | tf_op jit(solution)/shard_map/ppermute | solution.py:30
  11.7 5.6 %collective-permute-start.3 = (bf16[16,3072]{1,0:T(8,128)(2,1)S(1)}, bf16[16,3072]{1,0:T(8,128)(2,1)S(1)}, u32[]{:S(2)}, u32[]{:S(2)}) collective-permute-start(bf16[16,3072]{1,0:T(8,128)(2,1)S(1)} %get-tuple-element.29), channel_id=1, source_target_pairs={{0,4},{1,5},{2,6},{3,7},{4,0},{5,1},{6,2},{7,3},{8,12},{9,13},{10,... | collective-permute-start | bytes 294920 | tf_op jit(solution)/shard_map/ppermute | solution.py:30
  12.2 5.8 %collective-permute-start.2 = (bf16[16,3072]{1,0:T(8,128)(2,1)S(1)}, bf16[16,3072]{1,0:T(8,128)(2,1)S(1)}, u32[]{:S(2)}, u32[]{:S(2)}) collective-permute-start(bf16[16,3072]{1,0:T(8,128)(2,1)S(1)} %get-tuple-element.27), channel_id=1, source_target_pairs={{0,2},{1,3},{2,0},{3,1},{4,6},{5,7},{6,4},{7,5},{8,10},{9,11},{10,... | collective-permute-start | bytes 294920 | tf_op jit(solution)/shard_map/ppermute | solution.py:30
  12.8 7.3 %collective-permute-start.8 = (bf16[16,3072]{1,0:T(8,128)(2,1)S(1)}, bf16[16,3072]{1,0:T(8,128)(2,1)S(1)}, u32[]{:S(2)}, u32[]{:S(2)}) collective-permute-start(bf16[16,3072]{1,0:T(8,128)(2,1)S(1)} %pad_maximum_fusion.refs_0_), channel_id=1, source_target_pairs={{0,2},{1,3},{2,0},{3,1},{4,6},{5,7},{6,4},{7,5},{8,10},{9,11},{10,... | collective-permute-start | bytes 294920 | tf_op jit(solution)/shard_map/ppermute | solution.py:30
  14.3 7.5 %collective-permute-start.9 = (bf16[16,3072]{1,0:T(8,128)(2,1)S(1)}, bf16[16,3072]{1,0:T(8,128)(2,1)S(1)}, u32[]{:S(2)}, u32[]{:S(2)}) collective-permute-start(bf16[16,3072]{1,0:T(8,128)(2,1)S(1)} %pad_maximum_fusion.refs_0_), channel_id=1, source_target_pairs={{0,6},{1,7},{2,4},{3,5},{4,2},{5,3},{6,0},{7,1},{8,14},{9,15},{10,... | collective-permute-start | bytes 294920 | tf_op jit(solution)/shard_map/ppermute | solution.py:30
  15.8 6.1 %collective-permute-start.10 = (bf16[16,3072]{1,0:T(8,128)(2,1)S(1)}, bf16[16,3072]{1,0:T(8,128)(2,1)S(1)}, u32[]{:S(2)}, u32[]{:S(2)}) collective-permute-start(bf16[16,3072]{1,0:T(8,128)(2,1)S(1)} %pad_maximum_fusion.refs_0_), channel_id=1, source_target_pairs={{0,4},{1,5},{2,6},{3,7},{4,0},{5,1},{6,2},{7,3},{8,12},{9,13},{10,... | collective-permute-start | bytes 294920 | tf_op jit(solution)/shard_map/ppermute | solution.py:30
  17.9 9.1 %copy-start.1 = (bf16[1,4,3072]{2,1,0:T(4,128)(2,1)S(1)}, bf16[1,4,3072]{2,1,0:T(4,128)(2,1)}, u32[]{:S(2)}) copy-start(bf16[1,4,3072]{2,1,0:T(4,128)(2,1)} %param.6) | copy-start | bytes 73732
  18.0 4.2 %collective-permute-start.5 = (bf16[8,3072]{1,0:T(8,128)(2,1)S(1)}, bf16[8,3072]{1,0:T(8,128)(2,1)S(1)}, u32[]{:S(2)}, u32[]{:S(2)}) collective-permute-start(bf16[8,3072]{1,0:T(8,128)(2,1)S(1)} %slice.32), channel_id=1, source_target_pairs={{0,8},{1,9},{2,10},{3,11},{4,12},{5,13},{6,14},{7,15},{8,0},{9,1},... | collective-permute-start | bytes 147464 | tf_op jit(solution)/shard_map/ppermute | solution.py:30
  22.0 1.8 %collective-permute-start.11 = (bf16[64,3072]{1,0:T(8,128)(2,1)S(1)}, bf16[64,3072]{1,0:T(8,128)(2,1)S(1)}, u32[]{:S(2)}, u32[]{:S(2)}) collective-permute-start(bf16[64,3072]{1,0:T(8,128)(2,1)S(1)} %pack.1.refs_0_), channel_id=1, source_target_pairs={{0,1},{1,0},{2,3},{3,2},{4,5},{5,4},{6,7},{7,6},{8,9},{9,8},{10,11... | collective-permute-start | bytes 1179656 | tf_op jit(solution)/shard_map/ppermute | solution.py:30
  22.2 4.8 %collective-permute-start.6 = (bf16[4,3072]{1,0:T(4,128)(2,1)S(1)}, bf16[4,3072]{1,0:T(4,128)(2,1)S(1)}, u32[]{:S(2)}, u32[]{:S(2)}) collective-permute-start(bf16[4,3072]{1,0:T(4,128)(2,1)S(1)} %slice.33), channel_id=1, source_target_pairs={{0,16},{1,17},{2,18},{3,19},{4,20},{5,21},{6,22},{7,23},{8,24},{9,... | collective-permute-start | bytes 73736 | tf_op jit(solution)/shard_map/ppermute | solution.py:30
